TPU v7x, 32 devices: a whole 2x2x4 slice. The times are simulated.
32 devices in a mesh: dp: 32 (over z, y, x, core).
Axes of the slice: x: 2, y: 2, z: 4, core: 2. Of those that a mesh axis runs over, the one named last changes fastest.
Arguments:
- tokens: bfloat16 [16384, 1024], P('dp'), may hold values from -6 to 6
- segment_ids: int32 [16384], P('dp'), may hold values from 0 to 511, never falling along the last dimension, each value on 1 to 512 neighbouring positions
- cotangent: bfloat16 [16384, 1024], P('dp'), may hold values from -6 to 6
- norm1_gain: float32 [1024], P('dp'), may hold values from 0.5 to 1.5
- mixer_in: float32 [1024, 6144], P('dp'), may hold values from -0.1875 to 0.1875
- decay_in: float32 [1024, 16], P('dp'), may hold values from -0.375 to 0.375
- conv_weight: float32 [4, 4096], P(None, 'dp'), may hold values from -3 to 3
- decay_log: float32 [8], replicated, may hold values from -1 to 2.5
- decay_bias: float32 [8], replicated, may hold values from -7 to -2
- head_gain: float32 [256], replicated, may hold values from 0.25 to 1.75
- mixer_out: float32 [2048, 1024], P(None, 'dp'), may hold values from -0.25 to 0.25
- norm2_gain: float32 [1024], P('dp'), may hold values from 0.5 to 1.5
- ffn_in: float32 [1024, 5632], P('dp'), may hold values from -0.1875 to 0.1875
- ffn_out: float32 [2816, 1024], P(None, 'dp'), may hold values from -0.21875 to 0.21875
Outputs:
- output: bfloat16 [16384, 1024], P('dp')
- input_grad: float32 [16384, 1024], P('dp')
- norm1_grad: float32 [1024], P('dp')
- mixer_in_grad: float32 [1024, 6144], P('dp')
- decay_in_grad: float32 [1024, 16], P('dp')
- conv_grad: float32 [4, 4096], P(None, 'dp')
- decay_log_grad: float32 [8], replicated
- decay_bias_grad: float32 [8], replicated
- head_gain_grad: float32 [256], replicated
- mixer_out_grad: float32 [2048, 1024], P(None, 'dp')
- norm2_grad: float32 [1024], P('dp')
- ffn_in_grad: float32 [1024, 5632], P('dp')
- ffn_out_grad: float32 [2816, 1024], P(None, 'dp')
Inputs may be any that keep to these rules, and one draw needn't show every extreme that they name: `segment_ids`: segment numbers never fall along the tokens; each of the 512 documents holds 1 to 512 tokens, one of them exactly 512.
All inputs are finite; a program needn't handle non-finite values.
Results may differ from a plain program's by a relative error of at most 0.009.
The roundings to bfloat16 on the way count: a program that leaves them out, or rounds other values in their place, can miss the bound.
Values may be sent and summed in bfloat16 or wider, within the bound.
A program may use at most 384 MiB of HBM per device.

v0:
```python
from functools import partial

import jax
import jax.numpy as jnp
from jax import lax
from jax.sharding import PartitionSpec as P

HEADS = 8
DK = 128
DV = 256
GROUP = 64
SEQ = 256
MICRO = 2


MATMUL_EXACTNESS = lax.Precision.HIGHEST
epsilon = 1e-06
head_epsilon = 0.001


def rms_scale(values, gain_vec):
    return (
        values * lax.rsqrt(jnp.mean(values * values, axis=-1, keepdims=True) + epsilon) * gain_vec
    )


def swiglu(gate_up):
    split_at = gate_up.shape[-1] // 2
    return jax.nn.silu(gate_up[:, :split_at]) * gate_up[:, split_at:]


def short_conv(values, weight, segment):
    summed = values * weight[0]
    for offset in range(1, weight.shape[0]):
        shifted = jnp.pad(values[:-offset], ((offset, 0), (0, 0)))
        earlier = jnp.pad(segment[:-offset], (offset, 0), constant_values=-1)
        same_doc = (earlier == segment).astype(jnp.float32)[:, None]
        summed = summed + shifted * same_doc * weight[offset]
    return summed


def group_inverse(coupling):
    order_size = coupling.shape[-1]
    identity = jnp.eye(order_size, dtype=coupling.dtype)
    powers = -coupling
    result = identity + powers
    for section_index in range(order_size.bit_length() - 2):
        powers = jnp.matmul(powers, powers, precision=MATMUL_EXACTNESS)
        result = jnp.matmul(result, identity + powers, precision=MATMUL_EXACTNESS)
    return result


def delta_core(queries, key_vecs, values, log_decay, write_rate, segment):
    length, heads, key_size = queries.shape
    value_size = values.shape[-1]
    blocks = length // GROUP

    def by_block(array):
        shaped = array.reshape((blocks, GROUP) + array.shape[1:])
        return jnp.moveaxis(shaped, 2, 1)

    query_b = by_block(queries)
    keys_b = by_block(key_vecs)
    values_b = by_block(values)
    decay_b = by_block(log_decay)
    rate_b = by_block(write_rate)
    seg_b = segment.reshape(blocks, GROUP)
    previous = jnp.concatenate([jnp.full((1,), -1, jnp.int32), seg_b[:-1, -1]])
    carried = (seg_b == previous[:, None]).astype(jnp.float32)
    position = jnp.arange(GROUP)
    lower_tri = position[:, None] >= position[None, :]
    strict = position[:, None] > position[None, :]
    same_doc = ((seg_b[:, :, None] == seg_b[:, None, :]) & lower_tri)[:, None]
    cumulative = jnp.cumsum(decay_b, axis=-1)
    spread = cumulative[..., :, None] - cumulative[..., None, :]
    pair_decay = jnp.where(same_doc, jnp.exp(jnp.where(same_doc, spread, 0.0)), 0.0)
    start_decay = jnp.exp(cumulative) * carried[:, None, :]
    key_dots = jnp.einsum("nhik,nhjk->nhij", keys_b, keys_b, precision=MATMUL_EXACTNESS)
    coupling = jnp.where(strict, pair_decay * key_dots, 0.0) * rate_b[..., :, None]
    inverse = group_inverse(coupling)
    base_values = jnp.einsum(
        "nhij,nhjv->nhiv", inverse, rate_b[..., None] * values_b, precision=MATMUL_EXACTNESS
    )
    base_keys = jnp.einsum(
        "nhij,nhjk->nhik",
        inverse,
        (rate_b * start_decay)[..., None] * keys_b,
        precision=MATMUL_EXACTNESS,
    )
    scores = pair_decay * jnp.einsum("nhik,nhjk->nhij", query_b, keys_b, precision=MATMUL_EXACTNESS)
    start_query = start_decay[..., None] * query_b
    end_keys = pair_decay[..., -1, :, None] * keys_b
    end_decay = start_decay[..., -1]

    def advance(running_state, pieces):
        value_basis, key_basis, score, leading_query, final_keys, final_decay = pieces
        state_update = value_basis - jnp.einsum(
            "bil,blw->biw", key_basis, running_state, precision=MATMUL_EXACTNESS
        )
        output = jnp.einsum(
            "bil,blw->biw", leading_query, running_state, precision=MATMUL_EXACTNESS
        )
        output = output + jnp.einsum(
            "hij,hjv->hiv", score, state_update, precision=MATMUL_EXACTNESS
        )
        running_state = final_decay[:, None, None] * running_state + jnp.einsum(
            "uxp,uxo->upo", final_keys, state_update, precision=MATMUL_EXACTNESS
        )
        return (running_state, output)

    initial = jnp.zeros((heads, key_size, value_size), jnp.float32)
    _, outputs = lax.scan(
        advance, initial, (base_values, base_keys, scores, start_query, end_keys, end_decay)
    )
    return jnp.moveaxis(outputs, 1, 2).reshape(length, heads, value_size)


def mixer_piece(segment, projected, gate_logits, conv_taps, decay_log, decay_bias, head_gain):
    length = projected.shape[0]
    conv_width = conv_taps.shape[1]
    key_width = HEADS * DK
    activated = jax.nn.silu(short_conv(projected[:, :conv_width], conv_taps, segment))
    queries = activated[:, :key_width].reshape(length, HEADS, DK)
    key_vecs = activated[:, key_width : 2 * key_width].reshape(length, HEADS, DK)
    values = activated[:, 2 * key_width :].reshape(length, HEADS, DV)
    queries = (
        queries
        * lax.rsqrt(jnp.sum(queries * queries, axis=-1, keepdims=True) + epsilon)
        * DK ** (-0.5)
    )
    key_vecs = key_vecs * lax.rsqrt(jnp.sum(key_vecs * key_vecs, axis=-1, keepdims=True) + epsilon)
    log_decay = -jnp.exp(decay_log) * jax.nn.softplus(gate_logits[:, :HEADS] + decay_bias)
    write_rate = jax.nn.sigmoid(gate_logits[:, HEADS:])
    core = delta_core(queries, key_vecs, values, log_decay, write_rate, segment)
    normed = (
        core * lax.rsqrt(jnp.mean(core * core, axis=-1, keepdims=True) + head_epsilon) * head_gain
    )
    gated = normed * jax.nn.silu(projected[:, conv_width:].reshape(length, HEADS, DV))
    return gated.reshape(length, HEADS * DV)


def forward_pass(inputs, segment, gathered, decay_log, decay_bias, head_gain):
    (
        norm_first,
        weight_in,
        weight_decay,
        conv_taps,
        weight_out,
        norm_second,
        weight_ffin,
        weight_ffout,
    ) = gathered
    residual = inputs.astype(jnp.float32)
    scaled_in, first_back = jax.vjp(rms_scale, residual, norm_first.astype(jnp.float32))
    normed_in = scaled_in.astype(jnp.bfloat16)
    projected = jnp.dot(normed_in, weight_in, preferred_element_type=jnp.float32)
    gate_logits = jnp.dot(normed_in, weight_decay, preferred_element_type=jnp.float32)
    mixed_heads, mixer_back = jax.vjp(
        partial(mixer_piece, segment),
        projected,
        gate_logits,
        conv_taps.astype(jnp.float32),
        decay_log,
        decay_bias,
        head_gain,
    )
    mixed_low = mixed_heads.astype(jnp.bfloat16)
    middle = residual + jnp.dot(mixed_low, weight_out, preferred_element_type=jnp.float32)
    scaled_mid, second_back = jax.vjp(rms_scale, middle, norm_second.astype(jnp.float32))
    normed_mid = scaled_mid.astype(jnp.bfloat16)
    gate_up = jnp.dot(normed_mid, weight_ffin, preferred_element_type=jnp.float32)
    hidden_full, swiglu_back = jax.vjp(swiglu, gate_up)
    hidden = hidden_full.astype(jnp.bfloat16)
    output = (middle + jnp.dot(hidden, weight_ffout, preferred_element_type=jnp.float32)).astype(
        jnp.bfloat16
    )
    saved = (
        normed_in,
        mixed_low,
        normed_mid,
        hidden,
        first_back,
        mixer_back,
        second_back,
        swiglu_back,
    )
    return (output, saved)


def backward_pass(cotangent, saved, matrices):
    weight_in, weight_decay, weight_out, weight_ffin, weight_ffout = matrices
    normed_in, mixed_low, normed_mid, hidden, first_back, mixer_back, second_back, swiglu_back = (
        saved
    )
    upstream = cotangent.astype(jnp.float32)
    grad_hidden = jnp.dot(cotangent, weight_ffout.T, preferred_element_type=jnp.float32)
    grad_gate_up = swiglu_back(grad_hidden)[0].astype(jnp.bfloat16)
    grad_scaled_mid = jnp.dot(grad_gate_up, weight_ffin.T, preferred_element_type=jnp.float32)
    grad_middle, grad_norm_second = second_back(grad_scaled_mid)
    grad_middle = grad_middle + upstream
    grad_branch = grad_middle.astype(jnp.bfloat16)
    grad_mixed = jnp.dot(grad_branch, weight_out.T, preferred_element_type=jnp.float32)
    grad_proj, grad_logits, grad_conv, grad_dlog, grad_dbias, grad_hgain = mixer_back(grad_mixed)
    proj_low = grad_proj.astype(jnp.bfloat16)
    logits_low = grad_logits.astype(jnp.bfloat16)
    grad_scaled_in = jnp.dot(proj_low, weight_in.T, preferred_element_type=jnp.float32)
    grad_scaled_in = grad_scaled_in + jnp.dot(
        logits_low, weight_decay.T, preferred_element_type=jnp.float32
    )
    grad_residual, grad_norm_first = first_back(grad_scaled_in)
    grad_input = grad_residual + grad_middle
    factors = (
        normed_in,
        proj_low,
        logits_low,
        mixed_low,
        grad_branch,
        normed_mid,
        grad_gate_up,
        hidden,
        cotangent,
    )
    small = (grad_norm_first, grad_conv, grad_norm_second)
    replicated = (grad_dlog, grad_dbias, grad_hgain)
    return (grad_input, factors, small, replicated)


def weight_grads(factor_list, small):
    joined = [jnp.concatenate([entry[place] for entry in factor_list], 0) for place in range(9)]
    (
        normed_in,
        proj_low,
        logits_low,
        mixed_low,
        grad_branch,
        normed_mid,
        grad_gate_up,
        hidden,
        upstream,
    ) = joined
    grad_in = jnp.dot(normed_in.T, proj_low, preferred_element_type=jnp.float32)
    grad_decay = jnp.dot(normed_in.T, logits_low, preferred_element_type=jnp.float32)
    grad_out_t = jnp.dot(grad_branch.T, mixed_low, preferred_element_type=jnp.float32)
    grad_ffin = jnp.dot(normed_mid.T, grad_gate_up, preferred_element_type=jnp.float32)
    grad_ffout_t = jnp.dot(upstream.T, hidden, preferred_element_type=jnp.float32)
    return (
        small[0],
        grad_in,
        grad_decay,
        small[1].T,
        grad_out_t,
        small[2],
        grad_ffin,
        grad_ffout_t,
    )


def on_device(
    tokens,
    segment_ids,
    cotangent,
    norm1_gain,
    mixer_in,
    decay_in,
    conv_weight,
    decay_log,
    decay_bias,
    head_gain,
    mixer_out,
    norm2_gain,
    ffn_in,
    ffn_out,
):
    outputs = []
    input_grads = []
    factor_list = []
    small_total = None
    sharded_total = None
    replicated_total = None
    for micro_index in range(MICRO):
        start_row = micro_index * SEQ
        inputs = tokens[start_row : start_row + SEQ]
        segment = segment_ids[start_row : start_row + SEQ]
        upstream = cotangent[start_row : start_row + SEQ]
        forward_weights = (
            lax.all_gather(norm1_gain.astype(jnp.bfloat16), "dp", axis=0, tiled=True),
            lax.all_gather(mixer_in.astype(jnp.bfloat16), "dp", axis=0, tiled=True),
            lax.all_gather(decay_in.astype(jnp.bfloat16), "dp", axis=0, tiled=True),
            lax.all_gather(conv_weight.astype(jnp.bfloat16), "dp", axis=1, tiled=True),
            lax.all_gather(mixer_out.astype(jnp.bfloat16), "dp", axis=1, tiled=True),
            lax.all_gather(norm2_gain.astype(jnp.bfloat16), "dp", axis=0, tiled=True),
            lax.all_gather(ffn_in.astype(jnp.bfloat16), "dp", axis=0, tiled=True),
            lax.all_gather(ffn_out.astype(jnp.bfloat16), "dp", axis=1, tiled=True),
        )
        output, saved = forward_pass(
            inputs, segment, forward_weights, decay_log, decay_bias, head_gain
        )
        matrices = (
            lax.all_gather(mixer_in.astype(jnp.bfloat16), "dp", axis=0, tiled=True),
            lax.all_gather(decay_in.astype(jnp.bfloat16), "dp", axis=0, tiled=True),
            lax.all_gather(mixer_out.astype(jnp.bfloat16), "dp", axis=1, tiled=True),
            lax.all_gather(ffn_in.astype(jnp.bfloat16), "dp", axis=0, tiled=True),
            lax.all_gather(ffn_out.astype(jnp.bfloat16), "dp", axis=1, tiled=True),
        )
        grad_input, factors, small, replicated = backward_pass(upstream, saved, matrices)
        outputs.append(output)
        input_grads.append(grad_input)
        if replicated_total is None:
            replicated_total = replicated
        else:
            replicated_total = jax.tree.map(jnp.add, replicated_total, replicated)
        factor_list.append(factors)
        if small_total is None:
            small_total = small
        else:
            small_total = jax.tree.map(jnp.add, small_total, small)
    local = weight_grads(factor_list, small_total)
    sharded_total = (
        lax.psum_scatter(local[0], "dp", scatter_dimension=0, tiled=True),
        lax.psum_scatter(local[1], "dp", scatter_dimension=0, tiled=True),
        lax.psum_scatter(local[2], "dp", scatter_dimension=0, tiled=True),
        lax.psum_scatter(local[3], "dp", scatter_dimension=0, tiled=True),
        lax.psum_scatter(local[4], "dp", scatter_dimension=0, tiled=True),
        lax.psum_scatter(local[5], "dp", scatter_dimension=0, tiled=True),
        lax.psum_scatter(local[6], "dp", scatter_dimension=0, tiled=True),
        lax.psum_scatter(local[7], "dp", scatter_dimension=0, tiled=True),
    )
    replicated_sums = lax.psum(
        (replicated_total[0], replicated_total[1], replicated_total[2]), "dp"
    )
    return (
        jnp.concatenate(outputs, 0),
        jnp.concatenate(input_grads, 0),
        sharded_total[0],
        sharded_total[1],
        sharded_total[2],
        sharded_total[3].T,
        replicated_sums[0],
        replicated_sums[1],
        replicated_sums[2],
        sharded_total[4].T,
        sharded_total[5],
        sharded_total[6],
        sharded_total[7].T,
    )


def solution(mesh):
    in_specs = (
        P("dp", None),
        P("dp"),
        P("dp", None),
        P("dp"),
        P("dp", None),
        P("dp", None),
        P(None, "dp"),
        P(),
        P(),
        P(),
        P(None, "dp"),
        P("dp"),
        P("dp", None),
        P(None, "dp"),
    )
    out_specs = (
        P("dp", None),
        P("dp", None),
        P("dp"),
        P("dp", None),
        P("dp", None),
        P(None, "dp"),
        P(),
        P(),
        P(),
        P(None, "dp"),
        P("dp"),
        P("dp", None),
        P(None, "dp"),
    )
    return jax.shard_map(
        on_device, mesh=mesh, in_specs=in_specs, out_specs=out_specs, check_vma=False
    )
```

profile of v0, /device:TPU:0, one launch (start us, length us, event | category | flops | bytes accessed | tf_op | source)
XLA Modules:
  0.0 1969.0 jit_solution(12795654473371757264)
XLA Ops:
  14.6 43.0 %all-reduce.53 = (bf16[1024]{0:T(1024)(128)(2,1)S(1)}, bf16[1024]{0:T(1024)(128)(2,1)S(1)}) all-reduce(bf16[1024]{0:T(1024)(128)(2,1)S(1)} %dynamic-update-slice, bf16[1024]{0:T(1024)(128)(2,1)S(1)} %dynamic-update-slice.1), channel_id=1, replica_groups=mesh['dp'=32] {'dp'}, use_global_device_ids=true, to_apply=%add.48 | all-reduce | flops 2048 | bytes 8192
  58.5 41.8 %all-gather = bf16[32,32,16]{1,2,0:T(8,128)(2,1)S(1)} all-gather(bf16[1,32,16]{1,2,0:T(8,128)(2,1)S(1)} %convert_bitcast_fusion), channel_id=1, replica_groups=mesh['dp'=32] {'dp'}, dimensions={0}, use_global_device_ids=true | all-gather | bytes 33792 | tf_op jit(solution)/shard_map/all_gather | solution.py:288
  105.0 37.0 %all_gather.19 = bf16[4,4096]{1,0:T(4,128)(2,1)S(1)} all-gather(bf16[4,128]{1,0:T(4,128)(2,1)S(1)} %convert_element_type.198), channel_id=1, replica_groups=mesh['dp'=32] {'dp'}, dimensions={1}, use_global_device_ids=true | all-gather | bytes 33792 | tf_op jit(solution)/shard_map/all_gather | solution.py:289
  174.2 20.0 %fusion.165 = (f32[256,4096]{1,0:T(8,128)}, f32[256,4096]{1,0:T(8,128)}, f32[256,4096]{1,0:T(8,128)}, f32[256,4096]{1,0:T(8,128)}) fusion(f32[4096]{0:T(1024)S(1)} %bitcast.876, f32[256]{0:T(256)S(1)} %get-tuple-element.1582, f32[253,4096]{1,0:T(8,128)} %slice.246, f32[4096]{0:T(1024)S(1)} %bitcast.878, f32[256]{0:T(256)S(1)} %get-tuple-element.1581, ...), kind=kLoop, calls=%fused_computation.230 | loop fusion | flops 29360128 | bytes 50206720 | tf_op jit(solution)/shard_map/jvp(jit(silu))/mul | solution.py:122
  321.8 40.4 %while.92 = (s32[]{:T(128)}, f32[8,128,256]{2,1,0:T(8,128)S(1)}, f32[4,8,64,256]{3,2,1,0:T(8,128)}, f32[4,8,128,256]{3,2,1,0:T(8,128)}, f32[4,8,64,256]{3,2,1,0:...) while((s32[]{:T(128)}, f32[8,128,256]{2,1,0:T(8,128)S(1)}, ...), condition=%wide.region_5.7_spmd.clone, body=%wide.region_4.6_spmd.clone.sunk | while | flops 706478080 | bytes 11538700 | solution.py:112
  396.7 40.3 %while.93 = (s32[]{:T(128)}, f32[8,128,256]{2,1,0:T(8,128)S(1)}, f32[4,8,64,256]{3,2,1,0:T(8,128)}, f32[4,8,128,256]{3,2,1,0:T(8,128)}, f32[4,8,64,256]{3,2,1,0:...) while((s32[]{:T(128)}, f32[8,128,256]{2,1,0:T(8,128)S(1)}, ...), condition=%wide.region_13.15_spmd.clone, body=%wide.region_12.14_spmd.clone.sunk | while | flops 706478080 | bytes 11538700 | solution.py:112
  458.6 9.6 fusion.454
  468.2 8.0 fusion.386
  534.3 72.6 %while.95 = (s32[]{:T(128)}, f32[8,128,256]{2,1,0:T(8,128)S(1)}, f32[4,8,64,256]{3,2,1,0:T(8,128)}, f32[4,8,64,128]{3,2,1,0:T(8,128)}, f32[4,8,64,64]{2,3,1,0:T(...) while((s32[]{:T(128)}, f32[8,128,256]{2,1,0:T(8,128)S(1)}, ...), condition=%wide.region_36.38_spmd.clone, body=%wide.region_34.37_spmd.clone.sunk | while | flops 1412038656 | bytes 44050864 | solution.py:112
  627.2 83.8 %while.94 = (s32[]{:T(128)}, f32[8,128,256]{2,1,0:T(8,128)S(1)}, f32[4,8,64,256]{3,2,1,0:T(8,128)}, f32[4,8,64,128]{3,2,1,0:T(8,128)}, f32[4,8,64,64]{2,3,1,0:T(...) while((s32[]{:T(128)}, f32[8,128,256]{2,1,0:T(8,128)S(1)}, ...), condition=%wide.region_20.22_spmd.clone, body=%wide.region_18.21_spmd.clone.sunk | while | flops 1412038656 | bytes 44050864 | solution.py:112
  907.6 9.8 add_add_fusion.4
  917.5 11.2 multiply_reduce_fusion.7
  930.3 9.2 multiply_reduce_fusion.3
  956.4 11.9 copy.766
  985.6 11.2 multiply_add_fusion.1
  1003.5 12.0 fusion.146
  1016.0 13.0 fusion.150
  1029.1 7.4 fusion.477
  1044.8 37.5 %all-reduce.52 = (f32[1024]{0:T(1024)S(1)}, f32[8]{0:T(128)}, f32[8]{0:T(128)}, f32[256]{0:T(256)}, f32[1024]{0:T(1024)S(1)}) all-reduce(f32[1024]{0:T(1024)S(1)} %add.554, f32[8]{0:T(128)S(1)} %add_multiply_fusion, f32[8]{0:T(128)S(1)} %add.557, f32[256]{0:T(256)S(1)} %add.558, ...), channel_id=2, replica_groups=mesh['dp'=32] {'dp'}, use_global_device_ids=true, to_apply=%region_50.52.clone | all-reduce | flops 2320 | bytes 18560
  1099.6 64.0 %reduce-scatter.21.cloned.1.call-done = f32[128,4]{1,0:T(8,128)} async-done(((f32[4096,4]{1,0:T(8,128)}), f32[128,4]{1,0:T(8,128)}) %reduce-scatter.21.cloned.1.call-update) | async-done | bytes 2064
  1165.1 146.1 %reduce-scatter.15.cloned.1.call-done = f32[32,2048]{1,0:T(8,128)} async-done(((f32[1024,2048]{1,0:T(8,128)}), f32[32,2048]{1,0:T(8,128)}) %reduce-scatter.15.cloned.1.call-update) | async-done | bytes 262160 | tf_op jit(solution)/shard_map/reduce_scatter | solution.py:323
  1311.1 153.7 %reduce-scatter.23.cloned.1.call-done = f32[32,2816]{1,0:T(8,128)} async-done(((f32[1024,2816]{1,0:T(8,128)}), f32[32,2816]{1,0:T(8,128)}) %reduce-scatter.23.cloned.1.call-update) | async-done | bytes 360464
  1464.8 248.5 %reduce-scatter.13.cloned.1.call-done = f32[32,6144]{1,0:T(8,128)} async-done(((f32[1024,6144]{1,0:T(8,128)}), f32[32,6144]{1,0:T(8,128)}) %reduce-scatter.13.cloned.1.call-update) | async-done | bytes 786448 | tf_op jit(solution)/shard_map/reduce_scatter | solution.py:320
  1713.3 248.7 %reduce-scatter.17.cloned.1.call-done = f32[32,5632]{1,0:T(8,128)} async-done(((f32[1024,5632]{1,0:T(8,128)}), f32[32,5632]{1,0:T(8,128)}) %reduce-scatter.17.cloned.1.call-update) | async-done | bytes 720912 | tf_op jit(solution)/shard_map/reduce_scatter | solution.py:325
  (1160 shorter events, 805.9 us)
Async XLA Ops:
  7.3 137.6 %all-gather.6.cloned.1.call-start = ((), (), s32[]{:S(2)}) async-start(), calls=%async_computation.6 | async-start | bytes 12976128 | tf_op jit(solution)/shard_map/all_gather | solution.py:287
  9.4 441.9 %all-gather.8.cloned.1.call-start = ((), (), s32[]{:S(2)}) async-start(), calls=%async_computation.7 | async-start | bytes 4325376 | tf_op jit(solution)/shard_map/all_gather | solution.py:290
  11.1 447.5 %all-gather.10.cloned.1.call-start = ((), (), s32[]{:S(2)}) async-start(), calls=%async_computation.8 | async-start | bytes 11894784 | tf_op jit(solution)/shard_map/all_gather | solution.py:292
  13.1 455.1 %all-gather.12.cloned.1.call-start = ((), (), s32[]{:S(2)}) async-start(), calls=%async_computation.9 | async-start | bytes 5947392 | tf_op jit(solution)/shard_map/all_gather | solution.py:293
  13.8 91.1 %copy-start.288 = (f32[4,128]{1,0:T(4,128)S(1)}, f32[4,128]{1,0:T(4,128)}, u32[]{:S(2)}) copy-start(f32[4,128]{1,0:T(4,128)} %param.29) | copy-start | bytes 6148
  13.8 1084.4 %reduce-scatter.19.cloned.1.call-start = ((), (), s32[]{:S(2)}) async-start(), calls=%async_computation.13 | async-start | bytes 540672
  14.0 357.2 %copy-start.175 = (pred[64,64]{0,1:T(8,128)(4,1)}, pred[64,64]{0,1:T(8,128)(4,1)S(1)}, u32[]{:S(2)}) copy-start(pred[64,64]{0,1:T(8,128)(4,1)S(1)} %iota_compare_fusion) | copy-start | bytes 12292
  14.0 365.9 %copy-start.62 = (f32[64,64]{0,1:T(8,128)}, f32[64,64]{0,1:T(8,128)S(1)}, u32[]{:S(2)}) copy-start(f32[64,64]{0,1:T(8,128)S(1)} %fusion.388) | copy-start | bytes 49156
  14.1 90.8 %copy-start.284 = (f32[8]{0:T(128)}, f32[8]{0:T(128)S(1)}, u32[]{:S(2)}) copy-start(f32[8]{0:T(128)S(1)} %exponential_negate_fusion) | copy-start | bytes 100
  102.8 206.6 %copy-start.166 = (f32[4,64,8]{1,2,0:T(8,128)}, f32[4,64,8]{1,2,0:T(8,128)S(1)}, u32[]{:S(2)}) copy-start(f32[4,64,8]{1,2,0:T(8,128)S(1)} %copy.1056) | copy-start | bytes 24580
  103.7 194.4 %copy-start.132 = (f32[4,8,64]{2,1,0:T(8,128)}, f32[4,8,64]{2,1,0:T(8,128)S(1)}, u32[]{:S(2)}) copy-start(f32[4,8,64]{2,1,0:T(8,128)S(1)} %reduce_window_sum.34) | copy-start | bytes 24580
  103.7 132.5 %copy-start.194 = (f32[4,8,64]{2,1,0:T(8,128)}, f32[4,8,64]{2,1,0:T(8,128)S(1)}, u32[]{:S(2)}) copy-start(f32[4,8,64]{2,1,0:T(8,128)S(1)} %get-tuple-element.1494) | copy-start | bytes 24580
  103.8 209.7 %copy-start.199 = (f32[4,8,64]{2,1,0:T(8,128)}, f32[4,8,64]{2,1,0:T(8,128)S(1)}, u32[]{:S(2)}) copy-start(f32[4,8,64]{2,1,0:T(8,128)S(1)} %get-tuple-element.1493) | copy-start | bytes 24580
  104.9 193.2 %copy-start.161 = (pred[4,64,64]{1,2,0:T(8,128)(4,1)}, pred[4,64,64]{1,2,0:T(8,128)(4,1)S(1)}, u32[]{:S(2)}) copy-start(pred[4,64,64]{1,2,0:T(8,128)(4,1)S(1)} %get-tuple-element.1577) | copy-start | bytes 49156
  104.9 266.3 %copy-start.159 = (pred[4,64,64]{1,2,0:T(8,128)(4,1)}, pred[4,64,64]{1,2,0:T(8,128)(4,1)S(1)}, u32[]{:S(2)}) copy-start(pred[4,64,64]{1,2,0:T(8,128)(4,1)S(1)} %get-tuple-element.1578) | copy-start | bytes 49156
  143.3 228.0 %copy-start.130 = (f32[4,8,64]{2,1,0:T(8,128)}, f32[4,8,64]{2,1,0:T(8,128)S(1)}, u32[]{:S(2)}) copy-start(f32[4,8,64]{2,1,0:T(8,128)S(1)} %reduce_window_sum.35) | copy-start | bytes 24580
  143.3 150.5 %copy-start.196 = (f32[4,8,64]{2,1,0:T(8,128)}, f32[4,8,64]{2,1,0:T(8,128)S(1)}, u32[]{:S(2)}) copy-start(f32[4,8,64]{2,1,0:T(8,128)S(1)} %get-tuple-element.1498) | copy-start | bytes 24580
  197.2 116.2 %copy-start.4 = (f32[32,8,8,128]{3,2,1,0:T(8,128)}, f32[32,8,8,128]{3,2,1,0:T(8,128)S(1)}, u32[]{:S(2)}) copy-start(f32[32,8,8,128]{3,2,1,0:T(8,128)S(1)} %copy.875) | copy-start | bytes 3145732
  198.9 114.6 %copy-start.164 = (f32[4,64,8]{1,2,0:T(8,128)}, f32[4,64,8]{1,2,0:T(8,128)S(1)}, u32[]{:S(2)}) copy-start(f32[4,64,8]{1,2,0:T(8,128)S(1)} %copy.557) | copy-start | bytes 24580
  896.8 266.7 %reduce-scatter.21.cloned.1.call-start = ((), (), s32[]{:S(2)}) async-start(), calls=%async_computation.14 | async-start | bytes 2162688
  941.6 369.5 %reduce-scatter.15.cloned.1.call-start = ((), (), s32[]{:S(2)}) async-start(), calls=%async_computation.11 | async-start | bytes 8650752 | tf_op jit(solution)/shard_map/reduce_scatter | solution.py:323
  947.4 517.4 %reduce-scatter.23.cloned.1.call-start = ((), (), s32[]{:S(2)}) async-start(), calls=%async_computation.15 | async-start | bytes 11894784
  968.3 745.0 %reduce-scatter.13.cloned.1.call-start = ((), (), s32[]{:S(2)}) async-start(), calls=%async_computation.10 | async-start | bytes 25952256 | tf_op jit(solution)/shard_map/reduce_scatter | solution.py:320
  1015.5 946.4 %reduce-scatter.17.cloned.1.call-start = ((), (), s32[]{:S(2)}) async-start(), calls=%async_computation.12 | async-start | bytes 23789568 | tf_op jit(solution)/shard_map/reduce_scatter | solution.py:325
  (302 other events, 2436.7 us)
Sparse Core Ops, SparseCore 0:
  11.5 100.5 all-gather.5
  115.0 60.2 all-gather.7
  178.7 89.6 all-gather.9
  271.7 65.6 all-gather.11
  897.0 131.5 reduce-scatter.18
  1030.8 132.7 reduce-scatter.20
  1166.4 144.6 reduce-scatter.14
  1314.0 150.7 reduce-scatter.22
  1471.8 241.4 reduce-scatter.12
  1716.1 245.7 reduce-scatter.16
where the time goes:
time: 1980 us; the launch traced here: 1970 us
  waiting for transfers between devices  861 us (43%)
  matrix products  558 us (28%)
  local copies, waits for them, and re-layouts  194 us (10%)
  other arithmetic  176 us (9%)
  blocking collectives  159 us (8%)
    reduce_scatter x1, waiting for transfers between devices, on_device(): lax.psum_scatter(local[6], 'dp', scatter_dimension=0, tiled=True)  249 us
    reduce_scatter x1, waiting for transfers between devices, on_device(): lax.psum_scatter(local[1], 'dp', scatter_dimension=0, tiled=True)  249 us
    unnamed x13, waiting for transfers between devices  218 us
    reduce_scatter x1, waiting for transfers between devices, on_device(): lax.psum_scatter(local[4], 'dp', scatter_dimension=0, tiled=True)  146 us
    dot_general x30, matrix products, group_inverse(): powers = jnp.matmul(powers, powers, precision=MATMUL_EXACTNESS)  82.7 us
    unnamed x2, blocking collectives  80.5 us
    unnamed x631, local copies, waits for them, and re-layouts  70.7 us
    dot_general x24, matrix products, advance(): jnp.einsum('uxp,uxo->upo', final_keys, state_update, precision=MATMUL_EXA...  62.6 us
  transfers between devices with their start and end apart: 10, of which 5 were waited for; matrix products, arithmetic and copies ran while one was open for 24% of the time, Pallas kernels for 0%

commit v1 on v0

v1 whole, which is shorter than its diff:
```python
from functools import partial

import jax
import jax.numpy as jnp
from jax import lax
from jax.experimental import pallas as pl
from jax.experimental.pallas import tpu as pltpu
from jax.sharding import PartitionSpec as P

HEADS = 8
DK = 128
DV = 256
SEQ = 256
HEAD_COLS = 2 * DK + 2 * DV
CONV_COLS = 2 * DK + DV
TILE = 256
SMALL = 128
F32 = jnp.float32
BF16 = jnp.bfloat16
MESH = pl.DeviceIdType.MESH
MIB = 1 << 20
epsilon = 1e-06
head_epsilon = 0.001

NN = ((1,), (0,))
NT = ((1,), (1,))
TN = ((0,), (0,))


def dot1(left, right, dims):
    return lax.dot_general(
        left.astype(BF16), right.astype(BF16), (dims, ((), ())), preferred_element_type=F32
    )


def split(value):
    high = value.astype(BF16)
    return high, (value - high.astype(F32)).astype(BF16)


def dot3(left, right, dims):
    lh, ll = split(left)
    rh, rl = split(right)
    return dot1(lh, rh, dims) + (dot1(lh, rl, dims) + dot1(ll, rh, dims))


def sigmoid(value):
    return 1.0 / (1.0 + jnp.exp(-value))


def grid_of(size):
    rows = lax.broadcasted_iota(jnp.int32, (size, size), 0)
    cols = lax.broadcasted_iota(jnp.int32, (size, size), 1)
    return rows, cols


def unit_inverses(couplings):
    size = couplings[0].shape[0]
    rows, cols = grid_of(size)
    apart = rows ^ cols
    eye = jnp.where(apart == 0, 1.0, 0.0)
    lows = [a.astype(BF16) for a in couplings]
    inverses = [eye - jnp.where(apart < 2, a, 0.0) for a in couplings]
    block = 2
    while block < size:
        here = jnp.where((apart >= block) & (apart < 2 * block), 1.0, 0.0).astype(BF16)
        firsts = [dot1(low * here, inv, NN) for low, inv in zip(lows, inverses)]
        inverses = [inv - dot1(inv, first, NN) for inv, first in zip(inverses, firsts)]
        block *= 2
    return inverses


def pick_lane(columns, lane):
    at = lax.broadcasted_iota(jnp.int32, columns.shape, 1)
    return jnp.sum(jnp.where(at == lane, columns, 0.0), axis=1, keepdims=True)


def conv_of(values, taps, keep):
    total = values * taps[0:1]
    for back in (1, 2, 3):
        total = total + pltpu.roll(values, back, 0) * keep[back - 1] * taps[back : back + 1]
    return total


def decays(seg_col, seg_row, cum_col, cum_row):
    rows, cols = grid_of(SEQ)
    linked = (seg_col == seg_row) & (rows >= cols)
    return jnp.where(linked, jnp.exp(jnp.where(linked, cum_col - cum_row, 0.0)), 0.0)


def strict(value):
    rows, cols = grid_of(SEQ)
    return jnp.where(rows > cols, value, 0.0)


def head_inputs(projected, taps, cols, head):
    keep = [pick_lane(cols, 16 + i) for i in range(3)]
    conv = conv_of(projected[:, :CONV_COLS], taps, keep)
    gate = sigmoid(conv)
    act = conv * gate
    q_act, k_act, value = act[:, :DK], act[:, DK : 2 * DK], act[:, 2 * DK :]
    q_scale = lax.rsqrt(jnp.sum(q_act * q_act, axis=1, keepdims=True) + epsilon)
    k_scale = lax.rsqrt(jnp.sum(k_act * k_act, axis=1, keepdims=True) + epsilon)
    cum = pick_lane(cols, head)
    rate = pick_lane(cols, 8 + head)
    seg = pick_lane(cols, 19)
    return keep, conv, gate, act, q_act * q_scale, k_act * k_scale, value, q_scale, k_scale, cum, rate, seg


def mixer_fwd_body(xn_ref, w_ref, taps_ref, cols_ref, rows_ref, gain_ref, proj_ref, mixed_ref, inv_ref, upd_ref, core_ref):
    head = pl.program_id(0)
    tokens = xn_ref.shape[0]
    projected = jnp.dot(xn_ref[...], w_ref[...], preferred_element_type=F32)
    proj_ref[...] = projected
    _, _, _, _, q, k, value, _, _, cum, rate, seg = head_inputs(
        projected, taps_ref[...], cols_ref[...], head
    )
    q = q * DK**-0.5
    cum_row = rows_ref[pl.ds(head, 1), :]
    seg_row = rows_ref[8:9, :]
    parts = [slice(s, s + SEQ) for s in range(0, tokens, SEQ)]
    scores, couplings = [], []
    for part in parts:
        pair = decays(seg[part], seg_row[:, part], cum[part], cum_row[:, part])
        key_dots = dot3(k[part], k[part], NT)
        scores.append(pair * dot3(q[part], k[part], NT))
        couplings.append(strict(pair * key_dots) * rate[part])
    inverses = unit_inverses(couplings)
    for i, part in enumerate(parts):
        update = dot3(inverses[i], rate[part] * value[part], NN)
        core = dot3(scores[i], update, NN)
        inv_ref[0, part, :] = inverses[i].astype(BF16)
        upd_ref[0, part, :] = update
        core_ref[0, part, :] = core
        scale = lax.rsqrt(jnp.mean(core * core, axis=1, keepdims=True) + head_epsilon)
        out_gate = projected[part, CONV_COLS:]
        mixed_ref[part, :] = (core * scale * gain_ref[...] * (out_gate * sigmoid(out_gate))).astype(BF16)


def mixer_fwd(xn, w, taps, cols, rows, gain):
    tokens, width = xn.shape
    const = lambda h: (0, 0)
    by_head = lambda h: (0, h)
    save = pl.BlockSpec((1, tokens, SEQ), lambda h: (h, 0, 0))
    return pl.pallas_call(
        mixer_fwd_body,
        grid=(HEADS,),
        in_specs=[
            pl.BlockSpec((tokens, width), const),
            pl.BlockSpec((width, HEAD_COLS), by_head),
            pl.BlockSpec((4, CONV_COLS), by_head),
            pl.BlockSpec(cols.shape, const),
            pl.BlockSpec(rows.shape, const),
            pl.BlockSpec((1, DV), const),
        ],
        out_specs=[
            pl.BlockSpec((tokens, HEAD_COLS), by_head),
            pl.BlockSpec((tokens, DV), by_head),
            save,
            save,
            save,
        ],
        out_shape=[
            jax.ShapeDtypeStruct((tokens, HEADS * HEAD_COLS), F32),
            jax.ShapeDtypeStruct((tokens, HEADS * DV), BF16),
            jax.ShapeDtypeStruct((HEADS, tokens, SEQ), BF16),
            jax.ShapeDtypeStruct((HEADS, tokens, DV), F32),
            jax.ShapeDtypeStruct((HEADS, tokens, DV), F32),
        ],
        compiler_params=pltpu.CompilerParams(vmem_limit_bytes=56 * MIB),
        name="mixer_fwd",
    )(xn, w, taps, cols, rows, gain)


def mixer_bwd_body(
    gb_ref, gbt_ref, xnt_ref, wo_ref, w_ref, proj_ref, mixed_ref, inv_ref, upd_ref, core_ref,
    taps_ref, cols_ref, rows_ref, gain_ref,
    dw_ref, dwo_ref, gxn_ref, dcols_ref, drows_ref, dtaps_ref, dgain_ref, dproj_ref,
):
    head = pl.program_id(0)
    tokens = gb_ref.shape[0]

    @pl.when(head == 0)
    def _():
        gxn_ref[...] = jnp.zeros_like(gxn_ref)
        dcols_ref[...] = jnp.zeros_like(dcols_ref)
        drows_ref[...] = jnp.zeros_like(drows_ref)
        dgain_ref[...] = jnp.zeros_like(dgain_ref)

    grad_mixed = jnp.dot(gb_ref[...], wo_ref[...], preferred_element_type=F32)
    dwo_ref[...] = jnp.dot(gbt_ref[...], mixed_ref[...], preferred_element_type=F32).astype(BF16)

    projected = proj_ref[...]
    taps = taps_ref[...]
    keep, conv, gate, act, qn, k, value, q_scale, k_scale, cum, rate, seg = head_inputs(
        projected, taps, cols_ref[...], head
    )
    q = qn * DK**-0.5
    cum_row = rows_ref[pl.ds(head, 1), :]
    seg_row = rows_ref[8:9, :]
    gain = gain_ref[...]
    lanes = lax.broadcasted_iota(jnp.int32, (SEQ, 128), 1)
    d_act, d_gain = [], jnp.zeros((1, DV), F32)
    for start in range(0, tokens, SEQ):
        part = slice(start, start + SEQ)
        core, update, inverse = core_ref[0, part, :], upd_ref[0, part, :], inv_ref[0, part, :]
        grad = grad_mixed[part]
        scale = lax.rsqrt(jnp.mean(core * core, axis=1, keepdims=True) + head_epsilon)
        normed = core * scale
        out_gate = projected[part, CONV_COLS:]
        out_sig = sigmoid(out_gate)
        swish = out_gate * out_sig
        dproj_ref[part, CONV_COLS:] = (grad * normed * gain * (out_sig + swish * (1.0 - out_sig))).astype(BF16)
        d_normed = grad * swish
        d_gain = d_gain + jnp.sum(d_normed * normed, axis=0, keepdims=True)
        d_scaled = d_normed * gain
        d_core = scale * (d_scaled - normed * jnp.mean(d_scaled * normed, axis=1, keepdims=True))

        qs, ks, vs, rs = q[part], k[part], value[part], rate[part]
        pair = decays(seg[part], seg_row[:, part], cum[part], cum_row[:, part])
        key_dots = dot3(ks, ks, NT)
        query_dots = dot3(qs, ks, NT)
        d_scores = dot3(d_core, update, NT)
        d_update = dot1(pair * query_dots, d_core, TN)
        solved = dot1(inverse, d_update, TN)
        d_coupling = strict(-dot1(solved, update, NT)) * pair
        d_query_dots = pair * d_scores
        d_key_dots = d_coupling * rs
        weighed = d_coupling * key_dots
        d_spread = d_query_dots * query_dots + weighed * rs
        d_q = dot1(d_query_dots, ks, NN) * DK**-0.5
        d_k = dot1(d_query_dots, qs, TN) + dot1(d_key_dots, ks, NN) + dot1(d_key_dots, ks, TN)
        d_rate = jnp.sum(solved * vs, axis=1, keepdims=True) + jnp.sum(weighed, axis=1, keepdims=True)
        row_sum = jnp.sum(d_spread, axis=1, keepdims=True)
        dcols_ref[part, :] += jnp.where(lanes == head, d_rate, 0.0) + jnp.where(lanes == 8 + head, row_sum, 0.0)
        drows_ref[pl.ds(head, 1), part] = jnp.sum(d_spread, axis=0, keepdims=True)
        d_q_act = q_scale[part] * (d_q - qn[part] * jnp.sum(d_q * qn[part], axis=1, keepdims=True))
        d_k_act = k_scale[part] * (d_k - ks * jnp.sum(d_k * ks, axis=1, keepdims=True))
        d_act.append(jnp.concatenate([d_q_act, d_k_act, rs * solved], axis=1))
    dgain_ref[...] += d_gain
    d_conv = jnp.concatenate(d_act, axis=0) * (gate + act * (1.0 - gate))
    source = projected[:, :CONV_COLS]
    d_source = d_conv * taps[0:1]
    d_taps = [jnp.sum(d_conv * source, axis=0, keepdims=True)]
    for back in (1, 2, 3):
        kept = d_conv * keep[back - 1]
        d_source = d_source + pltpu.roll(kept, tokens - back, 0) * taps[back : back + 1]
        d_taps.append(jnp.sum(kept * pltpu.roll(source, back, 0), axis=0, keepdims=True))
    dtaps_ref[...] = jnp.concatenate(d_taps, axis=0)
    dproj_ref[:, :CONV_COLS] = d_source.astype(BF16)
    d_proj = dproj_ref[...]
    dw_ref[...] = jnp.dot(xnt_ref[...], d_proj, preferred_element_type=F32).astype(BF16)
    gxn_ref[...] += lax.dot_general(d_proj, w_ref[...], (NT, ((), ())), preferred_element_type=F32)


def mixer_bwd(gb, gbt, xnt, wo, w, proj, mixed, inv, upd, core, taps, cols, rows, gain):
    tokens, width = gb.shape
    const = lambda h: (0, 0)
    by_head = lambda h: (0, h)
    save = pl.BlockSpec((1, tokens, SEQ), lambda h: (h, 0, 0))
    return pl.pallas_call(
        mixer_bwd_body,
        grid=(HEADS,),
        in_specs=[
            pl.BlockSpec((tokens, width), const),
            pl.BlockSpec((width, tokens), const),
            pl.BlockSpec((width, tokens), const),
            pl.BlockSpec((width, DV), by_head),
            pl.BlockSpec((width, HEAD_COLS), by_head),
            pl.BlockSpec((tokens, HEAD_COLS), by_head),
            pl.BlockSpec((tokens, DV), by_head),
            save,
            save,
            save,
            pl.BlockSpec((4, CONV_COLS), by_head),
            pl.BlockSpec(cols.shape, const),
            pl.BlockSpec(rows.shape, const),
            pl.BlockSpec((1, DV), const),
        ],
        out_specs=[
            pl.BlockSpec((width, HEAD_COLS), by_head),
            pl.BlockSpec((width, DV), by_head),
            pl.BlockSpec((tokens, width), const),
            pl.BlockSpec((tokens, 128), const),
            pl.BlockSpec((HEADS, tokens), const),
            pl.BlockSpec((4, CONV_COLS), by_head),
            pl.BlockSpec((1, DV), const),
        ],
        out_shape=[
            jax.ShapeDtypeStruct((width, HEADS * HEAD_COLS), BF16),
            jax.ShapeDtypeStruct((width, HEADS * DV), BF16),
            jax.ShapeDtypeStruct((tokens, width), F32),
            jax.ShapeDtypeStruct((tokens, 128), F32),
            jax.ShapeDtypeStruct((HEADS, tokens), F32),
            jax.ShapeDtypeStruct((4, HEADS * CONV_COLS), F32),
            jax.ShapeDtypeStruct((1, DV), F32),
        ],
        scratch_shapes=[pltpu.VMEM((tokens, HEAD_COLS), BF16)],
        compiler_params=pltpu.CompilerParams(vmem_limit_bytes=60 * MIB),
        name="mixer_bwd",
    )(gb, gbt, xnt, wo, w, proj, mixed, inv, upd, core, taps, cols, rows, gain)


def ffn_body(nm_ref, nmt_ref, cot_ref, cott_ref, w_ref, dw_ref, out_ref, gnm_ref):
    @pl.when(pl.program_id(0) == 0)
    def _():
        out_ref[...] = jnp.zeros_like(out_ref)
        gnm_ref[...] = jnp.zeros_like(gnm_ref)

    w = w_ref[...]
    gate_up = jnp.dot(nm_ref[...], w[:, : 2 * TILE], preferred_element_type=F32)
    gate, up = gate_up[:, :TILE], gate_up[:, TILE:]
    sig = sigmoid(gate)
    swish = gate * sig
    hidden = (swish * up).astype(BF16)
    grad_hidden = jnp.dot(cot_ref[...], w[:, 2 * TILE :], preferred_element_type=F32)
    grad_gate = grad_hidden * up * (sig + swish * (1.0 - sig))
    grad_up = grad_hidden * swish
    grad_low = jnp.concatenate([grad_gate, grad_up], axis=1).astype(BF16)
    out_ref[...] += lax.dot_general(hidden, w[:, 2 * TILE :], (NT, ((), ())), preferred_element_type=F32)
    gnm_ref[...] += lax.dot_general(grad_low, w[:, : 2 * TILE], (NT, ((), ())), preferred_element_type=F32)
    dw_ref[:, : 2 * TILE] = jnp.dot(nmt_ref[...], grad_low, preferred_element_type=F32).astype(BF16)
    dw_ref[:, 2 * TILE :] = jnp.dot(cott_ref[...], hidden, preferred_element_type=F32).astype(BF16)


def ffn(nm, nmt, cot, cott, w):
    tokens, width = nm.shape
    tiles = w.shape[1] // (3 * TILE)
    const = lambda t: (0, 0)
    by_tile = lambda t: (0, t)
    return pl.pallas_call(
        ffn_body,
        grid=(tiles,),
        in_specs=[
            pl.BlockSpec((tokens, width), const),
            pl.BlockSpec((width, tokens), const),
            pl.BlockSpec((tokens, width), const),
            pl.BlockSpec((width, tokens), const),
            pl.BlockSpec((width, 3 * TILE), by_tile),
        ],
        out_specs=[
            pl.BlockSpec((width, 3 * TILE), by_tile),
            pl.BlockSpec((tokens, width), const),
            pl.BlockSpec((tokens, width), const),
        ],
        out_shape=[
            jax.ShapeDtypeStruct((width, tiles * 3 * TILE), BF16),
            jax.ShapeDtypeStruct((tokens, width), F32),
            jax.ShapeDtypeStruct((tokens, width), F32),
        ],
        compiler_params=pltpu.CompilerParams(vmem_limit_bytes=48 * MIB),
        name="ffn",
    )(nm, nmt, cot, cott, w)


def flip(number, bit):
    return number + bit - 2 * bit * ((number // bit) % 2)


def z_partner(me, planes, k):
    other = me
    bit = 1
    while bit < planes:
        if k & bit:
            other = flip(other, 8 * bit)
        bit *= 2
    return other


def z_of(plane, planes, k):
    bit = 1
    while bit < planes:
        if k & bit:
            plane = flip(plane, bit)
        bit *= 2
    return plane


def enter(planes):
    me = lax.axis_index("dp")
    barrier = pltpu.get_barrier_semaphore()
    partners = [flip(me, 1), flip(me, 2), flip(me, 4)]
    partners += [z_partner(me, planes, k) for k in range(1, planes)]
    for other in partners:
        pl.semaphore_signal(barrier, inc=1, device_id=(other,), device_id_type=MESH)
    pl.semaphore_wait(barrier, len(partners))
    return me


class Gather:
    def __init__(self, me, planes, shards, fulls, chunks, local_sem, send_sem, recv_sem):
        self.me, self.planes, self.shards, self.fulls, self.chunks = me, planes, shards, fulls, chunks
        self.local_sem, self.send_sem, self.recv_sem = local_sem, send_sem, recv_sem
        self.plane, self.place = me // 8, me % 8
        self.copies = {}

    def slot(self, k, place):
        array, start, size, _ = self.chunks[k]
        return self.fulls[array].at[:, place, :, pl.ds(start, size)]

    def send(self, k, number, source, target, other):
        copy = pltpu.make_async_remote_copy(
            src_ref=source,
            dst_ref=target,
            send_sem=self.send_sem.at[k, number],
            recv_sem=self.recv_sem.at[k, number],
            device_id=(other,),
            device_id_type=MESH,
        )
        copy.start()
        self.copies[k, number] = copy

    def forward(self, k, number, place, other):
        self.send(k, number, self.slot(k, place), self.slot(k, place), other)

    def planes_step(self, k):
        array, start, size, _ = self.chunks[k]
        own = self.shards[array].at[:, pl.ds(start, size)]
        home = self.fulls[array].at[self.plane, self.place, :, pl.ds(start, size)]
        local = pltpu.make_async_copy(own, home, self.local_sem.at[k])
        local.start()
        self.copies[k, "local"] = local
        for d in range(1, self.planes):
            self.send(k, 6 + d, own, home, z_partner(self.me, self.planes, d))

    def square_step(self, k):
        self.copies[k, "local"].wait()
        for d in range(1, self.planes):
            self.copies[k, 6 + d].wait_recv()
        self.forward(k, 0, self.place, flip(self.me, 2))
        self.forward(k, 1, self.place, flip(self.me, 4))
        self.forward(k, 3, self.place, flip(self.me, 1))

    def diagonal_step(self, k):
        by_y = self.chunks[k][3]
        for number, bit in ((1, 4), (0, 2)) if by_y else ((0, 2), (1, 4)):
            self.copies[k, number].wait_recv()
            place = flip(self.place, bit)
            if number == int(by_y):
                self.forward(k, 2, place, flip(self.me, 6 - bit))
            self.forward(k, 4 + number, place, flip(self.me, 1))

    def core_step(self, k):
        self.copies[k, 2].wait_recv()
        self.forward(k, 6, flip(flip(self.place, 2), 4), flip(self.me, 1))

    def finish(self, k):
        for number in (3, 4, 5, 6):
            self.copies[k, number].wait_recv()
        for number in range(6 + self.planes):
            self.copies[k, number].wait_send()


def gather_body(planes, chunks, count, *refs):
    shards, fulls = refs[:count], refs[count : 2 * count]
    me = enter(planes)
    work = Gather(me, planes, shards, fulls, chunks, *refs[2 * count :])
    total = len(chunks)
    for k in range(-2, total + 2):
        for ahead, step in ((2, work.planes_step), (0, work.square_step), (-1, work.diagonal_step), (-2, work.core_step)):
            if 0 <= k + ahead < total:
                step(k + ahead)
    for k in range(total):
        work.finish(k)


def gather_all(devices, shards, chunks):
    rows = shards[0].shape[0]
    planes = devices // 8
    hbm = pl.BlockSpec(memory_space=pl.ANY)
    fulls = pl.pallas_call(
        partial(gather_body, planes, chunks, len(shards)),
        in_specs=[hbm] * len(shards),
        out_specs=[hbm] * len(shards),
        out_shape=[jax.ShapeDtypeStruct((planes, 8, rows, s.shape[1]), s.dtype) for s in shards],
        scratch_shapes=[
            pltpu.SemaphoreType.DMA((len(chunks),)),
            pltpu.SemaphoreType.DMA((len(chunks), 6 + planes)),
            pltpu.SemaphoreType.DMA((len(chunks), 6 + planes)),
        ],
        compiler_params=pltpu.CompilerParams(collective_id=0, has_side_effects=True),
        name="gather_weights",
    )(*shards)
    return [f.reshape(devices * rows, f.shape[-1]) for f in fulls]


class Scatter:
    def __init__(self, me, planes, grads, out_ref, chunks, from_core, keep, from_x, from_y, from_xy, from_z,
                 local_sem, send_sem, recv_sem):
        self.me, self.planes, self.grads, self.out_ref, self.chunks = me, planes, grads, out_ref, chunks
        self.from_core, self.keep = from_core, keep
        self.from_x, self.from_y, self.from_xy, self.from_z = from_x, from_y, from_xy, from_z
        self.local_sem, self.send_sem, self.recv_sem = local_sem, send_sem, recv_sem
        self.plane, self.core = me // 8, me % 2
        self.here = (me // 2) % 4
        self.copies = {}

    def send(self, k, number, source, target, other):
        copy = pltpu.make_async_remote_copy(
            src_ref=source,
            dst_ref=target,
            send_sem=self.send_sem.at[k, number],
            recv_sem=self.recv_sem.at[k, number],
            device_id=(other,),
            device_id_type=MESH,
        )
        copy.start()
        self.copies[k, number] = copy

    def span(self, k):
        return pl.ds(self.chunks[k][4], self.chunks[k][2])

    def core_step(self, k):
        array, start, size, _, _ = self.chunks[k]
        source = self.grads[array].at[:, :, 1 - self.core, :, pl.ds(start, size)]
        self.send(k, 0, source, self.from_core.at[:, :, :, self.span(k)], flip(self.me, 1))
        mine = self.grads[array].at[:, :, self.core, :, pl.ds(start, size)]
        local = pltpu.make_async_copy(mine, self.keep.at[k % 2, :, :, :, pl.ds(0, size)], self.local_sem.at[k])
        local.start()
        self.copies[k, "local"] = local

    def add(self, k, place, others):
        span = self.span(k)

        def one(plane, carry):
            total = self.from_core[plane, place, :, span].astype(F32)
            for read in others:
                total = total + read(plane).astype(F32)
            self.from_core[plane, place, :, span] = total.astype(BF16)
            return carry

        lax.fori_loop(0, self.planes, one, 0)

    def chip_step(self, k):
        size, by_y = self.chunks[k][2], self.chunks[k][3]
        span = self.span(k)
        self.copies[k, 0].wait_recv()
        self.copies[k, "local"].wait()
        across_x, across_y = flip(self.here, 1), flip(self.here, 2)
        both = flip(across_x, 2)
        order = (both, across_y, across_x) if by_y else (both, across_x, across_y)
        for place in order + (self.here,):
            self.add(k, place, [lambda plane, place=place: self.keep[k % 2, plane, place, :, pl.ds(0, size)]])
            if place is both:
                source = self.from_core.at[:, both, :, span]
                self.send(k, 1, source, self.from_xy.at[:, :, span], flip(self.me, 4 if by_y else 2))
            elif place is order[1]:
                if by_y:
                    self.send_y(k)
                else:
                    self.send_x(k)

    def send_x(self, k):
        span = self.span(k)
        self.send(k, 2, self.from_core.at[:, flip(self.here, 1), :, span], self.from_x.at[:, :, span], flip(self.me, 2))

    def send_y(self, k):
        span = self.span(k)
        self.send(k, 3, self.from_core.at[:, flip(self.here, 2), :, span], self.from_y.at[:, :, span], flip(self.me, 4))

    def diagonal_step(self, k):
        by_y = self.chunks[k][3]
        span = self.span(k)
        self.copies[k, 1].wait_recv()
        place = flip(self.here, 1 if by_y else 2)
        self.add(k, place, [lambda plane: self.from_xy[plane, :, span]])
        if by_y:
            self.send_x(k)
        else:
            self.send_y(k)

    def square_step(self, k):
        span = self.span(k)
        self.copies[k, 2].wait_recv()
        self.copies[k, 3].wait_recv()
        self.add(k, self.here, [lambda plane: self.from_x[plane, :, span], lambda plane: self.from_y[plane, :, span]])
        for d in range(1, self.planes):
            source = self.from_core.at[z_of(self.plane, self.planes, d), self.here, :, span]
            self.send(k, 3 + d, source, self.from_z.at[d - 1, :, span], z_partner(self.me, self.planes, d))

    def planes_step(self, k):
        span = self.span(k)
        total = self.from_core[self.plane, self.here, :, span].astype(F32)
        for d in range(1, self.planes):
            self.copies[k, 3 + d].wait_recv()
            total = total + self.from_z[d - 1, :, span].astype(F32)
        self.out_ref[:, span] = total

    def finish(self, k):
        for number in range(3 + self.planes):
            self.copies[k, number].wait_send()


class Total:
    def __init__(self, me, planes, value_ref, out_ref, got, stage, send_sem, recv_sem):
        self.me, self.planes, self.value_ref, self.out_ref = me, planes, value_ref, out_ref
        self.got, self.stage, self.send_sem, self.recv_sem = got, stage, send_sem, recv_sem
        self.copies = {}

    def send(self, number, source, target, other):
        copy = pltpu.make_async_remote_copy(
            src_ref=source, dst_ref=target, send_sem=self.send_sem.at[number], recv_sem=self.recv_sem.at[number],
            device_id=(other,), device_id_type=MESH,
        )
        copy.start()
        self.copies[number] = copy

    def step(self, number):
        planes, plane = self.planes, self.me // 8
        if number == 0:
            self.stage[0] = self.value_ref[...]
        elif number <= 3:
            self.copies[number - 1].wait_recv()
            self.stage[number] = self.stage[number - 1] + self.got[number - 1]
        if number < 3:
            self.send(number, self.stage.at[number], self.got.at[number], flip(self.me, 1 << number))
        elif number == 3:
            for d in range(1, planes):
                self.send(2 + d, self.stage.at[3], self.got.at[3 + plane], z_partner(self.me, planes, d))
            self.got[3 + plane] = self.stage[3]
        else:
            for d in range(1, planes):
                self.copies[2 + d].wait_recv()
            total = self.got[3]
            for other in range(1, planes):
                total = total + self.got[3 + other]
            self.out_ref[...] = total
            for number in range(2 + planes):
                self.copies[number].wait_send()


def scatter_body(planes, chunks, count, *refs):
    grads, value_ref, out_ref, total_ref = refs[:count], refs[count], refs[count + 1], refs[count + 2]
    me = enter(planes)
    work = Scatter(me, planes, grads, out_ref, chunks, *refs[count + 3 : count + 12])
    small = Total(me, planes, value_ref, total_ref, *refs[count + 12 :])
    total = len(chunks)
    for k in range(-1, total + 3):
        stages = (
            (-3, work.planes_step),
            (-2, work.square_step),
            (-1, work.diagonal_step),
            (0, work.chip_step),
            (1, work.core_step),
        )
        for ahead, step in stages:
            if 0 <= k + ahead < total:
                step(k + ahead)
        if 0 <= k < 5:
            small.step(k)
    for k in range(total):
        work.finish(k)


def scatter_all(devices, grads, value, chunks):
    rows = grads[0].shape[0] // devices
    planes = devices // 8
    width = sum(c[2] for c in chunks)
    widest = max(c[2] for c in chunks)
    hbm = pl.BlockSpec(memory_space=pl.ANY)
    whole = pl.BlockSpec(memory_space=pltpu.VMEM)
    kinds = 3 + planes
    return pl.pallas_call(
        partial(scatter_body, planes, chunks, len(grads)),
        in_specs=[hbm] * len(grads) + [whole],
        out_specs=[whole, whole],
        out_shape=[jax.ShapeDtypeStruct((rows, width), F32), jax.ShapeDtypeStruct(value.shape, F32)],
        scratch_shapes=[
            pltpu.VMEM((planes, 4, rows, width), BF16),
            pltpu.VMEM((2, planes, 4, rows, widest), BF16),
            pltpu.VMEM((planes, rows, width), BF16),
            pltpu.VMEM((planes, rows, width), BF16),
            pltpu.VMEM((planes, rows, width), BF16),
            pltpu.VMEM((planes - 1, rows, width), BF16),
            pltpu.SemaphoreType.DMA((len(chunks),)),
            pltpu.SemaphoreType.DMA((len(chunks), kinds)),
            pltpu.SemaphoreType.DMA((len(chunks), kinds)),
            pltpu.VMEM((3 + planes,) + value.shape, F32),
            pltpu.VMEM((4,) + value.shape, F32),
            pltpu.SemaphoreType.DMA((2 + planes,)),
            pltpu.SemaphoreType.DMA((2 + planes,)),
        ],
        compiler_params=pltpu.CompilerParams(
            collective_id=1, has_side_effects=True, vmem_limit_bytes=60 * MIB
        ),
        name="scatter_grads",
    )(*[g.reshape(planes, 4, 2, rows, g.shape[1]) for g in grads], value)


def cut(chunk_sizes, widths):
    chunks, at = [], 0
    for array, sizes in enumerate(chunk_sizes):
        start = 0
        for size in sizes:
            chunks.append((array, start, size, len(chunks) % 2 == 1, at))
            start, at = start + size, at + size
        assert start == widths[array]
    return chunks


def rms_scale(values):
    return lax.rsqrt(jnp.mean(values * values, axis=-1, keepdims=True) + epsilon)


def rms_back(grad, values, scale, gain):
    normed = values * scale
    d_normed = grad * gain
    d_values = scale * (d_normed - normed * jnp.mean(d_normed * normed, axis=-1, keepdims=True))
    return d_values, jnp.sum(grad * normed, axis=0)


def by_head(parts):
    shaped = [p.reshape(p.shape[0], HEADS, -1) for p in parts]
    return jnp.concatenate(shaped, axis=2).reshape(parts[0].shape[0], -1)


def from_head(values, sizes):
    shaped = values.reshape(values.shape[0], HEADS, -1)
    ends = [sum(sizes[: i + 1]) for i in range(len(sizes))]
    cuts = [shaped[:, :, e - s : e].reshape(values.shape[0], -1) for s, e in zip(sizes, ends)]
    return jnp.concatenate(cuts, axis=1)


def split_heads(values):
    key = HEADS * DK
    val = HEADS * DV
    edges = [0, key, 2 * key, 2 * key + val, 2 * key + 2 * val]
    return [values[:, a:b] for a, b in zip(edges[:-1], edges[1:]) if b <= values.shape[1]]


def on_device(
    devices, tokens, segment_ids, cotangent, norm1_gain, mixer_in, decay_in, conv_weight, decay_log, decay_bias,
    head_gain, mixer_out, norm2_gain, ffn_in, ffn_out,
):
    rows, width = decay_in.shape[0], tokens.shape[1]
    count = tokens.shape[0]
    hidden = ffn_out.shape[0]
    tiles = hidden // TILE
    direct = rows % 16 == 0 and devices % 8 == 0

    low = lambda v: v.astype(BF16)
    shard_mixer = by_head(split_heads(low(mixer_in)))
    conv_cols = conv_weight.shape[1]
    shard_small = jnp.concatenate(
        [low(decay_in), low(norm1_gain)[:, None], low(norm2_gain)[:, None], low(conv_weight).reshape(rows, -1)], axis=1
    )
    shard_small = jnp.pad(shard_small, ((0, 0), (0, SMALL - shard_small.shape[1])))
    shard_out = low(mixer_out).T
    ffn_low = low(ffn_in)
    pieces = [ffn_low[:, :hidden], ffn_low[:, hidden:], low(ffn_out).T]
    shard_ffn = jnp.concatenate([p.reshape(rows, tiles, TILE) for p in pieces], axis=2).reshape(rows, -1)
    shards = [shard_small, shard_mixer, shard_out, shard_ffn]

    x = tokens.astype(F32)
    scale1 = rms_scale(x)
    if direct:
        sizes = [[SMALL], [768, 1536, 1536, 2304], [2048], [1536] * 5 + [768]]
        full_small, full_mixer, full_out, full_ffn = gather_all(
            devices, shards, [c[:4] for c in cut(sizes, [s.shape[1] for s in shards])]
        )
    else:
        full_small, full_mixer, full_out, full_ffn = [
            lax.all_gather(s, "dp", axis=0, tiled=True) for s in shards
        ]

    decay_full = full_small[:, :16]
    gain1 = full_small[:, 16].astype(F32)
    gain2 = full_small[:, 17].astype(F32)
    taps = full_small[:, 18 : 18 + 16].reshape(devices, 4, conv_cols)
    taps = jnp.moveaxis(taps, 0, 1).reshape(4, -1).astype(F32)
    taps = by_head(split_heads(taps))

    normed_in = low(x * scale1 * gain1)
    logits = jnp.dot(normed_in, decay_full, preferred_element_type=F32)
    shifted = logits[:, :HEADS] + decay_bias
    log_decay = -jnp.exp(decay_log) * jax.nn.softplus(shifted)
    rate = jax.nn.sigmoid(logits[:, HEADS:])
    sequences = count // SEQ
    lower = jnp.tril(jnp.ones((SEQ, SEQ), F32))
    cumulative = jnp.einsum(
        "ij,sjh->sih", lower, log_decay.reshape(sequences, SEQ, HEADS), precision=lax.Precision.HIGHEST
    ).reshape(count, HEADS)
    position = jnp.arange(count) % SEQ
    keeps = []
    for back in (1, 2, 3):
        earlier = jnp.pad(segment_ids[:-back], (back, 0), constant_values=-1)
        keeps.append(((earlier == segment_ids) & (position >= back)).astype(F32)[:, None])
    segment = segment_ids.astype(F32)
    cols = jnp.concatenate([cumulative, rate] + keeps + [segment[:, None]], axis=1)
    cols = jnp.pad(cols, ((0, 0), (0, 128 - cols.shape[1])))
    seq_rows = jnp.concatenate([cumulative.T, segment[None], jnp.zeros((7, count), F32)], axis=0)
    gain_row = head_gain[None]

    proj, mixed, inverse, update, core = mixer_fwd(normed_in, full_mixer, taps, cols, seq_rows, gain_row)

    middle = x + lax.dot_general(mixed, full_out, (NT, ((), ())), preferred_element_type=F32)
    scale2 = rms_scale(middle)
    normed_mid = low(middle * scale2 * gain2)
    dw_ffn, ffn_sum, grad_nm = ffn(normed_mid, normed_mid.T, cotangent, cotangent.T, full_ffn)
    output = low(middle + ffn_sum)

    d_middle, d_gain2 = rms_back(grad_nm, middle, scale2, gain2)
    grad_middle = d_middle + cotangent.astype(F32)
    branch = low(grad_middle)
    dw_mixer, dw_out, grad_xn, d_cols, d_rows, d_taps, d_gain = mixer_bwd(
        branch, branch.T, normed_in.T, full_out, full_mixer, proj, mixed, inverse, update, core,
        taps, cols, seq_rows, gain_row,
    )

    d_cum = d_cols[:, 8:16] - d_rows.T
    d_decay = jnp.einsum(
        "ji,sjh->sih", lower, d_cum.reshape(sequences, SEQ, HEADS), precision=lax.Precision.HIGHEST
    ).reshape(count, HEADS)
    d_shifted = -d_decay * jnp.exp(decay_log) * jax.nn.sigmoid(shifted)
    d_rate = d_cols[:, :8] * rate * (1.0 - rate)
    d_logits = low(jnp.concatenate([d_shifted, d_rate], axis=1))
    grad_xn = grad_xn + lax.dot_general(d_logits, decay_full, (NT, ((), ())), preferred_element_type=F32)
    d_x, d_gain1 = rms_back(grad_xn, x, scale1, gain1)
    input_grad = d_x + grad_middle

    d_decay_in = lax.dot_general(normed_in, d_logits, (TN, ((), ())), preferred_element_type=F32)
    d_taps = from_head(d_taps, [DK, DK, DV])
    d_taps = jnp.moveaxis(d_taps.reshape(4, devices, conv_cols), 1, 0).reshape(width, -1)
    dw_small = jnp.concatenate([d_decay_in, d_gain1[:, None], d_gain2[:, None], d_taps], axis=1)
    dw_small = low(jnp.pad(dw_small, ((0, 0), (0, SMALL - dw_small.shape[1]))))
    shared = jnp.concatenate([jnp.sum(d_decay * log_decay, axis=0), jnp.sum(d_shifted, axis=0), d_gain[0]])

    if direct:
        grads = [dw_ffn, dw_out, dw_mixer, dw_small]
        sizes = [[1536] * 5 + [768], [2048], [1536] * 4, [SMALL]]
        block = jnp.pad(shared, (0, 1024 - shared.shape[0])).reshape(8, 128)
        own, total = scatter_all(devices, grads, block, cut(sizes, [g.shape[1] for g in grads]))
        shared = total.reshape(-1)
        edges = [0]
        for g in grads:
            edges.append(edges[-1] + g.shape[1])
        own_ffn, own_out, own_mixer, own_small = [own[:, a:b] for a, b in zip(edges[:-1], edges[1:])]
    else:
        own_ffn, own_out, own_mixer, own_small = [
            lax.psum_scatter(g.astype(F32), "dp", scatter_dimension=0, tiled=True)
            for g in (dw_ffn, dw_out, dw_mixer, dw_small)
        ]
        shared = lax.psum(shared, "dp")

    own_tiles = own_ffn.reshape(rows, tiles, 3, TILE)
    ffn_in_grad = jnp.concatenate([own_tiles[:, :, i].reshape(rows, hidden) for i in (0, 1)], axis=1)
    ffn_out_grad = own_tiles[:, :, 2].reshape(rows, hidden).T
    return (
        output,
        input_grad,
        own_small[:, 16],
        from_head(own_mixer, [DK, DK, DV, DV]),
        own_small[:, :16],
        own_small[:, 18 : 18 + 16].reshape(4, conv_cols),
        shared[:HEADS],
        shared[HEADS : 2 * HEADS],
        shared[2 * HEADS : 2 * HEADS + DV],
        own_out.T,
        own_small[:, 17],
        ffn_in_grad,
        ffn_out_grad,
    )


def solution(mesh):
    in_specs = (
        P("dp", None), P("dp"), P("dp", None), P("dp"), P("dp", None), P("dp", None), P(None, "dp"), P(), P(), P(),
        P(None, "dp"), P("dp"), P("dp", None), P(None, "dp"),
    )
    out_specs = (
        P("dp", None), P("dp", None), P("dp"), P("dp", None), P("dp", None), P(None, "dp"), P(), P(), P(),
        P(None, "dp"), P("dp"), P("dp", None), P(None, "dp"),
    )
    return jax.shard_map(
        partial(on_device, mesh.shape["dp"]), mesh=mesh, in_specs=in_specs, out_specs=out_specs, check_vma=False
    )
```

time: 1980 us -> 576 us (0.29)
  waiting for transfers between devices: 861 us -> 0 us
  matrix products: 558 us -> 11.6 us
  Pallas kernels: 0 us -> 483 us
  blocking collectives: 159 us -> 0 us
  other arithmetic: 176 us -> 26.5 us
  local copies, waits for them, and re-layouts: 194 us -> 49.1 us
    reduce_scatter x3 -> x0, waiting for transfers between devices: 643 us -> none  [the longest x1 249 us: on_device(): lax.psum_scatter(local[6], 'dp', scatter_dimension=0, tiled=True)]
    dot_general x204 -> x6, matrix products: 556 us -> 11.6 us  [the longest x1 5.33 us: on_device(): lax.dot_general(mixed, full_out, (NT, ((), ())), preferred_element_type=F32)]
    pallas_call x0 -> x5, Pallas kernels: none -> 483 us  [the longest x1 195 us: scatter_all(): pl.pallas_call(partial(scatter_body, planes, chunks, len(grads)), in_spec...]
    unnamed x13 -> x0, waiting for transfers between devices: 218 us -> none
    unnamed x2 -> x0, blocking collectives: 80.5 us -> none
    all_gather x2 -> x0, blocking collectives: 78.7 us -> none  [the longest x1 41.8 us: on_device(): lax.all_gather(decay_in.astype(jnp.bfloat16), 'dp', axis=0, tiled=True)]
    unnamed x631 -> x80, local copies, waits for them, and re-layouts: 70.7 us -> 13.1 us
    reduce_sum x27 -> x2, other arithmetic: 55.5 us -> 2.57 us  [the longest x1 2.34 us: rms_back(): return (d_values, jnp.sum(grad * normed, axis=0))]
  transfers between devices with their start and end apart: 10 -> 0, of which waited for: 5 -> 0; matrix products, arithmetic and copies ran while one was open for 24% -> 0% of each run, Pallas kernels for 0% -> 0%
where the time goes in v1:
time: 576 us; the launch traced here: 572 us
  Pallas kernels  483 us (84%)
  local copies, waits for them, and re-layouts  49.1 us (9%)
  other arithmetic  26.5 us (5%)
  matrix products  11.6 us (2%)
    pallas_call x1, Pallas kernels, scatter_all(): pl.pallas_call(partial(scatter_body, planes, chunks, len(grads)), in_spec...  195 us
    pallas_call x1, Pallas kernels, gather_all(): pl.pallas_call(partial(gather_body, planes, chunks, len(shards)), in_spec...  159 us
    pallas_call x1, Pallas kernels, mixer_bwd(): pl.pallas_call(mixer_bwd_body, grid=(HEADS,), in_specs=[pl.BlockSpec((tok...  49.5 us
    pallas_call x1, Pallas kernels, mixer_fwd(): pl.pallas_call(mixer_fwd_body, grid=(HEADS,), in_specs=[pl.BlockSpec((tok...  46.8 us
    pallas_call x1, Pallas kernels, ffn(): pl.pallas_call(ffn_body, grid=(tiles,), in_specs=[pl.BlockSpec((tokens, w...  33 us
    unnamed x80, local copies, waits for them, and re-layouts  13.1 us

profile of v1, /device:TPU:0, one launch (start us, length us, event | category | flops | bytes accessed | tf_op | source)
XLA Modules:
  0.0 572.4 jit_solution(4652697251740589619)
XLA Ops:
  6.4 159.3 %gather_weights.1 = (bf16[4,8,32,128]{3,2,1,0:T(8,128)(2,1)}, bf16[4,8,32,6144]{3,2,1,0:T(8,128)(2,1)}, bf16[4,8,32,2048]{3,2,1,0:T(8,128)(2,1)}, bf16[4,8,32,8448]{3,2,1,0:T(8,128)(2,1)}) custom-call(bf16[32,128]{1,0:T(8,128)(2,1)} %fusion.36.refs_0_, bf16[32,6144]{1,0:T(8,128)(2,1)} %bitcast.159, bf16[32,2048]{1,0:T(8,128)(2,1)} %convert_bitcast_fusion.1.refs_2_, ...), custom_call_target="tpu_custom_call" | custom-call | tf_op jit(solution)/shard_map/gather_weights/pallas_call | solution.py:471
  174.1 46.8 %mixer_fwd.1 = (f32[512,6144]{1,0:T(8,128)}, bf16[512,2048]{1,0:T(8,128)(2,1)}, bf16[8,512,256]{2,1,0:T(8,128)(2,1)}, f32[8,512,256]{2,1,0:T(8,128)}, f32[8,512,256]{2,1,0:T(8,128)}) custom-call(bf16[512,1024]{1,0:T(8,128)(2,1)} %copy.79.xn_ref, bf16[1024,6144]{1,0:T(8,128)(2,1)} %bitcast.137, f32[4,4096]{1,0:T(4,128)} %bitcast.168, ...), custom_call_target="tpu_custom_call" | custom-call | tf_op jit(solution)/shard_map/mixer_fwd/pallas_call | solution.py:145
  220.9 5.3 multiply_reduce_fusion.2
  226.6 1.9 fusion.72.nmt_ref
  228.5 1.9 multiply_convert_fusion
  233.5 33.0 %ffn.1 = (bf16[1024,8448]{1,0:T(8,128)(2,1)}, f32[512,1024]{1,0:T(8,128)}, f32[512,1024]{1,0:T(8,128)}) custom-call(bf16[512,1024]{1,0:T(8,128)(2,1)S(1)} %copy-done.1, bf16[1024,512]{1,0:T(8,128)(2,1)S(1)} %fusion.72.nmt_ref, bf16[512,1024]{1,0:T(8,128)(2,1)S(1)} %copy-done, bf16[1024,512]{1,0:T(8,128)(2,1)S(1)} %bitcast.136, bf16[1024,8448]{1,0:T(8,128)(2,1)} %bitcast.140), custom_call_target="tpu_custom_call" | custom-call | tf_op jit(solution)/shard_map/ffn/pallas_call | solution.py:331
  266.5 3.1 copy.86
  269.6 2.3 multiply_reduce_fusion
  271.9 1.6 fusion.56
  273.5 2.3 copy.88.gb_ref
  275.8 2.5 fusion.71.xnt_ref
  278.3 49.5 %mixer_bwd.1 = (bf16[1024,6144]{1,0:T(8,128)(2,1)}, bf16[1024,2048]{1,0:T(8,128)(2,1)}, f32[512,1024]{1,0:T(8,128)}, f32[512,128]{1,0:T(8,128)}, f32[8,512]{1,0:...) custom-call(bf16[512,1024]{1,0:T(8,128)(2,1)} %copy.88.gb_ref, bf16[1024,512]{1,0:T(8,128)(2,1)} %bitcast.142, ...), custom_call_target="tpu_custom_call" | custom-call | tf_op jit(solution)/shard_map/mixer_bwd/pallas_call | solution.py:261
  327.8 1.8 copy.90
  332.2 1.6 convolution_convert_fusion
  335.7 1.7 copy.95
  337.3 3.1 copy.92
  340.5 3.9 fusion.9
  345.4 195.0 %scatter_grads.1 = (f32[32,16768]{1,0:T(8,128)}, f32[8,128]{1,0:T(8,128)}) custom-call(bf16[4,4,2,32,8448]{4,3,2,1,0:T(8,128)(2,1)} %bitcast.139, bf16[4,4,2,32,2048]{4,3,2,1,0:T(8,128)(2,1)} %bitcast.148, bf16[4,4,2,32,6144]{4,3,2,1,0:T(8,128)(2,1)} %bitcast.141, bf16[4,4,2,32,128]{4,3,2,1,0:T(8,128)(2,1)} %bitcast.163, f32[8,128]{1,0:T(8,128)} %fusion.37.refs_4_), custom_call_target="tpu_custom_call" | custom-call | tf_op jit(solution)/shard_map/scatter_grads/pallas_call | solution.py:663
  540.4 2.3 slice.164
  542.7 2.7 reshape.241
  545.4 5.7 %slice_reduce_fusion = (f32[32,11,256]{2,1,0:T(8,128)S(1)}, f32[32,11,256]{2,1,0:T(8,128)S(1)}, f32[32,11,256]{2,1,0:T(8,128)S(1)}) fusion(f32[32,11,3,256]{3,2,1,0:T(4,128)} %reshape.241), kind=kLoop, calls=%fused_computation.27 | loop fusion | bytes 2162688 | tf_op jit(solution)/shard_map/slice | solution.py:847
  559.9 2.9 copy.85
  562.8 4.9 fusion.8
  567.7 3.0 copy.98
  (147 shorter events, 32.6 us)
Async XLA Ops:
  0.6 2.3 copy-start.11
  2.1 1.2 copy-start.12
  3.1 1.4 copy-start.13
  3.3 2.0 copy-start.16
  3.3 2.0 copy-start.17
  3.3 2.1 copy-start.21
  3.3 2.2 copy-start.22
  3.5 163.3 %copy-start.10 = (bf16[512,1024]{1,0:T(8,128)(2,1)S(1)}, bf16[512,1024]{1,0:T(8,128)(2,1)}, u32[]{:S(2)}) copy-start(bf16[512,1024]{1,0:T(8,128)(2,1)} %param.14) | copy-start | bytes 3145732
  167.5 53.4 %copy-start.3 = (bf16[512,1024]{0,1:T(8,128)(2,1)}, bf16[512,1024]{0,1:T(8,128)(2,1)S(1)}, u32[]{:S(2)}) copy-start(bf16[512,1024]{0,1:T(8,128)(2,1)S(1)} %copy.75) | copy-start | bytes 3145732
  167.5 1.1 copy-start.6
  167.6 1.4 copy-start.23
  167.6 2.0 copy-start.18
  167.9 2.1 copy-start.15
  168.7 4.1 copy-start.5
  174.1 46.8 %copy-start.8 = (bf16[4,8,32,2048]{3,2,1,0:T(8,128)(2,1)S(1)}, bf16[4,8,32,2048]{3,2,1,0:T(8,128)(2,1)}, u32[]{:S(2)}) copy-start(bf16[4,8,32,2048]{3,2,1,0:T(8,128)(2,1)} %get-tuple-element.37) | copy-start | bytes 12582916
  228.4 3.3 copy-start
  232.3 1.2 copy-start.1
  266.5 3.1 copy-start.2
  269.6 2.4 copy-start.4
  278.3 52.3 %copy-start.20 = (f32[8]{0:T(128)S(1)}, f32[8]{0:T(128)}, u32[]{:S(2)}) copy-start(f32[8]{0:T(128)} %get-tuple-element.133) | copy-start | bytes 100
  340.5 4.0 copy-start.14
  551.2 2.3 copy-start.9
  553.8 3.3 copy-start.19
  567.7 3.0 copy-start.7

commit v2 on v1

--- a/solution.py
+++ b/solution.py
@@ -105,6 +105,835 @@
     rate = pick_lane(cols, 8 + head)
     seg = pick_lane(cols, 19)
     return keep, conv, gate, act, q_act * q_scale, k_act * k_scale, value, q_scale, k_scale, cum, rate, seg
+
+
+def flip(number, bit):
+    return number + bit - 2 * bit * ((number // bit) % 2)
+
+
+def flips(number, planes, k, unit):
+    bit = 1
+    while bit < planes:
+        if k & bit:
+            number = flip(number, unit * bit)
+        bit *= 2
+    return number
+
+
+def enter(planes):
+    me = lax.axis_index("dp")
+    barrier = pltpu.get_barrier_semaphore()
+    partners = [flip(me, 1), flip(me, 2), flip(me, 4)]
+    partners += [flips(me, planes, k, 8) for k in range(1, planes)]
+    for other in partners:
+        pl.semaphore_signal(barrier, inc=1, device_id=(other,), device_id_type=MESH)
+    pl.semaphore_wait(barrier, len(partners))
+    return me
+
+
+def columns(k, width):
+    start = k * width
+    return pl.ds(start if isinstance(start, int) else pl.multiple_of(start, 128), width)
+
+
+def remote(source, target, send_sem, recv_sem, other):
+    return pltpu.make_async_remote_copy(
+        src_ref=source, dst_ref=target, send_sem=send_sem, recv_sem=recv_sem,
+        device_id=(other,), device_id_type=MESH,
+    )
+
+
+class Gather:
+    def __init__(self, me, planes, kinds, local_sem, send_sem, recv_sem):
+        self.me, self.planes, self.kinds = me, planes, kinds
+        self.local_sem, self.send_sem, self.recv_sem = local_sem, send_sem, recv_sem
+        self.plane, self.place = me // 8, me % 8
+
+    def local(self, kind, k):
+        shard, full, width, base = self.kinds[kind]
+        cols = columns(k, width)
+        return pltpu.make_async_copy(
+            shard.at[:, cols], full.at[self.plane, self.place, :, cols], self.local_sem.at[base + k]
+        )
+
+    def copy(self, kind, k, number, by_y=False):
+        shard, full, width, base = self.kinds[kind]
+        cols = columns(k, width)
+        me, place = self.me, self.place
+        sems = self.send_sem.at[base + k, number], self.recv_sem.at[base + k, number]
+        if number > 6:
+            home = full.at[self.plane, place, :, cols]
+            return remote(shard.at[:, cols], home, *sems, flips(me, self.planes, number - 6, 8))
+        across_x, across_y = flip(place, 2), flip(place, 4)
+        which, other = (
+            (place, flip(me, 2)),
+            (place, flip(me, 4)),
+            (across_y, flip(me, 2)) if by_y else (across_x, flip(me, 4)),
+            (place, flip(me, 1)),
+            (across_x, flip(me, 1)),
+            (across_y, flip(me, 1)),
+            (flip(across_x, 4), flip(me, 1)),
+        )[number]
+        piece = full.at[:, which, :, cols]
+        return remote(piece, piece, *sems, other)
+
+    def planes_step(self, kind, k):
+        self.local(kind, k).start()
+        for d in range(1, self.planes):
+            self.copy(kind, k, 6 + d).start()
+
+    def square_step(self, kind, k):
+        self.local(kind, k).wait()
+        for d in range(1, self.planes):
+            self.copy(kind, k, 6 + d).wait_recv()
+        for number in (0, 1, 3):
+            self.copy(kind, k, number).start()
+
+    def diagonal_step(self, kind, k):
+        def go(by_y):
+            for number in (1, 0) if by_y else (0, 1):
+                self.copy(kind, k, number).wait_recv()
+                if number == int(by_y):
+                    self.copy(kind, k, 2, by_y).start()
+                self.copy(kind, k, 4 + number).start()
+
+        if isinstance(k, int):
+            go(k % 2 == 1)
+        else:
+            pl.when(k % 2 == 0)(lambda: go(False))
+            pl.when(k % 2 == 1)(lambda: go(True))
+
+    def core_step(self, kind, k):
+        self.copy(kind, k, 2).wait_recv()
+        self.copy(kind, k, 6).start()
+        for number in (3, 4, 5, 6):
+            self.copy(kind, k, number).wait_recv()
+
+    def finish(self, kind, k):
+        for number in range(6 + self.planes):
+            self.copy(kind, k, number).wait_send()
+
+
+class Scatter:
+    depths = {"core": 4, "keep": 2, "sums": 6, "x": 6, "y": 6, "xy": 4, "z": 4}
+
+    def __init__(self, me, planes, kinds, store, core, keep, sums, x, y, xy, z, local_sem, send_sem, recv_sem):
+        self.me, self.planes, self.kinds, self.store = me, planes, kinds, store
+        self.from_core, self.keep, self.sums = core, keep, sums
+        self.from_x, self.from_y, self.from_xy, self.from_z = x, y, xy, z
+        self.local_sem, self.send_sem, self.recv_sem = local_sem, send_sem, recv_sem
+        self.plane, self.core, self.here = me // 8, me % 2, (me // 2) % 4
+
+    def piece(self, r, place, width):
+        return self.sums.at[r % self.depths["sums"], :, place, :, pl.ds(0, width)]
+
+    def copy(self, kind, r, k, number, by_y=False):
+        width, source, _ = self.kinds[kind]
+        cols = pl.ds(0, width)
+        sems = self.send_sem.at[r, number], self.recv_sem.at[r, number]
+        me, here = self.me, self.here
+        if number == 0:
+            target = self.from_core.at[r % self.depths["core"], :, :, :, cols]
+            return remote(source(k, 1 - self.core), target, *sems, flip(me, 1))
+        if number == 1:
+            target = self.from_xy.at[r % self.depths["xy"], :, :, cols]
+            return remote(self.piece(r, flip(flip(here, 1), 2), width), target, *sems, flip(me, 4 if by_y else 2))
+        if number == 2:
+            target = self.from_x.at[r % self.depths["x"], :, :, cols]
+            return remote(self.piece(r, flip(here, 1), width), target, *sems, flip(me, 2))
+        if number == 3:
+            target = self.from_y.at[r % self.depths["y"], :, :, cols]
+            return remote(self.piece(r, flip(here, 2), width), target, *sems, flip(me, 4))
+        d = number - 3
+        own = self.sums.at[r % self.depths["sums"], flips(self.plane, self.planes, d, 1), here, :, cols]
+        target = self.from_z.at[r % self.depths["z"], d - 1, :, cols]
+        return remote(own, target, *sems, flips(me, self.planes, d, 8))
+
+    def load(self, kind, r, k):
+        width, source, in_place = self.kinds[kind]
+        return pltpu.make_async_copy(
+            source(k, self.core), self.keep.at[r % 2, :, :, :, pl.ds(0, width)], self.local_sem.at[r]
+        )
+
+    def core_step(self, kind, r, k):
+        self.copy(kind, r, k, 0).start()
+
+    def load_step(self, kind, r, k):
+        if self.kinds[kind][2] is None:
+            self.load(kind, r, k).start()
+
+    def add(self, kind, r, place, first, others):
+        cols = pl.ds(0, self.kinds[kind][0])
+
+        def one(plane, carry):
+            total = first(plane, cols).astype(F32)
+            for read in others:
+                total = total + read(plane, cols).astype(F32)
+            self.sums[r % self.depths["sums"], plane, place, :, cols] = total.astype(BF16)
+            return carry
+
+        lax.fori_loop(0, self.planes, one, 0)
+
+    def held(self, r, place):
+        return lambda plane, cols: self.sums[r % self.depths["sums"], plane, place, :, cols]
+
+    def chip_step(self, kind, r, k):
+        width, _, in_place = self.kinds[kind]
+        self.copy(kind, r, k, 0).wait_recv()
+        if in_place is None:
+            self.load(kind, r, k).wait()
+            mine = lambda place: (lambda plane, cols: self.keep[r % 2, plane, place, :, cols])
+        else:
+            mine = lambda place: (lambda plane, cols: in_place(k, plane, place, self.core))
+        got = lambda place: (lambda plane, cols: self.from_core[r % self.depths["core"], plane, place, :, cols])
+        across_x, across_y = flip(self.here, 1), flip(self.here, 2)
+        both = flip(across_x, 2)
+
+        def go(by_y):
+            self.add(kind, r, both, got(both), [mine(both)])
+            self.copy(kind, r, k, 1, by_y).start()
+            if by_y:
+                self.add(kind, r, across_y, got(across_y), [mine(across_y)])
+                self.copy(kind, r, k, 3).start()
+                self.add(kind, r, across_x, got(across_x), [mine(across_x)])
+            else:
+                self.add(kind, r, across_x, got(across_x), [mine(across_x)])
+                self.copy(kind, r, k, 2).start()
+                self.add(kind, r, across_y, got(across_y), [mine(across_y)])
+
+        pl.when(r % 2 == 0)(lambda: go(False))
+        pl.when(r % 2 == 1)(lambda: go(True))
+        self.add(kind, r, self.here, got(self.here), [mine(self.here)])
+        self.copy(kind, r, k, 0).wait_send()
+
+    def diagonal_step(self, kind, r, k):
+        self.copy(kind, r, k, 1).wait_recv()
+
+        def go(by_y):
+            place = flip(self.here, 1 if by_y else 2)
+            passed = lambda plane, cols: self.from_xy[r % self.depths["xy"], plane, :, cols]
+            self.add(kind, r, place, self.held(r, place), [passed])
+            self.copy(kind, r, k, 2 if by_y else 3).start()
+
+        pl.when(r % 2 == 0)(lambda: go(False))
+        pl.when(r % 2 == 1)(lambda: go(True))
+
+    def square_step(self, kind, r, k):
+        self.copy(kind, r, k, 2).wait_recv()
+        self.copy(kind, r, k, 3).wait_recv()
+        from_x = lambda plane, cols: self.from_x[r % self.depths["x"], plane, :, cols]
+        from_y = lambda plane, cols: self.from_y[r % self.depths["y"], plane, :, cols]
+        self.add(kind, r, self.here, self.held(r, self.here), [from_x, from_y])
+        for d in range(1, self.planes):
+            self.copy(kind, r, k, 3 + d).start()
+
+    def planes_step(self, kind, r, k):
+        cols = pl.ds(0, self.kinds[kind][0])
+        total = self.held(r, self.here)(self.plane, cols).astype(F32)
+        for d in range(1, self.planes):
+            self.copy(kind, r, k, 3 + d).wait_recv()
+            total = total + self.from_z[r % self.depths["z"], d - 1, :, cols].astype(F32)
+        self.store(kind, k, total)
+        for number in range(1, 3 + self.planes):
+            self.copy(kind, r, k, number).wait_send()
+
+
+class Total:
+    def __init__(self, me, planes, value_ref, out_ref, got, stage, send_sem, recv_sem):
+        self.me, self.planes, self.value_ref, self.out_ref = me, planes, value_ref, out_ref
+        self.got, self.stage, self.send_sem, self.recv_sem = got, stage, send_sem, recv_sem
+
+    def copy(self, number):
+        sems = self.send_sem.at[number], self.recv_sem.at[number]
+        if number < 3:
+            return remote(self.stage.at[number], self.got.at[number], *sems, flip(self.me, 1 << number))
+        other = flips(self.me, self.planes, number - 2, 8)
+        return remote(self.stage.at[3], self.got.at[3 + self.me // 8], *sems, other)
+
+    def step(self, number):
+        planes = self.planes
+        if number == 0:
+            self.stage[0] = self.value_ref[...]
+        elif number <= 3:
+            self.copy(number - 1).wait_recv()
+            self.stage[number] = self.stage[number - 1] + self.got[number - 1]
+        if number < 3:
+            self.copy(number).start()
+        elif number == 3:
+            for d in range(1, planes):
+                self.copy(2 + d).start()
+            self.got[3 + self.me // 8] = self.stage[3]
+        else:
+            for d in range(1, planes):
+                self.copy(2 + d).wait_recv()
+            total = self.got[3]
+            for other in range(1, planes):
+                total = total + self.got[3 + other]
+            self.out_ref[...] = total
+            for number in range(2 + planes):
+                self.copy(number).wait_send()
+
+
+def triangle_sum(values, dims):
+    rows, cols = grid_of(SEQ)
+    ones = jnp.where(rows >= cols, 1.0, 0.0).astype(BF16)
+    first, rest = values.astype(BF16), values - values.astype(BF16).astype(F32)
+    second, third = split(rest)
+    return dot1(ones, first, dims) + (dot1(ones, second, dims) + dot1(ones, third, dims))
+
+
+def log1p(value):
+    series = value * (1.0 - value * (0.5 - value * (1.0 / 3.0 - value * (0.25 - value * 0.2))))
+    return jnp.where(value < 0.01, series, jnp.log(1.0 + value))
+
+
+def softplus(value):
+    return jnp.maximum(value, 0.0) + log1p(jnp.exp(-jnp.abs(value)))
+
+
+def merge(block):
+    return block.reshape(-1, block.shape[-1])
+
+
+def head_taps(small_ref, head):
+    wide = 2 * head
+    places = [(0, head), (1, head)] + [(2 + head // 4, wide % 8 + i) for i in (0, 1)]
+    blocks = [small_ref[z, p, 0:16, SMALL : 2 * SMALL][0:4].astype(F32) for z, p in places]
+    return jnp.concatenate(blocks, axis=1)
+
+
+def row_blocks(count, body, size=128):
+    def one(i, carry):
+        body(pl.ds(pl.multiple_of(i * size, size), size))
+        return carry
+
+    lax.fori_loop(0, count // size, one, 0)
+
+
+def lane_index(shape):
+    return lax.broadcasted_iota(jnp.int32, shape, 1)
+
+
+def forward_body(
+    planes, tiles,
+    shard_small, shard_heads, shard_tiles, x_ref, cot_ref, aux_ref, seg_ref, consts_ref, gain_ref,
+    full_small, full_heads, full_tiles, small_ref, xnt_ref, cols_ref, rows_ref, logs_ref, factor_ref,
+    proj_ref, mixed_ref, inv_ref, upd_ref, core_ref, dw_ref,
+    output_ref, grad_mid_ref, branch_ref, brancht_ref, d_gain2_ref,
+    w_buf, xn, cott, middle, nm, nmt, out_sum, nm_sum, gains, scale2_ref, copy_sem, local_sem, send_sem, recv_sem,
+):
+    step = pl.program_id(0)
+    tokens = x_ref.shape[0]
+    chunks = HEADS + tiles
+    me = lax.axis_index("dp")
+    kinds = {
+        "small": (shard_small, full_small, 2 * SMALL, chunks),
+        "head": (shard_heads, full_heads, HEAD_COLS + DV, 0),
+        "tile": (shard_tiles, full_tiles, 3 * TILE, HEADS),
+    }
+    work = Gather(me, planes, kinds, local_sem, send_sem, recv_sem)
+
+    def at(chunk, act):
+        pl.when((chunk >= 0) & (chunk < HEADS))(lambda: act("head", chunk))
+        pl.when((chunk >= HEADS) & (chunk < chunks))(lambda: act("tile", chunk - HEADS))
+
+    @pl.when(step == 0)
+    def _():
+        enter(planes)
+        work.planes_step("small", 0)
+        for k in (0, 1, 2):
+            work.planes_step("head", k)
+
+        def prepare(rows):
+            middle[rows, :] = x_ref[rows, :].astype(F32)
+            cott[:, rows] = cot_ref[rows, :].astype(F32).T.astype(BF16)
+
+        row_blocks(tokens, prepare)
+        out_sum[...] = jnp.zeros_like(out_sum)
+        nm_sum[...] = jnp.zeros_like(nm_sum)
+        d_gain2_ref[...] = jnp.zeros_like(d_gain2_ref)
+        work.square_step("small", 0)
+        work.square_step("head", 0)
+        work.diagonal_step("small", 0)
+        work.square_step("head", 1)
+        work.core_step("small", 0)
+        work.diagonal_step("head", 0)
+        copy = pltpu.make_async_copy(full_small, small_ref, copy_sem)
+        copy.start()
+        copy.wait()
+        small = merge(small_ref[:, :, :, 0:SMALL])
+        turned = small.astype(F32).T
+        gains[0:1, :] = turned[16:17, :]
+        gains[1:2, :] = turned[17:18, :]
+
+        def norm(rows):
+            x = middle[rows, :]
+            scale = lax.rsqrt(jnp.mean(x * x, axis=1, keepdims=True) + epsilon)
+            normed = x * scale * gains[0:1, :]
+            xn[rows, :] = normed.astype(BF16)
+            xnt_ref[:, rows] = normed.T.astype(BF16)
+
+        row_blocks(tokens, norm)
+        logits = jnp.dot(xn[...], small, preferred_element_type=F32)
+        lanes = lane_index(logits.shape)
+        decay_scale, bias = consts_ref[0:1, :], consts_ref[1:2, :]
+        shifted = logits + bias
+        rate = sigmoid(logits)
+        log_decay = decay_scale * softplus(shifted)
+        logs_ref[...] = log_decay
+        factor_ref[...] = jnp.where(
+            lanes < 8, decay_scale * sigmoid(shifted), jnp.where(lanes < 16, rate * (1.0 - rate), 0.0)
+        )
+        for start in range(0, tokens, SEQ):
+            part = slice(start, start + SEQ)
+            cum = triangle_sum(log_decay[part], NN)
+            cols_ref[part, :] = jnp.where(
+                lanes[part] < 8, cum, jnp.where(lanes[part] < 16, rate[part], aux_ref[part, :])
+            )
+            rows_ref[0:8, part] = cum.T[0:8]
+        rows_ref[8:16, :] = seg_ref[...]
+        work.finish("small", 0)
+
+    at(step + 3, work.planes_step)
+    at(step + 2, work.square_step)
+    at(step + 1, work.diagonal_step)
+    at(step, work.core_step)
+    at(step - 1, work.finish)
+
+    @pl.when(step < HEADS)
+    def _():
+        copy = pltpu.make_async_copy(full_heads.at[:, :, :, columns(step, HEAD_COLS + DV)], w_buf, copy_sem)
+        copy.start()
+        copy.wait()
+        w = merge(w_buf[...])
+        projected = jnp.dot(xn[...], w[:, :HEAD_COLS], preferred_element_type=F32)
+        proj_ref[...] = projected
+        _, _, _, _, q, k, value, _, _, cum, rate, seg = head_inputs(
+            projected, head_taps(small_ref, step), cols_ref[...], step
+        )
+        q = q * DK**-0.5
+        cum_row = rows_ref[pl.ds(step, 1), :]
+        seg_row = rows_ref[8:9, :]
+        parts = [slice(s, s + SEQ) for s in range(0, tokens, SEQ)]
+        scores, couplings = [], []
+        for part in parts:
+            pair = decays(seg[part], seg_row[:, part], cum[part], cum_row[:, part])
+            key_dots = dot3(k[part], k[part], NT)
+            scores.append(pair * dot3(q[part], k[part], NT))
+            couplings.append(strict(pair * key_dots) * rate[part])
+        inverses = unit_inverses(couplings)
+        for i, part in enumerate(parts):
+            update = dot3(inverses[i], rate[part] * value[part], NN)
+            core = dot3(scores[i], update, NN)
+            inv_ref[0, part, :] = inverses[i].astype(BF16)
+            upd_ref[0, part, :] = update
+            core_ref[0, part, :] = core
+            scale = lax.rsqrt(jnp.mean(core * core, axis=1, keepdims=True) + head_epsilon)
+            out_gate = projected[part, CONV_COLS:]
+            mixed_ref[part, :] = (core * scale * gain_ref[...] * (out_gate * sigmoid(out_gate))).astype(BF16)
+        middle[...] += lax.dot_general(mixed_ref[...], w[:, HEAD_COLS:], (NT, ((), ())), preferred_element_type=F32)
+
+    @pl.when(step == HEADS)
+    def _():
+        def norm(rows):
+            mid = middle[rows, :]
+            scale = lax.rsqrt(jnp.mean(mid * mid, axis=1, keepdims=True) + epsilon)
+            normed = mid * scale * gains[1:2, :]
+            nm[rows, :] = normed.astype(BF16)
+            nmt[:, rows] = normed.T.astype(BF16)
+
+        row_blocks(tokens, norm)
+
+    @pl.when(step >= HEADS)
+    def _():
+        place = w_buf.at[:, :, :, pl.ds(0, 3 * TILE)]
+        copy = pltpu.make_async_copy(full_tiles.at[:, :, :, columns(step - HEADS, 3 * TILE)], place, copy_sem)
+        copy.start()
+        copy.wait()
+        w = merge(w_buf[:, :, :, 0 : 3 * TILE])
+        gate_up = jnp.dot(nm[...], w[:, : 2 * TILE], preferred_element_type=F32)
+        gate, up = gate_up[:, :TILE], gate_up[:, TILE:]
+        sig = sigmoid(gate)
+        swish = gate * sig
+        hidden = (swish * up).astype(BF16)
+        grad_hidden = jnp.dot(cot_ref[...], w[:, 2 * TILE :], preferred_element_type=F32)
+        grad_gate = grad_hidden * up * (sig + swish * (1.0 - sig))
+        grad_up = grad_hidden * swish
+        grad_low = jnp.concatenate([grad_gate, grad_up], axis=1).astype(BF16)
+        out_sum[...] += lax.dot_general(hidden, w[:, 2 * TILE :], (NT, ((), ())), preferred_element_type=F32)
+        nm_sum[...] += lax.dot_general(grad_low, w[:, : 2 * TILE], (NT, ((), ())), preferred_element_type=F32)
+        dw_ref[:, : 2 * TILE] = jnp.dot(nmt[...], grad_low, preferred_element_type=F32).astype(BF16)
+        dw_ref[:, 2 * TILE :] = jnp.dot(cott[...], hidden, preferred_element_type=F32).astype(BF16)
+
+    @pl.when(step == chunks - 1)
+    def _():
+        def back(rows):
+            mid = middle[rows, :]
+            output_ref[rows, :] = (mid + out_sum[rows, :]).astype(BF16)
+            scale = lax.rsqrt(jnp.mean(mid * mid, axis=1, keepdims=True) + epsilon)
+            normed = mid * scale
+            grad = nm_sum[rows, :]
+            d_gain2_ref[0:1, :] += jnp.sum(grad * normed, axis=0, keepdims=True)
+            d_normed = grad * gains[1:2, :]
+            d_mid = scale * (d_normed - normed * jnp.mean(d_normed * normed, axis=1, keepdims=True))
+            d_mid = d_mid + cot_ref[rows, :].astype(F32)
+            grad_mid_ref[rows, :] = d_mid
+            branch_ref[rows, :] = d_mid.astype(BF16)
+            brancht_ref[:, rows] = d_mid.T.astype(BF16)
+
+        row_blocks(tokens, back)
+        work.finish("tile", tiles - 1)
+
+
+def once(shape):
+    return pl.BlockSpec(shape, lambda i: (0,) * len(shape), pipeline_mode=pl.Buffered(1))
+
+
+def forward(planes, shards, x, cot, aux, seg_rows, consts, gain):
+    rows, tokens, width = shards[0].shape[0], *x.shape
+    tiles = shards[2].shape[1] // (3 * TILE)
+    chunks = HEADS + tiles
+    hbm = pl.BlockSpec(memory_space=pl.ANY)
+    head = lambda i: jnp.minimum(i, HEADS - 1)
+    tile = lambda i: jnp.maximum(i - HEADS, 0)
+    save = pl.BlockSpec((1, tokens, SEQ), lambda i: (head(i), 0, 0))
+    shape = jax.ShapeDtypeStruct
+    whole = [((planes, 8, rows, s.shape[1]), BF16) for s in shards]
+    outs = [
+        (hbm, *whole[0]),
+        (hbm, *whole[1]),
+        (hbm, *whole[2]),
+        (once(whole[0][0]), *whole[0]),
+        (once((width, tokens)), (width, tokens), BF16),
+        (once((tokens, 128)), (tokens, 128), F32),
+        (once((16, tokens)), (16, tokens), F32),
+        (once((tokens, 128)), (tokens, 128), F32),
+        (once((tokens, 128)), (tokens, 128), F32),
+        (pl.BlockSpec((tokens, HEAD_COLS), lambda i: (0, head(i))), (tokens, HEADS * HEAD_COLS), F32),
+        (pl.BlockSpec((tokens, DV), lambda i: (0, head(i))), (tokens, HEADS * DV), BF16),
+        (save, (HEADS, tokens, SEQ), BF16),
+        (save, (HEADS, tokens, DV), F32),
+        (save, (HEADS, tokens, DV), F32),
+        (pl.BlockSpec((width, 3 * TILE), lambda i: (0, tile(i))), (width, tiles * 3 * TILE), BF16),
+        (once((tokens, width)), (tokens, width), BF16),
+        (once((tokens, width)), (tokens, width), F32),
+        (once((tokens, width)), (tokens, width), BF16),
+        (once((width, tokens)), (width, tokens), BF16),
+        (once((8, width)), (8, width), F32),
+    ]
+    return pl.pallas_call(
+        partial(forward_body, planes, tiles),
+        grid=(chunks,),
+        in_specs=[hbm, hbm, hbm] + [once(a.shape) for a in (x, cot, aux, seg_rows, consts, gain)],
+        out_specs=[o[0] for o in outs],
+        out_shape=[shape(o[1], o[2]) for o in outs],
+        scratch_shapes=[
+            pltpu.VMEM((planes, 8, rows, HEAD_COLS + DV), BF16),
+            pltpu.VMEM((tokens, width), BF16),
+            pltpu.VMEM((width, tokens), BF16),
+            pltpu.VMEM((tokens, width), F32),
+            pltpu.VMEM((tokens, width), BF16),
+            pltpu.VMEM((width, tokens), BF16),
+            pltpu.VMEM((tokens, width), F32),
+            pltpu.VMEM((tokens, width), F32),
+            pltpu.VMEM((8, width), F32),
+            pltpu.VMEM((tokens, 128), F32),
+            pltpu.SemaphoreType.DMA,
+            pltpu.SemaphoreType.DMA((chunks + 1,)),
+            pltpu.SemaphoreType.DMA((chunks + 1, 6 + planes)),
+            pltpu.SemaphoreType.DMA((chunks + 1, 6 + planes)),
+        ],
+        compiler_params=pltpu.CompilerParams(
+            collective_id=0, has_side_effects=True, vmem_limit_bytes=60 * MIB
+        ),
+        name="forward",
+    )(*shards, x, cot, aux, seg_rows, consts, gain)
+
+
+LAG = 2
+
+
+def head_step(j):
+    return jnp.minimum(j // 2, HEADS - 1)
+
+
+def backward_body(
+    planes, tiles, total_chunks,
+    dwf_ref, gb_ref, gbt_ref, xnt_ref, w_ref, proj_ref, mixed_ref, inv_ref, upd_ref, core_ref,
+    small_ref, cols_ref, rows_ref, logs_ref, factor_ref, gain_ref, x_ref, grad_mid_ref, d_gain2_ref,
+    input_grad_ref, own_mixer, own_out, own_ffn, own_down, own_small, shared_ref,
+    dw, d_small, gxn, dcols, drows, dgain, dproj, value_ref,
+    from_core, keep, sums, from_x, from_y, from_xy, from_z, got, stage,
+    local_sem, send_sem, recv_sem, total_send, total_recv,
+):
+    step = pl.program_id(0)
+    tokens = gb_ref.shape[0]
+    rows = own_small.shape[0]
+    hidden = tiles * TILE
+    me = lax.axis_index("dp")
+
+    def tile_source(k, core):
+        return dwf_ref.at[:, :, core, :, columns(k, 3 * TILE)]
+
+    kinds = {
+        "tile": (3 * TILE, tile_source, None),
+        "head": (
+            HEAD_COLS + DV,
+            lambda k, core: dw.at[k % 2, :, :, core],
+            lambda k, plane, place, core: dw[k % 2, plane, place, core],
+        ),
+        "small": (
+            2 * SMALL,
+            lambda k, core: d_small.at[:, :, core],
+            lambda k, plane, place, core: d_small[plane, place, core],
+        ),
+    }
+
+    def store(kind, k, total):
+        def put(ref, start, source, width):
+            ref[:, pl.ds(pl.multiple_of(start, 128), width)] = total[:, source : source + width]
+
+        if kind == "small":
+            own_small[...] = total
+        elif kind == "head":
+            put(own_mixer, k * DK, 0, DK)
+            put(own_mixer, HEADS * DK + k * DK, DK, DK)
+            put(own_mixer, 2 * HEADS * DK + k * DV, 2 * DK, DV)
+            put(own_mixer, 2 * HEADS * DK + HEADS * DV + k * DV, 2 * DK + DV, DV)
+            put(own_out, k * DV, HEAD_COLS, DV)
+        else:
+            put(own_ffn, k * TILE, 0, TILE)
+            put(own_ffn, hidden + k * TILE, TILE, TILE)
+            put(own_down, k * TILE, 2 * TILE, TILE)
+
+    work = Scatter(
+        me, planes, kinds, store, from_core, keep, sums, from_x, from_y, from_xy, from_z, local_sem, send_sem, recv_sem
+    )
+    small_sum = Total(me, planes, value_ref, shared_ref, got, stage, total_send, total_recv)
+
+    last = total_chunks - 1
+
+    def at(r, act):
+        is_head = (r >= 3) & (r < last) & (r % 2 == 1)
+        is_tile = (r >= 0) & (r < last) & ((r < 3) | (r % 2 == 0))
+        pl.when(is_tile)(lambda: act("tile", r, r // 2 + (r + last - 2) // (last - 1)))
+        pl.when(is_head)(lambda: act("head", r, (r - 3) // 2))
+        pl.when(r == last)(lambda: act("small", r, 0))
+
+    @pl.when(step == 0)
+    def _():
+        enter(planes)
+        for r in (0, 1):
+            work.core_step("tile", r, r)
+        work.load_step("tile", 0, 0)
+        gxn[...] = jnp.zeros_like(gxn)
+        dcols[...] = jnp.zeros_like(dcols)
+        drows[...] = jnp.zeros_like(drows)
+        dgain[...] = jnp.zeros_like(dgain)
+        d_small[...] = jnp.zeros_like(d_small)
+
+    at(step - 3 * LAG, work.planes_step)
+    at(step - 2 * LAG, work.square_step)
+    at(step - LAG, work.diagonal_step)
+    at(step, work.chip_step)
+    at(step + 2, work.core_step)
+    at(step + 1, work.load_step)
+
+    @pl.when((step < 2 * HEADS) & (step % 2 == 0))
+    def _():
+        head = step // 2
+        w = merge(w_ref[...])
+        grad_mixed = jnp.dot(gb_ref[...], w[:, HEAD_COLS:], preferred_element_type=F32)
+        d_out = jnp.dot(gbt_ref[...], mixed_ref[...], preferred_element_type=F32).astype(BF16)
+        dw[head % 2, :, :, :, :, pl.ds(HEAD_COLS, DV)] = d_out.reshape(dw.shape[1:5] + (DV,))
+
+        projected = proj_ref[...]
+        taps = head_taps(small_ref, head)
+        keeps, conv, gate, act, qn, k, value, q_scale, k_scale, cum, rate, seg = head_inputs(
+            projected, taps, cols_ref[...], head
+        )
+        q = qn * DK**-0.5
+        cum_row = rows_ref[pl.ds(head, 1), :]
+        seg_row = rows_ref[8:9, :]
+        gain = gain_ref[...]
+        lanes = lane_index((SEQ, 128))
+        d_act, d_gain = [], jnp.zeros((1, DV), F32)
+        for start in range(0, tokens, SEQ):
+            part = slice(start, start + SEQ)
+            core, update, inverse = core_ref[0, part, :], upd_ref[0, part, :], inv_ref[0, part, :]
+            grad = grad_mixed[part]
+            scale = lax.rsqrt(jnp.mean(core * core, axis=1, keepdims=True) + head_epsilon)
+            normed = core * scale
+            out_gate = projected[part, CONV_COLS:]
+            out_sig = sigmoid(out_gate)
+            swish = out_gate * out_sig
+            dproj[part, CONV_COLS:] = (grad * normed * gain * (out_sig + swish * (1.0 - out_sig))).astype(BF16)
+            d_normed = grad * swish
+            d_gain = d_gain + jnp.sum(d_normed * normed, axis=0, keepdims=True)
+            d_scaled = d_normed * gain
+            d_core = scale * (d_scaled - normed * jnp.mean(d_scaled * normed, axis=1, keepdims=True))
+
+            qs, ks, vs, rs = q[part], k[part], value[part], rate[part]
+            pair = decays(seg[part], seg_row[:, part], cum[part], cum_row[:, part])
+            key_dots = dot3(ks, ks, NT)
+            query_dots = dot3(qs, ks, NT)
+            d_scores = dot3(d_core, update, NT)
+            d_update = dot1(pair * query_dots, d_core, TN)
+            solved = dot1(inverse, d_update, TN)
+            d_coupling = strict(-dot1(solved, update, NT)) * pair
+            d_query_dots = pair * d_scores
+            d_key_dots = d_coupling * rs
+            weighed = d_coupling * key_dots
+            d_spread = d_query_dots * query_dots + weighed * rs
+            d_q = dot1(d_query_dots, ks, NN) * DK**-0.5
+            d_k = dot1(d_query_dots, qs, TN) + dot1(d_key_dots, ks, NN) + dot1(d_key_dots, ks, TN)
+            d_rate = jnp.sum(solved * vs, axis=1, keepdims=True) + jnp.sum(weighed, axis=1, keepdims=True)
+            row_sum = jnp.sum(d_spread, axis=1, keepdims=True)
+            dcols[part, :] += jnp.where(lanes == head, row_sum, 0.0) + jnp.where(lanes == 8 + head, d_rate, 0.0)
+            drows[pl.ds(head, 1), part] = jnp.sum(d_spread, axis=0, keepdims=True)
+            d_q_act = q_scale[part] * (d_q - qn[part] * jnp.sum(d_q * qn[part], axis=1, keepdims=True))
+            d_k_act = k_scale[part] * (d_k - ks * jnp.sum(d_k * ks, axis=1, keepdims=True))
+            d_act.append(jnp.concatenate([d_q_act, d_k_act, rs * solved], axis=1))
+        dgain[0:1, :] += d_gain
+        d_conv = jnp.concatenate(d_act, axis=0) * (gate + act * (1.0 - gate))
+        source = projected[:, :CONV_COLS]
+        d_source = d_conv * taps[0:1]
+        d_taps = [jnp.sum(d_conv * source, axis=0, keepdims=True)]
+        for back in (1, 2, 3):
+            kept = d_conv * keeps[back - 1]
+            d_source = d_source + pltpu.roll(kept, tokens - back, 0) * taps[back : back + 1]
+            d_taps.append(jnp.sum(kept * pltpu.roll(source, back, 0), axis=0, keepdims=True))
+        d_taps = jnp.concatenate(d_taps + [jnp.zeros((rows - 4, CONV_COLS), F32)], axis=0).astype(BF16)
+        wide = 2 * head
+        places = [(0, head), (1, head)] + [(2 + head // 4, wide % 8 + i) for i in (0, 1)]
+        for i, (z, p) in enumerate(places):
+            d_small[z, p // 2, p % 2, :, SMALL:] = d_taps[:, i * SMALL : (i + 1) * SMALL]
+        dproj[:, :CONV_COLS] = d_source.astype(BF16)
+        d_proj = dproj[...]
+        d_in = jnp.dot(xnt_ref[...], d_proj, preferred_element_type=F32).astype(BF16)
+        dw[head % 2, :, :, :, :, pl.ds(0, HEAD_COLS)] = d_in.reshape(dw.shape[1:5] + (HEAD_COLS,))
+        gxn[...] += lax.dot_general(d_proj, w[:, :HEAD_COLS], (NT, ((), ())), preferred_element_type=F32)
+
+    @pl.when(step == 2 * HEADS - 1)
+    def _():
+        small = merge(small_ref[:, :, :, 0:SMALL])
+        turned = small.astype(F32).T
+        gain1 = turned[16:17, :]
+        lanes = lane_index((SEQ, 128))
+        padded = jnp.concatenate([drows[...], jnp.zeros((120, tokens), F32)], axis=0).T
+        d_logs = jnp.zeros((1, 128), F32)
+        d_bias = jnp.zeros((1, 128), F32)
+        d_logits = []
+        for start in range(0, tokens, SEQ):
+            part = slice(start, start + SEQ)
+            d_cum = jnp.where(lanes < 8, dcols[part, :], 0.0) - padded[part]
+            d_decay = triangle_sum(d_cum, TN)
+            d_logit = jnp.where(lanes < 8, d_decay, dcols[part, :]) * factor_ref[part, :]
+            d_logs = d_logs + jnp.sum(jnp.where(lanes < 8, d_decay * logs_ref[part, :], 0.0), axis=0, keepdims=True)
+            d_bias = d_bias + jnp.sum(jnp.where(lanes < 8, d_logit, 0.0), axis=0, keepdims=True)
+            d_logits.append(d_logit.astype(BF16))
+        d_logits = jnp.concatenate(d_logits, axis=0)
+        value_ref[...] = jnp.concatenate(
+            [d_logs, d_bias, dgain[0:1, :128], dgain[0:1, 128:], jnp.zeros((4, 128), F32)], axis=0
+        )
+        gxn[...] += lax.dot_general(d_logits, small, (NT, ((), ())), preferred_element_type=F32)
+        drows[...] = jnp.zeros_like(drows)
+        d_gain1 = [jnp.zeros((1, gxn.shape[1]), F32)]
+
+        def back(at_rows, total):
+            x = x_ref[at_rows, :].astype(F32)
+            scale = lax.rsqrt(jnp.mean(x * x, axis=1, keepdims=True) + epsilon)
+            normed = x * scale
+            grad = gxn[at_rows, :]
+            d_normed = grad * gain1
+            d_x = scale * (d_normed - normed * jnp.mean(d_normed * normed, axis=1, keepdims=True))
+            input_grad_ref[at_rows, :] = d_x + grad_mid_ref[at_rows, :]
+            return total + jnp.sum(grad * normed, axis=0, keepdims=True)
+
+        total = lax.fori_loop(
+            0, tokens // 128, lambda i, t: back(pl.ds(pl.multiple_of(i * 128, 128), 128), t), d_gain1[0]
+        )
+        line = lax.broadcasted_iota(jnp.int32, (128, total.shape[1]), 0)
+        gains = jnp.where(line == 16, total, jnp.where(line == 17, d_gain2_ref[0:1, :], 0.0))
+        own = jnp.dot(xnt_ref[...], d_logits, preferred_element_type=F32) + gains.T
+        d_small[:, :, :, :, 0:SMALL] = own.astype(BF16).reshape(d_small.shape[:4] + (SMALL,))
+
+    for number in range(5):
+        pl.when(step == 2 * HEADS + number)(lambda number=number: small_sum.step(number))
+
+
+def backward(planes, dwf, gb, gbt, xnt, w, proj, mixed, inv, upd, core, small, cols, seq_rows, logs, factor, gain, x,
+             grad_mid, d_gain2):
+    tokens, width = gb.shape
+    rows = small.shape[2]
+    tiles = dwf.shape[1] // (3 * TILE)
+    chunks = tiles + HEADS + 1
+    hbm = pl.BlockSpec(memory_space=pl.ANY)
+    head = head_step
+    save = pl.BlockSpec((1, tokens, SEQ), lambda i: (head(i), 0, 0))
+    shape = jax.ShapeDtypeStruct
+    widest = HEAD_COLS + DV
+    depth = Scatter.depths
+    kinds = 3 + planes
+    outs = [
+        ((tokens, width), F32),
+        ((rows, HEADS * HEAD_COLS), F32),
+        ((rows, HEADS * DV), F32),
+        ((rows, 2 * tiles * TILE), F32),
+        ((rows, tiles * TILE), F32),
+        ((rows, 2 * SMALL), F32),
+        ((8, 128), F32),
+    ]
+    return pl.pallas_call(
+        partial(backward_body, planes, tiles, chunks),
+        grid=(chunks + 3 * LAG,),
+        in_specs=[
+            hbm,
+            once((tokens, width)),
+            once((width, tokens)),
+            once((width, tokens)),
+            pl.BlockSpec((planes, 8, rows, widest), lambda i: (0, 0, 0, head(i))),
+            pl.BlockSpec((tokens, HEAD_COLS), lambda i: (0, head(i))),
+            pl.BlockSpec((tokens, DV), lambda i: (0, head(i))),
+            save,
+            save,
+            save,
+        ]
+        + [once(a.shape) for a in (small, cols, seq_rows, logs, factor, gain, x, grad_mid, d_gain2)],
+        out_specs=[once(o[0]) for o in outs],
+        out_shape=[shape(*o) for o in outs],
+        scratch_shapes=[
+            pltpu.VMEM((2, planes, 4, 2, rows, widest), BF16),
+            pltpu.VMEM((planes, 4, 2, rows, 2 * SMALL), BF16),
+            pltpu.VMEM((tokens, width), F32),
+            pltpu.VMEM((tokens, 128), F32),
+            pltpu.VMEM((HEADS, tokens), F32),
+            pltpu.VMEM((8, DV), F32),
+            pltpu.VMEM((tokens, HEAD_COLS), BF16),
+            pltpu.VMEM((8, 128), F32),
+            pltpu.VMEM((depth["core"], planes, 4, rows, widest), BF16),
+            pltpu.VMEM((depth["keep"], planes, 4, rows, 3 * TILE), BF16),
+            pltpu.VMEM((depth["sums"], planes, 4, rows, widest), BF16),
+            pltpu.VMEM((depth["x"], planes, rows, widest), BF16),
+            pltpu.VMEM((depth["y"], planes, rows, widest), BF16),
+            pltpu.VMEM((depth["xy"], planes, rows, widest), BF16),
+            pltpu.VMEM((depth["z"], planes - 1, rows, widest), BF16),
+            pltpu.VMEM((3 + planes, 8, 128), F32),
+            pltpu.VMEM((4, 8, 128), F32),
+            pltpu.SemaphoreType.DMA((chunks,)),
+            pltpu.SemaphoreType.DMA((chunks, kinds)),
+            pltpu.SemaphoreType.DMA((chunks, kinds)),
+            pltpu.SemaphoreType.DMA((2 + planes,)),
+            pltpu.SemaphoreType.DMA((2 + planes,)),
+        ],
+        compiler_params=pltpu.CompilerParams(
+            collective_id=1, has_side_effects=True, vmem_limit_bytes=63 * MIB
+        ),
+        name="backward",
+    )(
+        dwf.reshape(planes, 4, 2, rows, dwf.shape[1]), gb, gbt, xnt, w, proj, mixed, inv, upd, core, small, cols,
+        seq_rows, logs, factor, gain, x, grad_mid, d_gain2,
+    )
 
 
 def mixer_fwd_body(xn_ref, w_ref, taps_ref, cols_ref, rows_ref, gain_ref, proj_ref, mixed_ref, inv_ref, upd_ref, core_ref):
@@ -353,351 +1182,6 @@
     )(nm, nmt, cot, cott, w)
 
 
-def flip(number, bit):
-    return number + bit - 2 * bit * ((number // bit) % 2)
-
-
-def z_partner(me, planes, k):
-    other = me
-    bit = 1
-    while bit < planes:
-        if k & bit:
-            other = flip(other, 8 * bit)
-        bit *= 2
-    return other
-
-
-def z_of(plane, planes, k):
-    bit = 1
-    while bit < planes:
-        if k & bit:
-            plane = flip(plane, bit)
-        bit *= 2
-    return plane
-
-
-def enter(planes):
-    me = lax.axis_index("dp")
-    barrier = pltpu.get_barrier_semaphore()
-    partners = [flip(me, 1), flip(me, 2), flip(me, 4)]
-    partners += [z_partner(me, planes, k) for k in range(1, planes)]
-    for other in partners:
-        pl.semaphore_signal(barrier, inc=1, device_id=(other,), device_id_type=MESH)
-    pl.semaphore_wait(barrier, len(partners))
-    return me
-
-
-class Gather:
-    def __init__(self, me, planes, shards, fulls, chunks, local_sem, send_sem, recv_sem):
-        self.me, self.planes, self.shards, self.fulls, self.chunks = me, planes, shards, fulls, chunks
-        self.local_sem, self.send_sem, self.recv_sem = local_sem, send_sem, recv_sem
-        self.plane, self.place = me // 8, me % 8
-        self.copies = {}
-
-    def slot(self, k, place):
-        array, start, size, _ = self.chunks[k]
-        return self.fulls[array].at[:, place, :, pl.ds(start, size)]
-
-    def send(self, k, number, source, target, other):
-        copy = pltpu.make_async_remote_copy(
-            src_ref=source,
-            dst_ref=target,
-            send_sem=self.send_sem.at[k, number],
-            recv_sem=self.recv_sem.at[k, number],
-            device_id=(other,),
-            device_id_type=MESH,
-        )
-        copy.start()
-        self.copies[k, number] = copy
-
-    def forward(self, k, number, place, other):
-        self.send(k, number, self.slot(k, place), self.slot(k, place), other)
-
-    def planes_step(self, k):
-        array, start, size, _ = self.chunks[k]
-        own = self.shards[array].at[:, pl.ds(start, size)]
-        home = self.fulls[array].at[self.plane, self.place, :, pl.ds(start, size)]
-        local = pltpu.make_async_copy(own, home, self.local_sem.at[k])
-        local.start()
-        self.copies[k, "local"] = local
-        for d in range(1, self.planes):
-            self.send(k, 6 + d, own, home, z_partner(self.me, self.planes, d))
-
-    def square_step(self, k):
-        self.copies[k, "local"].wait()
-        for d in range(1, self.planes):
-            self.copies[k, 6 + d].wait_recv()
-        self.forward(k, 0, self.place, flip(self.me, 2))
-        self.forward(k, 1, self.place, flip(self.me, 4))
-        self.forward(k, 3, self.place, flip(self.me, 1))
-
-    def diagonal_step(self, k):
-        by_y = self.chunks[k][3]
-        for number, bit in ((1, 4), (0, 2)) if by_y else ((0, 2), (1, 4)):
-            self.copies[k, number].wait_recv()
-            place = flip(self.place, bit)
-            if number == int(by_y):
-                self.forward(k, 2, place, flip(self.me, 6 - bit))
-            self.forward(k, 4 + number, place, flip(self.me, 1))
-
-    def core_step(self, k):
-        self.copies[k, 2].wait_recv()
-        self.forward(k, 6, flip(flip(self.place, 2), 4), flip(self.me, 1))
-
-    def finish(self, k):
-        for number in (3, 4, 5, 6):
-            self.copies[k, number].wait_recv()
-        for number in range(6 + self.planes):
-            self.copies[k, number].wait_send()
-
-
-def gather_body(planes, chunks, count, *refs):
-    shards, fulls = refs[:count], refs[count : 2 * count]
-    me = enter(planes)
-    work = Gather(me, planes, shards, fulls, chunks, *refs[2 * count :])
-    total = len(chunks)
-    for k in range(-2, total + 2):
-        for ahead, step in ((2, work.planes_step), (0, work.square_step), (-1, work.diagonal_step), (-2, work.core_step)):
-            if 0 <= k + ahead < total:
-                step(k + ahead)
-    for k in range(total):
-        work.finish(k)
-
-
-def gather_all(devices, shards, chunks):
-    rows = shards[0].shape[0]
-    planes = devices // 8
-    hbm = pl.BlockSpec(memory_space=pl.ANY)
-    fulls = pl.pallas_call(
-        partial(gather_body, planes, chunks, len(shards)),
-        in_specs=[hbm] * len(shards),
-        out_specs=[hbm] * len(shards),
-        out_shape=[jax.ShapeDtypeStruct((planes, 8, rows, s.shape[1]), s.dtype) for s in shards],
-        scratch_shapes=[
-            pltpu.SemaphoreType.DMA((len(chunks),)),
-            pltpu.SemaphoreType.DMA((len(chunks), 6 + planes)),
-            pltpu.SemaphoreType.DMA((len(chunks), 6 + planes)),
-        ],
-        compiler_params=pltpu.CompilerParams(collective_id=0, has_side_effects=True),
-        name="gather_weights",
-    )(*shards)
-    return [f.reshape(devices * rows, f.shape[-1]) for f in fulls]
-
-
-class Scatter:
-    def __init__(self, me, planes, grads, out_ref, chunks, from_core, keep, from_x, from_y, from_xy, from_z,
-                 local_sem, send_sem, recv_sem):
-        self.me, self.planes, self.grads, self.out_ref, self.chunks = me, planes, grads, out_ref, chunks
-        self.from_core, self.keep = from_core, keep
-        self.from_x, self.from_y, self.from_xy, self.from_z = from_x, from_y, from_xy, from_z
-        self.local_sem, self.send_sem, self.recv_sem = local_sem, send_sem, recv_sem
-        self.plane, self.core = me // 8, me % 2
-        self.here = (me // 2) % 4
-        self.copies = {}
-
-    def send(self, k, number, source, target, other):
-        copy = pltpu.make_async_remote_copy(
-            src_ref=source,
-            dst_ref=target,
-            send_sem=self.send_sem.at[k, number],
-            recv_sem=self.recv_sem.at[k, number],
-            device_id=(other,),
-            device_id_type=MESH,
-        )
-        copy.start()
-        self.copies[k, number] = copy
-
-    def span(self, k):
-        return pl.ds(self.chunks[k][4], self.chunks[k][2])
-
-    def core_step(self, k):
-        array, start, size, _, _ = self.chunks[k]
-        source = self.grads[array].at[:, :, 1 - self.core, :, pl.ds(start, size)]
-        self.send(k, 0, source, self.from_core.at[:, :, :, self.span(k)], flip(self.me, 1))
-        mine = self.grads[array].at[:, :, self.core, :, pl.ds(start, size)]
-        local = pltpu.make_async_copy(mine, self.keep.at[k % 2, :, :, :, pl.ds(0, size)], self.local_sem.at[k])
-        local.start()
-        self.copies[k, "local"] = local
-
-    def add(self, k, place, others):
-        span = self.span(k)
-
-        def one(plane, carry):
-            total = self.from_core[plane, place, :, span].astype(F32)
-            for read in others:
-                total = total + read(plane).astype(F32)
-            self.from_core[plane, place, :, span] = total.astype(BF16)
-            return carry
-
-        lax.fori_loop(0, self.planes, one, 0)
-
-    def chip_step(self, k):
-        size, by_y = self.chunks[k][2], self.chunks[k][3]
-        span = self.span(k)
-        self.copies[k, 0].wait_recv()
-        self.copies[k, "local"].wait()
-        across_x, across_y = flip(self.here, 1), flip(self.here, 2)
-        both = flip(across_x, 2)
-        order = (both, across_y, across_x) if by_y else (both, across_x, across_y)
-        for place in order + (self.here,):
-            self.add(k, place, [lambda plane, place=place: self.keep[k % 2, plane, place, :, pl.ds(0, size)]])
-            if place is both:
-                source = self.from_core.at[:, both, :, span]
-                self.send(k, 1, source, self.from_xy.at[:, :, span], flip(self.me, 4 if by_y else 2))
-            elif place is order[1]:
-                if by_y:
-                    self.send_y(k)
-                else:
-                    self.send_x(k)
-
-    def send_x(self, k):
-        span = self.span(k)
-        self.send(k, 2, self.from_core.at[:, flip(self.here, 1), :, span], self.from_x.at[:, :, span], flip(self.me, 2))
-
-    def send_y(self, k):
-        span = self.span(k)
-        self.send(k, 3, self.from_core.at[:, flip(self.here, 2), :, span], self.from_y.at[:, :, span], flip(self.me, 4))
-
-    def diagonal_step(self, k):
-        by_y = self.chunks[k][3]
-        span = self.span(k)
-        self.copies[k, 1].wait_recv()
-        place = flip(self.here, 1 if by_y else 2)
-        self.add(k, place, [lambda plane: self.from_xy[plane, :, span]])
-        if by_y:
-            self.send_x(k)
-        else:
-            self.send_y(k)
-
-    def square_step(self, k):
-        span = self.span(k)
-        self.copies[k, 2].wait_recv()
-        self.copies[k, 3].wait_recv()
-        self.add(k, self.here, [lambda plane: self.from_x[plane, :, span], lambda plane: self.from_y[plane, :, span]])
-        for d in range(1, self.planes):
-            source = self.from_core.at[z_of(self.plane, self.planes, d), self.here, :, span]
-            self.send(k, 3 + d, source, self.from_z.at[d - 1, :, span], z_partner(self.me, self.planes, d))
-
-    def planes_step(self, k):
-        span = self.span(k)
-        total = self.from_core[self.plane, self.here, :, span].astype(F32)
-        for d in range(1, self.planes):
-            self.copies[k, 3 + d].wait_recv()
-            total = total + self.from_z[d - 1, :, span].astype(F32)
-        self.out_ref[:, span] = total
-
-    def finish(self, k):
-        for number in range(3 + self.planes):
-            self.copies[k, number].wait_send()
-
-
-class Total:
-    def __init__(self, me, planes, value_ref, out_ref, got, stage, send_sem, recv_sem):
-        self.me, self.planes, self.value_ref, self.out_ref = me, planes, value_ref, out_ref
-        self.got, self.stage, self.send_sem, self.recv_sem = got, stage, send_sem, recv_sem
-        self.copies = {}
-
-    def send(self, number, source, target, other):
-        copy = pltpu.make_async_remote_copy(
-            src_ref=source, dst_ref=target, send_sem=self.send_sem.at[number], recv_sem=self.recv_sem.at[number],
-            device_id=(other,), device_id_type=MESH,
-        )
-        copy.start()
-        self.copies[number] = copy
-
-    def step(self, number):
-        planes, plane = self.planes, self.me // 8
-        if number == 0:
-            self.stage[0] = self.value_ref[...]
-        elif number <= 3:
-            self.copies[number - 1].wait_recv()
-            self.stage[number] = self.stage[number - 1] + self.got[number - 1]
-        if number < 3:
-            self.send(number, self.stage.at[number], self.got.at[number], flip(self.me, 1 << number))
-        elif number == 3:
-            for d in range(1, planes):
-                self.send(2 + d, self.stage.at[3], self.got.at[3 + plane], z_partner(self.me, planes, d))
-            self.got[3 + plane] = self.stage[3]
-        else:
-            for d in range(1, planes):
-                self.copies[2 + d].wait_recv()
-            total = self.got[3]
-            for other in range(1, planes):
-                total = total + self.got[3 + other]
-            self.out_ref[...] = total
-            for number in range(2 + planes):
-                self.copies[number].wait_send()
-
-
-def scatter_body(planes, chunks, count, *refs):
-    grads, value_ref, out_ref, total_ref = refs[:count], refs[count], refs[count + 1], refs[count + 2]
-    me = enter(planes)
-    work = Scatter(me, planes, grads, out_ref, chunks, *refs[count + 3 : count + 12])
-    small = Total(me, planes, value_ref, total_ref, *refs[count + 12 :])
-    total = len(chunks)
-    for k in range(-1, total + 3):
-        stages = (
-            (-3, work.planes_step),
-            (-2, work.square_step),
-            (-1, work.diagonal_step),
-            (0, work.chip_step),
-            (1, work.core_step),
-        )
-        for ahead, step in stages:
-            if 0 <= k + ahead < total:
-                step(k + ahead)
-        if 0 <= k < 5:
-            small.step(k)
-    for k in range(total):
-        work.finish(k)
-
-
-def scatter_all(devices, grads, value, chunks):
-    rows = grads[0].shape[0] // devices
-    planes = devices // 8
-    width = sum(c[2] for c in chunks)
-    widest = max(c[2] for c in chunks)
-    hbm = pl.BlockSpec(memory_space=pl.ANY)
-    whole = pl.BlockSpec(memory_space=pltpu.VMEM)
-    kinds = 3 + planes
-    return pl.pallas_call(
-        partial(scatter_body, planes, chunks, len(grads)),
-        in_specs=[hbm] * len(grads) + [whole],
-        out_specs=[whole, whole],
-        out_shape=[jax.ShapeDtypeStruct((rows, width), F32), jax.ShapeDtypeStruct(value.shape, F32)],
-        scratch_shapes=[
-            pltpu.VMEM((planes, 4, rows, width), BF16),
-            pltpu.VMEM((2, planes, 4, rows, widest), BF16),
-            pltpu.VMEM((planes, rows, width), BF16),
-            pltpu.VMEM((planes, rows, width), BF16),
-            pltpu.VMEM((planes, rows, width), BF16),
-            pltpu.VMEM((planes - 1, rows, width), BF16),
-            pltpu.SemaphoreType.DMA((len(chunks),)),
-            pltpu.SemaphoreType.DMA((len(chunks), kinds)),
-            pltpu.SemaphoreType.DMA((len(chunks), kinds)),
-            pltpu.VMEM((3 + planes,) + value.shape, F32),
-            pltpu.VMEM((4,) + value.shape, F32),
-            pltpu.SemaphoreType.DMA((2 + planes,)),
-            pltpu.SemaphoreType.DMA((2 + planes,)),
-        ],
-        compiler_params=pltpu.CompilerParams(
-            collective_id=1, has_side_effects=True, vmem_limit_bytes=60 * MIB
-        ),
-        name="scatter_grads",
-    )(*[g.reshape(planes, 4, 2, rows, g.shape[1]) for g in grads], value)
-
-
-def cut(chunk_sizes, widths):
-    chunks, at = [], 0
-    for array, sizes in enumerate(chunk_sizes):
-        start = 0
-        for size in sizes:
-            chunks.append((array, start, size, len(chunks) % 2 == 1, at))
-            start, at = start + size, at + size
-        assert start == widths[array]
-    return chunks
-
-
 def rms_scale(values):
     return lax.rsqrt(jnp.mean(values * values, axis=-1, keepdims=True) + epsilon)
 
@@ -728,7 +1212,7 @@
     return [values[:, a:b] for a, b in zip(edges[:-1], edges[1:]) if b <= values.shape[1]]
 
 
-def on_device(
+def plain_block(
     devices, tokens, segment_ids, cotangent, norm1_gain, mixer_in, decay_in, conv_weight, decay_log, decay_bias,
     head_gain, mixer_out, norm2_gain, ffn_in, ffn_out,
 ):
@@ -736,7 +1220,6 @@
     count = tokens.shape[0]
     hidden = ffn_out.shape[0]
     tiles = hidden // TILE
-    direct = rows % 16 == 0 and devices % 8 == 0
 
     low = lambda v: v.astype(BF16)
     shard_mixer = by_head(split_heads(low(mixer_in)))
@@ -753,15 +1236,7 @@
 
     x = tokens.astype(F32)
     scale1 = rms_scale(x)
-    if direct:
-        sizes = [[SMALL], [768, 1536, 1536, 2304], [2048], [1536] * 5 + [768]]
-        full_small, full_mixer, full_out, full_ffn = gather_all(
-            devices, shards, [c[:4] for c in cut(sizes, [s.shape[1] for s in shards])]
-        )
-    else:
-        full_small, full_mixer, full_out, full_ffn = [
-            lax.all_gather(s, "dp", axis=0, tiled=True) for s in shards
-        ]
+    full_small, full_mixer, full_out, full_ffn = [lax.all_gather(s, "dp", axis=0, tiled=True) for s in shards]
 
     decay_full = full_small[:, :16]
     gain1 = full_small[:, 16].astype(F32)
@@ -825,22 +1300,11 @@
     dw_small = low(jnp.pad(dw_small, ((0, 0), (0, SMALL - dw_small.shape[1]))))
     shared = jnp.concatenate([jnp.sum(d_decay * log_decay, axis=0), jnp.sum(d_shifted, axis=0), d_gain[0]])
 
-    if direct:
-        grads = [dw_ffn, dw_out, dw_mixer, dw_small]
-        sizes = [[1536] * 5 + [768], [2048], [1536] * 4, [SMALL]]
-        block = jnp.pad(shared, (0, 1024 - shared.shape[0])).reshape(8, 128)
-        own, total = scatter_all(devices, grads, block, cut(sizes, [g.shape[1] for g in grads]))
-        shared = total.reshape(-1)
-        edges = [0]
-        for g in grads:
-            edges.append(edges[-1] + g.shape[1])
-        own_ffn, own_out, own_mixer, own_small = [own[:, a:b] for a, b in zip(edges[:-1], edges[1:])]
-    else:
-        own_ffn, own_out, own_mixer, own_small = [
-            lax.psum_scatter(g.astype(F32), "dp", scatter_dimension=0, tiled=True)
-            for g in (dw_ffn, dw_out, dw_mixer, dw_small)
-        ]
-        shared = lax.psum(shared, "dp")
+    own_ffn, own_out, own_mixer, own_small = [
+        lax.psum_scatter(g.astype(F32), "dp", scatter_dimension=0, tiled=True)
+        for g in (dw_ffn, dw_out, dw_mixer, dw_small)
+    ]
+    shared = lax.psum(shared, "dp")
 
     own_tiles = own_ffn.reshape(rows, tiles, 3, TILE)
     ffn_in_grad = jnp.concatenate([own_tiles[:, :, i].reshape(rows, hidden) for i in (0, 1)], axis=1)
@@ -862,6 +1326,69 @@
     )
 
 
+def direct_block(
+    devices, tokens, segment_ids, cotangent, norm1_gain, mixer_in, decay_in, conv_weight, decay_log, decay_bias,
+    head_gain, mixer_out, norm2_gain, ffn_in, ffn_out,
+):
+    rows = decay_in.shape[0]
+    count = tokens.shape[0]
+    hidden = ffn_out.shape[0]
+    tiles = hidden // TILE
+    planes = devices // 8
+    low = lambda v: v.astype(BF16)
+    pad = lambda v, lanes: jnp.pad(v, ((0, 0), (0, lanes - v.shape[1])))
+
+    first = pad(jnp.concatenate([low(decay_in), low(norm1_gain)[:, None], low(norm2_gain)[:, None]], axis=1), SMALL)
+    second = jnp.pad(low(conv_weight), ((0, rows - 4), (0, 0)))
+    shard_small = jnp.concatenate([first, second], axis=1)
+    shard_heads = by_head(split_heads(low(mixer_in)) + [low(mixer_out).T])
+    ffn_low = low(ffn_in)
+    pieces = [ffn_low[:, :hidden], ffn_low[:, hidden:], low(ffn_out).T]
+    shard_tiles = jnp.concatenate([p.reshape(rows, tiles, TILE) for p in pieces], axis=2).reshape(rows, -1)
+
+    position = jnp.arange(count) % SEQ
+    keeps = [jnp.zeros((count, 16), F32)]
+    for back in (1, 2, 3):
+        earlier = jnp.pad(segment_ids[:-back], (back, 0), constant_values=-1)
+        keeps.append(((earlier == segment_ids) & (position >= back)).astype(F32)[:, None])
+    segment = segment_ids.astype(F32)
+    aux = pad(jnp.concatenate(keeps + [segment[:, None]], axis=1), 128)
+    seg_rows = jnp.broadcast_to(segment[None], (8, count))
+    lines = jnp.stack([-jnp.exp(decay_log), decay_bias])
+    consts = jnp.pad(lines, ((0, 6), (0, 128 - HEADS)))
+    gain = head_gain[None]
+
+    (
+        _, full_heads, _, small, xnt, cols, seq_rows, logs, factor, proj, mixed, inverse, update, core, dwf,
+        output, grad_mid, branch, brancht, d_gain2,
+    ) = forward(planes, [shard_small, shard_heads, shard_tiles], tokens, cotangent, aux, seg_rows, consts, gain)
+    input_grad, own_mixer, own_out, own_ffn, own_down, own_small, shared = backward(
+        planes, dwf, branch, brancht, xnt, full_heads, proj, mixed, inverse, update, core, small, cols, seq_rows, logs,
+        factor, gain, tokens, grad_mid, d_gain2,
+    )
+    return (
+        output,
+        input_grad,
+        own_small[:, 16],
+        own_mixer,
+        own_small[:, :16],
+        own_small[:4, SMALL:],
+        shared[0, :HEADS],
+        shared[1, :HEADS],
+        shared[2:4].reshape(-1),
+        own_out.T,
+        own_small[:, 17],
+        own_ffn,
+        own_down.T,
+    )
+
+
+def on_device(devices, *arguments):
+    rows, conv_cols = arguments[4].shape[0], arguments[6].shape[1]
+    direct = rows % 16 == 0 and devices == 32 and conv_cols == 128
+    return (direct_block if direct else plain_block)(devices, *arguments)
+
+
 def solution(mesh):
     in_specs = (
         P("dp", None), P("dp"), P("dp", None), P("dp"), P("dp", None), P("dp", None), P(None, "dp"), P(), P(), P(),

time: 576 us -> 428 us (0.74)
  Pallas kernels: 483 us -> 398 us
  local copies, waits for them, and re-layouts: 49.1 us -> 18.4 us
  other arithmetic: 26.5 us -> 9.09 us
  matrix products: 11.6 us -> 0 us
    pallas_call x5 -> x2, Pallas kernels: 483 us -> 398 us  [the longest x1 220 us: forward(): pl.pallas_call(partial(forward_body, planes, tiles), grid=(chunks,), in_s...]
    dot_general x6 -> x0, matrix products: 11.6 us -> none  [the longest x1 5.33 us: on_device(): lax.dot_general(mixed, full_out, (NT, ((), ())), preferred_element_type=F32)]
    pallas_call x4 -> x0, local copies, waits for them, and re-layouts: 10.9 us -> none  [the longest x2 6.01 us: ffn(): pl.pallas_call(ffn_body, grid=(tiles,), in_specs=[pl.BlockSpec((tokens, w...]
    slice x10 -> x4, local copies, waits for them, and re-layouts: 11 us -> 3.5 us  [the longest x1 1.5 us: direct_block(): own_small[:, 17]]
    unnamed x80 -> x33, local copies, waits for them, and re-layouts: 13.1 us -> 10 us
where the time goes in v2:
time: 428 us; the launch traced here: 426 us
  Pallas kernels  398 us (93%)
  local copies, waits for them, and re-layouts  18.4 us (4%)
  other arithmetic  9.09 us (2%)
    pallas_call x1, Pallas kernels, forward(): pl.pallas_call(partial(forward_body, planes, tiles), grid=(chunks,), in_s...  220 us
    pallas_call x1, Pallas kernels, backward(): pl.pallas_call(partial(backward_body, planes, tiles, chunks), grid=(chunk...  178 us
    unnamed x33, local copies, waits for them, and re-layouts  10 us

profile of v2, /device:TPU:0, one launch (start us, length us, event | category | flops | bytes accessed | tf_op | source)
XLA Modules:
  0.0 426.2 jit_solution(131772495332005386)
XLA Ops:
  0.7 0.7 convert_bitcast_fusion.2
  2.7 0.7 convert_element_type.41
  3.4 0.7 convert_element_type.46
  4.1 1.3 select_maximum_fusion.consts_ref
  5.3 0.7 convert_element_type.38
  6.1 0.9 fusion.17
  8.6 1.0 convert_element_type.43
  9.6 1.0 convert_bitcast_fusion
  10.9 0.7 pad.33.aux_ref
  12.0 1.0 copy.55
  13.3 1.1 copy.54
  14.4 219.6 %forward.1 = (bf16[4,8,32,256]{3,2,1,0:T(8,128)(2,1)}, bf16[4,8,32,8192]{3,2,1,0:T(8,128)(2,1)}, bf16[4,8,32,8448]{3,2,1,0:T(8,128)(2,1)}, bf16[4,8,32,256]{3,2,...) custom-call(bf16[32,256]{1,0:T(8,128)(2,1)} %fusion.1.shard_small, ...), custom_call_target="tpu_custom_call" | custom-call | tf_op jit(solution)/shard_map/forward/pallas_call | solution.py:624
  234.0 178.3 %backward.1 = (f32[512,1024]{1,0:T(8,128)}, f32[32,6144]{1,0:T(8,128)}, f32[32,2048]{1,0:T(8,128)}, f32[32,5632]{1,0:T(8,128)}, f32[32,2816]{1,0:T(8,128)}, /*index=5*/f32[32,256]{1,0:T(8,128)}, f32[8,128]{1,0:T(8,128)}) custom-call(bf16[4,4,2,32,8448]{4,3,2,1,0:T(8,128)(2,1)} %bitcast.43, bf16[512,1024]{1,0:T(8,128)(2,1)} %get-tuple-element.40.gb_ref, ...), custom_call_target="tpu_custom_call" | custom-call | tf_op jit(solution)/shard_map/backward/pallas_call | solution.py:887
  412.3 1.4 slice_bitcast_fusion.2
  413.7 1.3 slice_bitcast_fusion.3
  415.0 1.5 slice_reduce_fusion
  416.5 1.3 slice.59
  417.7 0.7 slice.58
  419.1 2.3 copy.66
  421.4 1.3 copy.67
  423.1 0.9 copy.68
  423.9 0.7 copy.69
  424.6 0.9 copy.70
  425.5 0.7 copy.71
  (45 shorter events, 4.9 us)
Async XLA Ops:
  0.6 10.9 %copy-start.3 = (f32[32,5632]{1,0:T(8,128)S(1)}, f32[32,5632]{1,0:T(8,128)}, u32[]{:S(2)}) copy-start(f32[32,5632]{1,0:T(8,128)} %param.26) | copy-start | bytes 2162692
  11.6 1.4 copy-start.1
  412.3 9.1 %copy-start = (f32[512,1024]{1,0:T(8,128)S(1)}, f32[512,1024]{1,0:T(8,128)}, u32[]{:S(2)}) copy-start(f32[512,1024]{1,0:T(8,128)} %get-tuple-element.142) | copy-start | bytes 6291460
  421.4 1.7 copy-start.2
  421.4 2.6 copy-start.6
  423.1 1.6 copy-start.4
  423.1 2.5 copy-start.5

commit v3 on v2

--- a/solution.py
+++ b/solution.py
@@ -111,29 +111,19 @@
     return number + bit - 2 * bit * ((number // bit) % 2)
 
 
-def flips(number, planes, k, unit):
-    bit = 1
-    while bit < planes:
-        if k & bit:
-            number = flip(number, unit * bit)
-        bit *= 2
-    return number
-
-
-def enter(planes):
+def enter():
     me = lax.axis_index("dp")
     barrier = pltpu.get_barrier_semaphore()
-    partners = [flip(me, 1), flip(me, 2), flip(me, 4)]
-    partners += [flips(me, planes, k, 8) for k in range(1, planes)]
+    partners = [flip(me, bit) for bit in (1, 2, 4, 8, 16)]
     for other in partners:
         pl.semaphore_signal(barrier, inc=1, device_id=(other,), device_id_type=MESH)
     pl.semaphore_wait(barrier, len(partners))
     return me
 
 
-def columns(k, width):
-    start = k * width
-    return pl.ds(start if isinstance(start, int) else pl.multiple_of(start, 128), width)
+def span(k, width, start, size):
+    first = k * width + start
+    return pl.ds(first if isinstance(first, int) else pl.multiple_of(first, 128), size)
 
 
 def remote(source, target, send_sem, recv_sem, other):
@@ -143,234 +133,358 @@
     )
 
 
+(
+    G_NEAR, G_FAR, G_RELAY, G_X, G_Y, G_CORNER_Y, G_CORNER_X, G_CORE_OWN,
+    G_CORE_OTHER, G_TWO_X, G_TWO_Y, G_TWO_CORNER, G_TWO_NEAR, G_TWO_FAR, G_TWO_RELAY, G_TWO_CORE,
+) = range(16)
+(
+    S_CORE, S_XY_X, S_XY_Y, S_X_EARLY, S_X_LATE, S_Y_EARLY, S_Y_LATE, S_RELAY,
+    S_NEAR, S_FAR, S_TWO_RELAY, S_TWO_NEAR, S_TWO_FAR, S_TWO_XY, S_TWO_X, S_TWO_Y,
+) = range(16)
+B_CORE, B_KEEP, B_SUMS, B_XY, B_X, B_Y, B_Z, B_TWO_Z, B_TWO = range(9)
+HEAD, FFN_TILE, SMALLS = range(3)
+
+
+SHAPES = {
+    HEAD: (HEAD_COLS + DV, HEAD_COLS, HEAD_COLS // 2),
+    FFN_TILE: (3 * TILE, 5 * TILE // 2, 3 * TILE // 2),
+    SMALLS: (2 * SMALL, 2 * SMALL, SMALL),
+}
+
+
 class Gather:
-    def __init__(self, me, planes, kinds, local_sem, send_sem, recv_sem):
-        self.me, self.planes, self.kinds = me, planes, kinds
+    copies = 16
+
+    def __init__(self, me, kinds, local_sem, send_sem, recv_sem):
+        self.me, self.kinds = me, kinds
         self.local_sem, self.send_sem, self.recv_sem = local_sem, send_sem, recv_sem
-        self.plane, self.place = me // 8, me % 8
+        self.z, self.y, self.x, self.core = me // 8, (me // 4) % 2, (me // 2) % 2, me % 2
 
     def local(self, kind, k):
-        shard, full, width, base = self.kinds[kind]
-        cols = columns(k, width)
+        shard, full, base = self.kinds[kind]
+        width = SHAPES[kind][0]
+        cols = span(k, width, 0, width)
         return pltpu.make_async_copy(
-            shard.at[:, cols], full.at[self.plane, self.place, :, cols], self.local_sem.at[base + k]
+            shard.at[:, cols], full.at[self.z, self.y, self.x, self.core, :, cols], self.local_sem.at[base + k]
         )
 
-    def copy(self, kind, k, number, by_y=False):
-        shard, full, width, base = self.kinds[kind]
-        cols = columns(k, width)
-        me, place = self.me, self.place
-        sems = self.send_sem.at[base + k, number], self.recv_sem.at[base + k, number]
-        if number > 6:
-            home = full.at[self.plane, place, :, cols]
-            return remote(shard.at[:, cols], home, *sems, flips(me, self.planes, number - 6, 8))
-        across_x, across_y = flip(place, 2), flip(place, 4)
-        which, other = (
-            (place, flip(me, 2)),
-            (place, flip(me, 4)),
-            (across_y, flip(me, 2)) if by_y else (across_x, flip(me, 4)),
-            (place, flip(me, 1)),
-            (across_x, flip(me, 1)),
-            (across_y, flip(me, 1)),
-            (flip(across_x, 4), flip(me, 1)),
-        )[number]
-        piece = full.at[:, which, :, cols]
-        return remote(piece, piece, *sems, other)
-
-    def planes_step(self, kind, k):
+    def copy(self, kind, k, name):
+        shard, full, base = self.kinds[kind]
+        width, part, half = SHAPES[kind]
+        one = span(k, width, 0, part)
+        two = span(k, width, part, width - part)
+        z, y, x, core = self.z, self.y, self.x, self.core
+        near, far = flip(z, 1), flip(z, 2)
+        here = lambda cols: (shard.at[:, cols], full.at[z, y, x, core, :, cols])
+        same = lambda ref: (ref, ref)
+        by_y = kind == FFN_TILE
+        (source, target), bit = {
+            G_NEAR: lambda: (here(one), 8),
+            G_FAR: lambda: (here(one), 16),
+            G_RELAY: lambda: (same(full.at[far, y, x, core, :, one]), 8),
+            G_X: lambda: (same(full.at[:, y, x, core, :, one]), 2),
+            G_Y: lambda: (same(full.at[:, y, x, core, :, one]), 4),
+            G_CORNER_Y: lambda: (same(full.at[:, y, 1 - x, core, :, span(k, width, 0, half)]), 4),
+            G_CORNER_X: lambda: (same(full.at[:, 1 - y, x, core, :, span(k, width, half, part - half)]), 2),
+            G_CORE_OWN: lambda: (same(full.at[:, y, :, core, :, one]), 1),
+            G_CORE_OTHER: lambda: (same(full.at[:, 1 - y, :, core, :, one]), 1),
+            G_TWO_X: lambda: (here(two), 2),
+            G_TWO_Y: lambda: (here(two), 4),
+            G_TWO_CORNER: lambda: (
+                (same(full.at[z, 1 - y, x, core, :, two]), 2)
+                if by_y
+                else (same(full.at[z, y, 1 - x, core, :, two]), 4)
+            ),
+            G_TWO_NEAR: lambda: (same(full.at[z, :, :, core, :, two]), 8),
+            G_TWO_FAR: lambda: (same(full.at[z, :, :, core, :, two]), 16),
+            G_TWO_RELAY: lambda: (same(full.at[far, :, :, core, :, two]), 8),
+            G_TWO_CORE: lambda: (same(full.at[:, :, :, core, :, two]), 1),
+        }[name]()
+        sems = self.send_sem.at[base + k, name], self.recv_sem.at[base + k, name]
+        return remote(source, target, *sems, flip(self.me, bit))
+
+    def send(self, kind, k, *names):
+        for name in names:
+            self.copy(kind, k, name).start()
+
+    def wait(self, kind, k, *names):
+        for name in names:
+            self.copy(kind, k, name).wait_recv()
+
+    def two(self, kind):
+        return SHAPES[kind][0] > SHAPES[kind][1]
+
+    def start(self, kind, k):
         self.local(kind, k).start()
-        for d in range(1, self.planes):
-            self.copy(kind, k, 6 + d).start()
-
-    def square_step(self, kind, k):
+        self.send(kind, k, G_FAR, G_NEAR)
+        if self.two(kind):
+            self.send(kind, k, G_TWO_X, G_TWO_Y)
+
+    def relay(self, kind, k):
+        self.wait(kind, k, G_FAR)
+        self.send(kind, k, G_RELAY)
+        if self.two(kind):
+            self.wait(kind, k, *((G_TWO_Y,) if kind == FFN_TILE else (G_TWO_X,)))
+            self.send(kind, k, G_TWO_CORNER)
+
+    def square(self, kind, k):
         self.local(kind, k).wait()
-        for d in range(1, self.planes):
-            self.copy(kind, k, 6 + d).wait_recv()
-        for number in (0, 1, 3):
-            self.copy(kind, k, number).start()
-
-    def diagonal_step(self, kind, k):
-        def go(by_y):
-            for number in (1, 0) if by_y else (0, 1):
-                self.copy(kind, k, number).wait_recv()
-                if number == int(by_y):
-                    self.copy(kind, k, 2, by_y).start()
-                self.copy(kind, k, 4 + number).start()
-
-        if isinstance(k, int):
-            go(k % 2 == 1)
-        else:
-            pl.when(k % 2 == 0)(lambda: go(False))
-            pl.when(k % 2 == 1)(lambda: go(True))
-
-    def core_step(self, kind, k):
-        self.copy(kind, k, 2).wait_recv()
-        self.copy(kind, k, 6).start()
-        for number in (3, 4, 5, 6):
-            self.copy(kind, k, number).wait_recv()
+        self.wait(kind, k, G_NEAR, G_RELAY)
+        self.send(kind, k, G_X, G_Y)
+        if self.two(kind):
+            self.wait(kind, k, *((G_TWO_X,) if kind == FFN_TILE else (G_TWO_Y,)), G_TWO_CORNER)
+            self.send(kind, k, G_TWO_FAR, G_TWO_NEAR)
+
+    def corner(self, kind, k):
+        self.wait(kind, k, G_X)
+        self.send(kind, k, G_CORNER_Y, G_CORE_OWN)
+        self.wait(kind, k, G_Y)
+        self.send(kind, k, G_CORNER_X)
+        if self.two(kind):
+            self.wait(kind, k, G_TWO_FAR)
+            self.send(kind, k, G_TWO_RELAY)
+
+    def across(self, kind, k):
+        self.wait(kind, k, G_CORNER_Y, G_CORNER_X)
+        self.send(kind, k, G_CORE_OTHER)
+        if self.two(kind):
+            self.wait(kind, k, G_TWO_NEAR, G_TWO_RELAY)
+            self.send(kind, k, G_TWO_CORE)
+
+    def complete(self, kind, k):
+        self.wait(kind, k, G_CORE_OWN, G_CORE_OTHER)
+        if self.two(kind):
+            self.wait(kind, k, G_TWO_CORE)
 
     def finish(self, kind, k):
-        for number in range(6 + self.planes):
-            self.copy(kind, k, number).wait_send()
+        names = [G_NEAR, G_FAR, G_RELAY, G_X, G_Y, G_CORNER_Y, G_CORNER_X, G_CORE_OWN, G_CORE_OTHER]
+        if self.two(kind):
+            names += [G_TWO_X, G_TWO_Y, G_TWO_CORNER, G_TWO_NEAR, G_TWO_FAR, G_TWO_RELAY, G_TWO_CORE]
+        for name in names:
+            self.copy(kind, k, name).wait_send()
 
 
 class Scatter:
-    depths = {"core": 4, "keep": 2, "sums": 6, "x": 6, "y": 6, "xy": 4, "z": 4}
-
-    def __init__(self, me, planes, kinds, store, core, keep, sums, x, y, xy, z, local_sem, send_sem, recv_sem):
-        self.me, self.planes, self.kinds, self.store = me, planes, kinds, store
+    copies = 16
+    depths = {B_CORE: 4, B_KEEP: 2, B_SUMS: 6, B_XY: 4, B_X: 8, B_Y: 8, B_Z: 4, B_TWO_Z: 8, B_TWO: 4}
+
+    def __init__(self, me, kinds, store, core, keep, sums, xy, x, y, z, two_z, two, local_sem, send_sem, recv_sem):
+        self.me, self.kinds, self.store = me, kinds, store
         self.from_core, self.keep, self.sums = core, keep, sums
-        self.from_x, self.from_y, self.from_xy, self.from_z = x, y, xy, z
+        self.from_xy, self.from_x, self.from_y, self.from_z = xy, x, y, z
+        self.two_z, self.from_two = two_z, two
         self.local_sem, self.send_sem, self.recv_sem = local_sem, send_sem, recv_sem
-        self.plane, self.core, self.here = me // 8, me % 2, (me // 2) % 4
-
-    def piece(self, r, place, width):
-        return self.sums.at[r % self.depths["sums"], :, place, :, pl.ds(0, width)]
-
-    def copy(self, kind, r, k, number, by_y=False):
-        width, source, _ = self.kinds[kind]
-        cols = pl.ds(0, width)
-        sems = self.send_sem.at[r, number], self.recv_sem.at[r, number]
-        me, here = self.me, self.here
-        if number == 0:
-            target = self.from_core.at[r % self.depths["core"], :, :, :, cols]
-            return remote(source(k, 1 - self.core), target, *sems, flip(me, 1))
-        if number == 1:
-            target = self.from_xy.at[r % self.depths["xy"], :, :, cols]
-            return remote(self.piece(r, flip(flip(here, 1), 2), width), target, *sems, flip(me, 4 if by_y else 2))
-        if number == 2:
-            target = self.from_x.at[r % self.depths["x"], :, :, cols]
-            return remote(self.piece(r, flip(here, 1), width), target, *sems, flip(me, 2))
-        if number == 3:
-            target = self.from_y.at[r % self.depths["y"], :, :, cols]
-            return remote(self.piece(r, flip(here, 2), width), target, *sems, flip(me, 4))
-        d = number - 3
-        own = self.sums.at[r % self.depths["sums"], flips(self.plane, self.planes, d, 1), here, :, cols]
-        target = self.from_z.at[r % self.depths["z"], d - 1, :, cols]
-        return remote(own, target, *sems, flips(me, self.planes, d, 8))
+        self.z, self.core = me // 8, me % 2
+        self.here = (me // 2) % 4
+        self.across_x, self.across_y = flip(self.here, 1), flip(self.here, 2)
+        self.both = 3 - self.here
+        self.near, self.far = flip(self.z, 1), flip(self.z, 2)
+        self.opposite = 3 - self.z
+
+    def slot(self, name, r):
+        return r % self.depths[name]
+
+    def copy(self, kind, r, k, name):
+        source = self.kinds[kind][0]
+        width, part, half = SHAPES[kind]
+        whole, one, two = pl.ds(0, width), pl.ds(0, part), pl.ds(part, width - part)
+        first, second = pl.ds(0, half), pl.ds(half, part - half)
+        rest = pl.ds(0, width - part)
+        sums = self.sums.at[self.slot(B_SUMS, r)]
+        here, across_x, across_y, both, z = self.here, self.across_x, self.across_y, self.both, self.z
+        by_y = kind == FFN_TILE
+        place = lambda where, cols: sums.at[:, where, :, cols]
+        origin, target, bit = {
+            S_CORE: lambda: (
+                source(k, 1 - self.core), self.from_core.at[self.slot(B_CORE, r), :, :, :, whole], 1
+            ),
+            S_XY_X: lambda: (place(both, first), self.from_xy.at[self.slot(B_XY, r), :, :, first], 2),
+            S_XY_Y: lambda: (place(both, second), self.from_xy.at[self.slot(B_XY, r), :, :, second], 4),
+            S_X_EARLY: lambda: (place(across_x, first), self.from_x.at[self.slot(B_X, r), :, :, first], 2),
+            S_X_LATE: lambda: (place(across_x, second), self.from_x.at[self.slot(B_X, r), :, :, second], 2),
+            S_Y_EARLY: lambda: (place(across_y, second), self.from_y.at[self.slot(B_Y, r), :, :, second], 4),
+            S_Y_LATE: lambda: (place(across_y, first), self.from_y.at[self.slot(B_Y, r), :, :, first], 4),
+            S_RELAY: lambda: (sums.at[self.opposite, here, :, one], self.from_z.at[self.slot(B_Z, r), 0, :, one], 8),
+            S_NEAR: lambda: (sums.at[self.near, here, :, one], self.from_z.at[self.slot(B_Z, r), 1, :, one], 8),
+            S_FAR: lambda: (sums.at[self.far, here, :, one], self.from_z.at[self.slot(B_Z, r), 2, :, one], 16),
+            S_TWO_RELAY: lambda: (
+                sums.at[self.opposite, :, :, two], self.two_z.at[self.slot(B_TWO_Z, r), 0, :, :, rest], 8
+            ),
+            S_TWO_NEAR: lambda: (
+                sums.at[self.near, :, :, two], self.two_z.at[self.slot(B_TWO_Z, r), 1, :, :, rest], 8
+            ),
+            S_TWO_FAR: lambda: (
+                sums.at[self.far, :, :, two], self.two_z.at[self.slot(B_TWO_Z, r), 2, :, :, rest], 16
+            ),
+            S_TWO_XY: lambda: (
+                sums.at[z, both, :, two], self.from_two.at[self.slot(B_TWO, r), 0, :, rest], 4 if by_y else 2
+            ),
+            S_TWO_X: lambda: (sums.at[z, across_x, :, two], self.from_two.at[self.slot(B_TWO, r), 1, :, rest], 2),
+            S_TWO_Y: lambda: (sums.at[z, across_y, :, two], self.from_two.at[self.slot(B_TWO, r), 2, :, rest], 4),
+        }[name]()
+        sems = self.send_sem.at[r, name], self.recv_sem.at[r, name]
+        return remote(origin, target, *sems, flip(self.me, bit))
+
+    def send(self, kind, r, k, *names):
+        for name in names:
+            self.copy(kind, r, k, name).start()
+
+    def wait(self, kind, r, k, *names):
+        for name in names:
+            self.copy(kind, r, k, name).wait_recv()
+
+    def two(self, kind):
+        return SHAPES[kind][0] > SHAPES[kind][1]
 
     def load(self, kind, r, k):
-        width, source, in_place = self.kinds[kind]
+        source = self.kinds[kind][0]
         return pltpu.make_async_copy(
-            source(k, self.core), self.keep.at[r % 2, :, :, :, pl.ds(0, width)], self.local_sem.at[r]
+            source(k, self.core), self.keep.at[r % 2, :, :, :, pl.ds(0, SHAPES[kind][0])], self.local_sem.at[r]
         )
 
     def core_step(self, kind, r, k):
-        self.copy(kind, r, k, 0).start()
+        self.send(kind, r, k, S_CORE)
 
     def load_step(self, kind, r, k):
-        if self.kinds[kind][2] is None:
+        if self.kinds[kind][1] is None:
             self.load(kind, r, k).start()
 
-    def add(self, kind, r, place, first, others):
-        cols = pl.ds(0, self.kinds[kind][0])
-
+    def add_planes(self, r, place, cols, first, others):
         def one(plane, carry):
-            total = first(plane, cols).astype(F32)
+            total = first(plane).astype(F32)
             for read in others:
-                total = total + read(plane, cols).astype(F32)
-            self.sums[r % self.depths["sums"], plane, place, :, cols] = total.astype(BF16)
+                total = total + read(plane).astype(F32)
+            self.sums[self.slot(B_SUMS, r), plane, place, :, cols] = total.astype(BF16)
             return carry
 
-        lax.fori_loop(0, self.planes, one, 0)
-
-    def held(self, r, place):
-        return lambda plane, cols: self.sums[r % self.depths["sums"], plane, place, :, cols]
+        lax.fori_loop(0, 4, one, 0)
+
+    def add_places(self, r, plane, cols, others):
+        slot = self.slot(B_SUMS, r)
+        for place in range(4):
+            total = self.sums[slot, plane, place, :, cols].astype(F32)
+            for read in others:
+                total = total + read(place).astype(F32)
+            self.sums[slot, plane, place, :, cols] = total.astype(BF16)
+
+    def held(self, r, place, cols):
+        return lambda plane: self.sums[self.slot(B_SUMS, r), plane, place, :, cols]
 
     def chip_step(self, kind, r, k):
-        width, _, in_place = self.kinds[kind]
-        self.copy(kind, r, k, 0).wait_recv()
+        in_place = self.kinds[kind][1]
+        width, part, half = SHAPES[kind]
+        whole = pl.ds(0, width)
+        self.wait(kind, r, k, S_CORE)
         if in_place is None:
             self.load(kind, r, k).wait()
-            mine = lambda place: (lambda plane, cols: self.keep[r % 2, plane, place, :, cols])
+            mine = lambda place: (lambda plane: self.keep[r % 2, plane, place, :, whole])
         else:
-            mine = lambda place: (lambda plane, cols: in_place(k, plane, place, self.core))
-        got = lambda place: (lambda plane, cols: self.from_core[r % self.depths["core"], plane, place, :, cols])
-        across_x, across_y = flip(self.here, 1), flip(self.here, 2)
-        both = flip(across_x, 2)
-
-        def go(by_y):
-            self.add(kind, r, both, got(both), [mine(both)])
-            self.copy(kind, r, k, 1, by_y).start()
-            if by_y:
-                self.add(kind, r, across_y, got(across_y), [mine(across_y)])
-                self.copy(kind, r, k, 3).start()
-                self.add(kind, r, across_x, got(across_x), [mine(across_x)])
-            else:
-                self.add(kind, r, across_x, got(across_x), [mine(across_x)])
-                self.copy(kind, r, k, 2).start()
-                self.add(kind, r, across_y, got(across_y), [mine(across_y)])
-
-        pl.when(r % 2 == 0)(lambda: go(False))
-        pl.when(r % 2 == 1)(lambda: go(True))
-        self.add(kind, r, self.here, got(self.here), [mine(self.here)])
-        self.copy(kind, r, k, 0).wait_send()
-
-    def diagonal_step(self, kind, r, k):
-        self.copy(kind, r, k, 1).wait_recv()
-
-        def go(by_y):
-            place = flip(self.here, 1 if by_y else 2)
-            passed = lambda plane, cols: self.from_xy[r % self.depths["xy"], plane, :, cols]
-            self.add(kind, r, place, self.held(r, place), [passed])
-            self.copy(kind, r, k, 2 if by_y else 3).start()
-
-        pl.when(r % 2 == 0)(lambda: go(False))
-        pl.when(r % 2 == 1)(lambda: go(True))
+            mine = lambda place: (lambda plane: in_place(k, plane, place, self.core))
+        got = lambda place: (lambda plane: self.from_core[self.slot(B_CORE, r), plane, place, :, whole])
+        for place, names in (
+            (self.both, (S_XY_X, S_XY_Y)),
+            (self.across_x, (S_X_EARLY,)),
+            (self.across_y, (S_Y_EARLY,)),
+            (self.here, (S_TWO_RELAY, S_TWO_NEAR) if self.two(kind) else ()),
+        ):
+            self.add_planes(r, place, whole, got(place), [mine(place)])
+            self.send(kind, r, k, *names)
+        self.copy(kind, r, k, S_CORE).wait_send()
+
+    def corner_step(self, kind, r, k):
+        width, part, half = SHAPES[kind]
+        first, second = pl.ds(0, half), pl.ds(half, part - half)
+        passed = lambda cols: (lambda plane: self.from_xy[self.slot(B_XY, r), plane, :, cols])
+        self.wait(kind, r, k, S_XY_X)
+        self.add_planes(r, self.across_y, first, self.held(r, self.across_y, first), [passed(first)])
+        self.send(kind, r, k, S_Y_LATE)
+        self.wait(kind, r, k, S_XY_Y)
+        self.add_planes(r, self.across_x, second, self.held(r, self.across_x, second), [passed(second)])
+        self.send(kind, r, k, S_X_LATE)
+        if self.two(kind):
+            two, rest = pl.ds(part, width - part), pl.ds(0, width - part)
+            self.wait(kind, r, k, S_TWO_RELAY)
+            self.add_places(r, self.far, two, [lambda place: self.two_z[self.slot(B_TWO_Z, r), 0, place, :, rest]])
+            self.send(kind, r, k, S_TWO_FAR)
 
     def square_step(self, kind, r, k):
-        self.copy(kind, r, k, 2).wait_recv()
-        self.copy(kind, r, k, 3).wait_recv()
-        from_x = lambda plane, cols: self.from_x[r % self.depths["x"], plane, :, cols]
-        from_y = lambda plane, cols: self.from_y[r % self.depths["y"], plane, :, cols]
-        self.add(kind, r, self.here, self.held(r, self.here), [from_x, from_y])
-        for d in range(1, self.planes):
-            self.copy(kind, r, k, 3 + d).start()
-
-    def planes_step(self, kind, r, k):
-        cols = pl.ds(0, self.kinds[kind][0])
-        total = self.held(r, self.here)(self.plane, cols).astype(F32)
-        for d in range(1, self.planes):
-            self.copy(kind, r, k, 3 + d).wait_recv()
-            total = total + self.from_z[r % self.depths["z"], d - 1, :, cols].astype(F32)
+        width, part, half = SHAPES[kind]
+        one = pl.ds(0, part)
+        self.wait(kind, r, k, S_X_EARLY, S_X_LATE, S_Y_EARLY, S_Y_LATE)
+        from_x = lambda plane: self.from_x[self.slot(B_X, r), plane, :, one]
+        from_y = lambda plane: self.from_y[self.slot(B_Y, r), plane, :, one]
+        self.add_planes(r, self.here, one, self.held(r, self.here, one), [from_x, from_y])
+        self.send(kind, r, k, S_RELAY, S_NEAR)
+        if self.two(kind):
+            two, rest = pl.ds(part, width - part), pl.ds(0, width - part)
+            self.wait(kind, r, k, S_TWO_NEAR, S_TWO_FAR)
+            self.add_places(
+                r, self.z, two,
+                [lambda place, i=i: self.two_z[self.slot(B_TWO_Z, r), i, place, :, rest] for i in (1, 2)],
+            )
+            self.send(kind, r, k, S_TWO_XY, S_TWO_X if kind != FFN_TILE else S_TWO_Y)
+
+    def relay_step(self, kind, r, k):
+        width, part, half = SHAPES[kind]
+        slot, one = self.slot(B_SUMS, r), pl.ds(0, part)
+        self.wait(kind, r, k, S_RELAY)
+        total = self.sums[slot, self.far, self.here, :, one].astype(F32)
+        total = total + self.from_z[self.slot(B_Z, r), 0, :, one].astype(F32)
+        self.sums[slot, self.far, self.here, :, one] = total.astype(BF16)
+        self.send(kind, r, k, S_FAR)
+        if self.two(kind):
+            two, rest = pl.ds(part, width - part), pl.ds(0, width - part)
+            place = self.across_x if kind == FFN_TILE else self.across_y
+            self.wait(kind, r, k, S_TWO_XY)
+            total = self.sums[slot, self.z, place, :, two].astype(F32)
+            total = total + self.from_two[self.slot(B_TWO, r), 0, :, rest].astype(F32)
+            self.sums[slot, self.z, place, :, two] = total.astype(BF16)
+            self.send(kind, r, k, S_TWO_X if kind == FFN_TILE else S_TWO_Y)
+
+    def last_step(self, kind, r, k):
+        width, part, half = SHAPES[kind]
+        slot, one = self.slot(B_SUMS, r), pl.ds(0, part)
+        self.wait(kind, r, k, S_NEAR, S_FAR)
+        total = self.sums[slot, self.z, self.here, :, one].astype(F32)
+        for i in (1, 2):
+            total = total + self.from_z[self.slot(B_Z, r), i, :, one].astype(F32)
+        names = [S_XY_X, S_XY_Y, S_X_EARLY, S_X_LATE, S_Y_EARLY, S_Y_LATE, S_RELAY, S_NEAR, S_FAR]
+        if self.two(kind):
+            two, rest = pl.ds(part, width - part), pl.ds(0, width - part)
+            self.wait(kind, r, k, S_TWO_X, S_TWO_Y)
+            more = self.sums[slot, self.z, self.here, :, two].astype(F32)
+            for i in (1, 2):
+                more = more + self.from_two[self.slot(B_TWO, r), i, :, rest].astype(F32)
+            total = jnp.concatenate([total, more], axis=1)
+            names += [S_TWO_RELAY, S_TWO_NEAR, S_TWO_FAR, S_TWO_XY, S_TWO_X, S_TWO_Y]
         self.store(kind, k, total)
-        for number in range(1, 3 + self.planes):
-            self.copy(kind, r, k, number).wait_send()
+        for name in names:
+            self.copy(kind, r, k, name).wait_send()
 
 
 class Total:
-    def __init__(self, me, planes, value_ref, out_ref, got, stage, send_sem, recv_sem):
-        self.me, self.planes, self.value_ref, self.out_ref = me, planes, value_ref, out_ref
+    bits = (1, 2, 4, 8, 16)
+
+    def __init__(self, me, value_ref, out_ref, got, stage, send_sem, recv_sem):
+        self.me, self.value_ref, self.out_ref = me, value_ref, out_ref
         self.got, self.stage, self.send_sem, self.recv_sem = got, stage, send_sem, recv_sem
 
     def copy(self, number):
         sems = self.send_sem.at[number], self.recv_sem.at[number]
-        if number < 3:
-            return remote(self.stage.at[number], self.got.at[number], *sems, flip(self.me, 1 << number))
-        other = flips(self.me, self.planes, number - 2, 8)
-        return remote(self.stage.at[3], self.got.at[3 + self.me // 8], *sems, other)
+        return remote(self.stage.at[number], self.got.at[number], *sems, flip(self.me, self.bits[number]))
 
     def step(self, number):
-        planes = self.planes
-        if number == 0:
-            self.stage[0] = self.value_ref[...]
-        elif number <= 3:
+        last = len(self.bits)
+        value = self.value_ref[...]
+        if number > 0:
             self.copy(number - 1).wait_recv()
-            self.stage[number] = self.stage[number - 1] + self.got[number - 1]
-        if number < 3:
+            value = self.stage[number - 1] + self.got[number - 1]
+        if number < last:
+            self.stage[number] = value
             self.copy(number).start()
-        elif number == 3:
-            for d in range(1, planes):
-                self.copy(2 + d).start()
-            self.got[3 + self.me // 8] = self.stage[3]
         else:
-            for d in range(1, planes):
-                self.copy(2 + d).wait_recv()
-            total = self.got[3]
-            for other in range(1, planes):
-                total = total + self.got[3 + other]
-            self.out_ref[...] = total
-            for number in range(2 + planes):
+            self.out_ref[...] = value
+            for number in range(last):
                 self.copy(number).wait_send()
 
 
@@ -398,7 +512,9 @@
 def head_taps(small_ref, head):
     wide = 2 * head
     places = [(0, head), (1, head)] + [(2 + head // 4, wide % 8 + i) for i in (0, 1)]
-    blocks = [small_ref[z, p, 0:16, SMALL : 2 * SMALL][0:4].astype(F32) for z, p in places]
+    blocks = [
+        small_ref[z, p // 4, (p // 2) % 2, p % 2, 0:16, SMALL : 2 * SMALL][0:4].astype(F32) for z, p in places
+    ]
     return jnp.concatenate(blocks, axis=1)
 
 
@@ -419,49 +535,68 @@
     shard_small, shard_heads, shard_tiles, x_ref, cot_ref, aux_ref, seg_ref, consts_ref, gain_ref,
     full_small, full_heads, full_tiles, small_ref, xnt_ref, cols_ref, rows_ref, logs_ref, factor_ref,
     proj_ref, mixed_ref, inv_ref, upd_ref, core_ref, dw_ref,
-    output_ref, grad_mid_ref, branch_ref, brancht_ref, d_gain2_ref,
-    w_buf, xn, cott, middle, nm, nmt, out_sum, nm_sum, gains, scale2_ref, copy_sem, local_sem, send_sem, recv_sem,
+    output_ref, middle, nm_sum,
+    w_buf, xn, cott, nm, nmt, out_sum, gains, copy_sem, w_sem, local_sem, send_sem, recv_sem,
 ):
     step = pl.program_id(0)
     tokens = x_ref.shape[0]
     chunks = HEADS + tiles
     me = lax.axis_index("dp")
     kinds = {
-        "small": (shard_small, full_small, 2 * SMALL, chunks),
-        "head": (shard_heads, full_heads, HEAD_COLS + DV, 0),
-        "tile": (shard_tiles, full_tiles, 3 * TILE, HEADS),
+        SMALLS: (shard_small, full_small, chunks),
+        HEAD: (shard_heads, full_heads, 0),
+        FFN_TILE: (shard_tiles, full_tiles, HEADS),
     }
-    work = Gather(me, planes, kinds, local_sem, send_sem, recv_sem)
+    work = Gather(me, kinds, local_sem, send_sem, recv_sem)
 
     def at(chunk, act):
-        pl.when((chunk >= 0) & (chunk < HEADS))(lambda: act("head", chunk))
-        pl.when((chunk >= HEADS) & (chunk < chunks))(lambda: act("tile", chunk - HEADS))
+        pl.when((chunk >= 0) & (chunk < HEADS))(lambda: act(HEAD, chunk))
+        pl.when((chunk >= HEADS) & (chunk < chunks))(lambda: act(FFN_TILE, chunk - HEADS))
+
+    def weights(kind, k, slot):
+        full, width = kinds[kind][1], SHAPES[kind][0]
+        place = w_buf.at[slot, :, :, :, :, :, pl.ds(0, width)]
+        return pltpu.make_async_copy(full.at[:, :, :, :, :, span(k, width, 0, width)], place, w_sem.at[slot])
+
+    ahead = ((6, work.start), (5, work.relay), (4, work.square), (2, work.corner), (1, work.across))
+
+    def early(step):
+        for lead, act in ahead:
+            if step + lead >= 0:
+                act(HEAD, step + lead)
+
+    def midway():
+        for lead, act in ahead[:3]:
+            at(step + lead, act)
+        at(step + 1, work.complete)
+        at(step + 1, lambda kind, k: weights(kind, k, (step + 1) % 2).start())
 
     @pl.when(step == 0)
     def _():
-        enter(planes)
-        work.planes_step("small", 0)
-        for k in (0, 1, 2):
-            work.planes_step("head", k)
+        enter()
+        work.start(SMALLS, 0)
+        early(-6)
 
         def prepare(rows):
             middle[rows, :] = x_ref[rows, :].astype(F32)
             cott[:, rows] = cot_ref[rows, :].astype(F32).T.astype(BF16)
 
         row_blocks(tokens, prepare)
+        work.relay(SMALLS, 0)
+        early(-5)
+        work.square(SMALLS, 0)
+        early(-4)
+        work.corner(SMALLS, 0)
+        early(-3)
+        work.across(SMALLS, 0)
         out_sum[...] = jnp.zeros_like(out_sum)
         nm_sum[...] = jnp.zeros_like(nm_sum)
-        d_gain2_ref[...] = jnp.zeros_like(d_gain2_ref)
-        work.square_step("small", 0)
-        work.square_step("head", 0)
-        work.diagonal_step("small", 0)
-        work.square_step("head", 1)
-        work.core_step("small", 0)
-        work.diagonal_step("head", 0)
+        work.complete(SMALLS, 0)
+        early(-2)
         copy = pltpu.make_async_copy(full_small, small_ref, copy_sem)
         copy.start()
         copy.wait()
-        small = merge(small_ref[:, :, :, 0:SMALL])
+        small = merge(small_ref[..., 0:SMALL])
         turned = small.astype(F32).T
         gains[0:1, :] = turned[16:17, :]
         gains[1:2, :] = turned[17:18, :]
@@ -492,22 +627,22 @@
             )
             rows_ref[0:8, part] = cum.T[0:8]
         rows_ref[8:16, :] = seg_ref[...]
-        work.finish("small", 0)
-
-    at(step + 3, work.planes_step)
-    at(step + 2, work.square_step)
-    at(step + 1, work.diagonal_step)
-    at(step, work.core_step)
+        early(-1)
+        work.finish(SMALLS, 0)
+        work.complete(HEAD, 0)
+        weights(HEAD, 0, 0).start()
+
+    for lead, act in ahead[3:]:
+        at(step + lead, act)
+    at(step, lambda kind, k: weights(kind, k, step % 2).wait())
     at(step - 1, work.finish)
 
     @pl.when(step < HEADS)
     def _():
-        copy = pltpu.make_async_copy(full_heads.at[:, :, :, columns(step, HEAD_COLS + DV)], w_buf, copy_sem)
-        copy.start()
-        copy.wait()
-        w = merge(w_buf[...])
+        w = merge(w_buf[step % 2])
         projected = jnp.dot(xn[...], w[:, :HEAD_COLS], preferred_element_type=F32)
         proj_ref[...] = projected
+        midway()
         _, _, _, _, q, k, value, _, _, cum, rate, seg = head_inputs(
             projected, head_taps(small_ref, step), cols_ref[...], step
         )
@@ -546,16 +681,13 @@
 
     @pl.when(step >= HEADS)
     def _():
-        place = w_buf.at[:, :, :, pl.ds(0, 3 * TILE)]
-        copy = pltpu.make_async_copy(full_tiles.at[:, :, :, columns(step - HEADS, 3 * TILE)], place, copy_sem)
-        copy.start()
-        copy.wait()
-        w = merge(w_buf[:, :, :, 0 : 3 * TILE])
+        w = merge(w_buf[step % 2, :, :, :, :, :, 0 : 3 * TILE])
         gate_up = jnp.dot(nm[...], w[:, : 2 * TILE], preferred_element_type=F32)
         gate, up = gate_up[:, :TILE], gate_up[:, TILE:]
         sig = sigmoid(gate)
         swish = gate * sig
         hidden = (swish * up).astype(BF16)
+        midway()
         grad_hidden = jnp.dot(cot_ref[...], w[:, 2 * TILE :], preferred_element_type=F32)
         grad_gate = grad_hidden * up * (sig + swish * (1.0 - sig))
         grad_up = grad_hidden * swish
@@ -567,22 +699,11 @@
 
     @pl.when(step == chunks - 1)
     def _():
-        def back(rows):
-            mid = middle[rows, :]
-            output_ref[rows, :] = (mid + out_sum[rows, :]).astype(BF16)
-            scale = lax.rsqrt(jnp.mean(mid * mid, axis=1, keepdims=True) + epsilon)
-            normed = mid * scale
-            grad = nm_sum[rows, :]
-            d_gain2_ref[0:1, :] += jnp.sum(grad * normed, axis=0, keepdims=True)
-            d_normed = grad * gains[1:2, :]
-            d_mid = scale * (d_normed - normed * jnp.mean(d_normed * normed, axis=1, keepdims=True))
-            d_mid = d_mid + cot_ref[rows, :].astype(F32)
-            grad_mid_ref[rows, :] = d_mid
-            branch_ref[rows, :] = d_mid.astype(BF16)
-            brancht_ref[:, rows] = d_mid.T.astype(BF16)
-
-        row_blocks(tokens, back)
-        work.finish("tile", tiles - 1)
+        def add(rows):
+            output_ref[rows, :] = (middle[rows, :] + out_sum[rows, :]).astype(BF16)
+
+        row_blocks(tokens, add)
+        work.finish(FFN_TILE, tiles - 1)
 
 
 def once(shape):
@@ -598,7 +719,7 @@
     tile = lambda i: jnp.maximum(i - HEADS, 0)
     save = pl.BlockSpec((1, tokens, SEQ), lambda i: (head(i), 0, 0))
     shape = jax.ShapeDtypeStruct
-    whole = [((planes, 8, rows, s.shape[1]), BF16) for s in shards]
+    whole = [((planes, 2, 2, 2, rows, s.shape[1]), BF16) for s in shards]
     outs = [
         (hbm, *whole[0]),
         (hbm, *whole[1]),
@@ -617,9 +738,7 @@
         (pl.BlockSpec((width, 3 * TILE), lambda i: (0, tile(i))), (width, tiles * 3 * TILE), BF16),
         (once((tokens, width)), (tokens, width), BF16),
         (once((tokens, width)), (tokens, width), F32),
-        (once((tokens, width)), (tokens, width), BF16),
-        (once((width, tokens)), (width, tokens), BF16),
-        (once((8, width)), (8, width), F32),
+        (once((tokens, width)), (tokens, width), F32),
     ]
     return pl.pallas_call(
         partial(forward_body, planes, tiles),
@@ -628,20 +747,18 @@
         out_specs=[o[0] for o in outs],
         out_shape=[shape(o[1], o[2]) for o in outs],
         scratch_shapes=[
-            pltpu.VMEM((planes, 8, rows, HEAD_COLS + DV), BF16),
+            pltpu.VMEM((2, planes, 2, 2, 2, rows, HEAD_COLS + DV), BF16),
+            pltpu.VMEM((tokens, width), BF16),
+            pltpu.VMEM((width, tokens), BF16),
             pltpu.VMEM((tokens, width), BF16),
             pltpu.VMEM((width, tokens), BF16),
             pltpu.VMEM((tokens, width), F32),
-            pltpu.VMEM((tokens, width), BF16),
-            pltpu.VMEM((width, tokens), BF16),
-            pltpu.VMEM((tokens, width), F32),
-            pltpu.VMEM((tokens, width), F32),
             pltpu.VMEM((8, width), F32),
-            pltpu.VMEM((tokens, 128), F32),
             pltpu.SemaphoreType.DMA,
+            pltpu.SemaphoreType.DMA((2,)),
             pltpu.SemaphoreType.DMA((chunks + 1,)),
-            pltpu.SemaphoreType.DMA((chunks + 1, 6 + planes)),
-            pltpu.SemaphoreType.DMA((chunks + 1, 6 + planes)),
+            pltpu.SemaphoreType.DMA((chunks + 1, Gather.copies)),
+            pltpu.SemaphoreType.DMA((chunks + 1, Gather.copies)),
         ],
         compiler_params=pltpu.CompilerParams(
             collective_id=0, has_side_effects=True, vmem_limit_bytes=60 * MIB
@@ -650,7 +767,14 @@
     )(*shards, x, cot, aux, seg_rows, consts, gain)
 
 
-LAG = 2
+FIRST = 4
+
+
+def row_sums(count, body, width, size=128):
+    def one(i, total):
+        return body(pl.ds(pl.multiple_of(i * size, size), size), total)
+
+    return lax.fori_loop(0, count // size, one, jnp.zeros((1, width), F32))
 
 
 def head_step(j):
@@ -659,31 +783,29 @@
 
 def backward_body(
     planes, tiles, total_chunks,
-    dwf_ref, gb_ref, gbt_ref, xnt_ref, w_ref, proj_ref, mixed_ref, inv_ref, upd_ref, core_ref,
-    small_ref, cols_ref, rows_ref, logs_ref, factor_ref, gain_ref, x_ref, grad_mid_ref, d_gain2_ref,
+    dwf_ref, middle_ref, nm_sum_ref, cot_ref, xnt_ref, w_ref, proj_ref, mixed_ref, inv_ref, upd_ref, core_ref,
+    small_ref, cols_ref, rows_ref, logs_ref, factor_ref, gain_ref, x_ref,
     input_grad_ref, own_mixer, own_out, own_ffn, own_down, own_small, shared_ref,
-    dw, d_small, gxn, dcols, drows, dgain, dproj, value_ref,
-    from_core, keep, sums, from_x, from_y, from_xy, from_z, got, stage,
-    local_sem, send_sem, recv_sem, total_send, total_recv,
+    gb_ref, gbt_ref, grad_mid_ref, gains, dw, d_small, gxn, dcols, drows, dgain, dproj, value_ref,
+    *scratch,
 ):
+    *buffers, got, stage, local_sem, send_sem, recv_sem, total_send, total_recv = scratch
     step = pl.program_id(0)
-    tokens = gb_ref.shape[0]
+    tokens = middle_ref.shape[0]
     rows = own_small.shape[0]
     hidden = tiles * TILE
     me = lax.axis_index("dp")
 
     def tile_source(k, core):
-        return dwf_ref.at[:, :, core, :, columns(k, 3 * TILE)]
+        return dwf_ref.at[:, :, core, :, span(k, 3 * TILE, 0, 3 * TILE)]
 
     kinds = {
-        "tile": (3 * TILE, tile_source, None),
-        "head": (
-            HEAD_COLS + DV,
+        FFN_TILE: (tile_source, None),
+        HEAD: (
             lambda k, core: dw.at[k % 2, :, :, core],
             lambda k, plane, place, core: dw[k % 2, plane, place, core],
         ),
-        "small": (
-            2 * SMALL,
+        SMALLS: (
             lambda k, core: d_small.at[:, :, core],
             lambda k, plane, place, core: d_small[plane, place, core],
         ),
@@ -693,9 +815,9 @@
         def put(ref, start, source, width):
             ref[:, pl.ds(pl.multiple_of(start, 128), width)] = total[:, source : source + width]
 
-        if kind == "small":
+        if kind == SMALLS:
             own_small[...] = total
-        elif kind == "head":
+        elif kind == HEAD:
             put(own_mixer, k * DK, 0, DK)
             put(own_mixer, HEADS * DK + k * DK, DK, DK)
             put(own_mixer, 2 * HEADS * DK + k * DV, 2 * DK, DV)
@@ -706,38 +828,63 @@
             put(own_ffn, hidden + k * TILE, TILE, TILE)
             put(own_down, k * TILE, 2 * TILE, TILE)
 
-    work = Scatter(
-        me, planes, kinds, store, from_core, keep, sums, from_x, from_y, from_xy, from_z, local_sem, send_sem, recv_sem
-    )
-    small_sum = Total(me, planes, value_ref, shared_ref, got, stage, total_send, total_recv)
+    work = Scatter(me, kinds, store, *buffers, local_sem, send_sem, recv_sem)
+    small_sum = Total(me, value_ref, shared_ref, got, stage, total_send, total_recv)
 
     last = total_chunks - 1
 
     def at(r, act):
-        is_head = (r >= 3) & (r < last) & (r % 2 == 1)
-        is_tile = (r >= 0) & (r < last) & ((r < 3) | (r % 2 == 0))
-        pl.when(is_tile)(lambda: act("tile", r, r // 2 + (r + last - 2) // (last - 1)))
-        pl.when(is_head)(lambda: act("head", r, (r - 3) // 2))
-        pl.when(r == last)(lambda: act("small", r, 0))
+        is_head = (r >= FIRST) & (r < last) & ((r - FIRST) % 2 == 0)
+        is_early = (r >= 0) & (r < FIRST)
+        is_tile = (r > FIRST) & (r < last) & ((r - FIRST) % 2 == 1)
+        pl.when(is_early)(lambda: act(FFN_TILE, r, r))
+        pl.when(is_tile)(lambda: act(FFN_TILE, r, (r + FIRST - 1) // 2))
+        pl.when(is_head)(lambda: act(HEAD, r, (r - FIRST) // 2))
+        pl.when(r == last)(lambda: act(SMALLS, r, 0))
 
     @pl.when(step == 0)
     def _():
-        enter(planes)
-        for r in (0, 1):
-            work.core_step("tile", r, r)
-        work.load_step("tile", 0, 0)
+        enter()
+        work.core_step(FFN_TILE, 0, 0)
+        work.core_step(FFN_TILE, 1, 1)
+        work.load_step(FFN_TILE, 0, 0)
         gxn[...] = jnp.zeros_like(gxn)
         dcols[...] = jnp.zeros_like(dcols)
         drows[...] = jnp.zeros_like(drows)
         dgain[...] = jnp.zeros_like(dgain)
         d_small[...] = jnp.zeros_like(d_small)
-
-    at(step - 3 * LAG, work.planes_step)
-    at(step - 2 * LAG, work.square_step)
-    at(step - LAG, work.diagonal_step)
-    at(step, work.chip_step)
-    at(step + 2, work.core_step)
-    at(step + 1, work.load_step)
+        for r in (0, 1):
+            work.chip_step(FFN_TILE, r, r)
+            work.core_step(FFN_TILE, r + 2, r + 2)
+            work.load_step(FFN_TILE, r + 1, r + 1)
+
+    at(step - 4, work.last_step)
+    at(step - 3, work.relay_step)
+    at(step - 2, work.square_step)
+    at(step, work.corner_step)
+    at(step + 2, work.chip_step)
+    at(step + 3, work.load_step)
+
+    @pl.when(step == 0)
+    def _():
+        turned = merge(small_ref[..., 0:SMALL]).astype(F32).T
+        gains[0:1, :] = turned[16:17, :]
+        gains[1:2, :] = turned[17:18, :]
+
+        def back(rows, total):
+            mid = middle_ref[rows, :]
+            scale = lax.rsqrt(jnp.mean(mid * mid, axis=1, keepdims=True) + epsilon)
+            normed = mid * scale
+            grad = nm_sum_ref[rows, :]
+            d_normed = grad * gains[1:2, :]
+            d_mid = scale * (d_normed - normed * jnp.mean(d_normed * normed, axis=1, keepdims=True))
+            d_mid = d_mid + cot_ref[rows, :].astype(F32)
+            grad_mid_ref[rows, :] = d_mid
+            gb_ref[rows, :] = d_mid.astype(BF16)
+            gbt_ref[:, rows] = d_mid.T.astype(BF16)
+            return total + jnp.sum(grad * normed, axis=0, keepdims=True)
+
+        gains[2:3, :] = row_sums(tokens, back, gains.shape[1])
 
     @pl.when((step < 2 * HEADS) & (step % 2 == 0))
     def _():
@@ -816,9 +963,7 @@
 
     @pl.when(step == 2 * HEADS - 1)
     def _():
-        small = merge(small_ref[:, :, :, 0:SMALL])
-        turned = small.astype(F32).T
-        gain1 = turned[16:17, :]
+        small = merge(small_ref[..., 0:SMALL])
         lanes = lane_index((SEQ, 128))
         padded = jnp.concatenate([drows[...], jnp.zeros((120, tokens), F32)], axis=0).T
         d_logs = jnp.zeros((1, 128), F32)
@@ -837,44 +982,41 @@
             [d_logs, d_bias, dgain[0:1, :128], dgain[0:1, 128:], jnp.zeros((4, 128), F32)], axis=0
         )
         gxn[...] += lax.dot_general(d_logits, small, (NT, ((), ())), preferred_element_type=F32)
-        drows[...] = jnp.zeros_like(drows)
-        d_gain1 = [jnp.zeros((1, gxn.shape[1]), F32)]
 
         def back(at_rows, total):
             x = x_ref[at_rows, :].astype(F32)
             scale = lax.rsqrt(jnp.mean(x * x, axis=1, keepdims=True) + epsilon)
             normed = x * scale
             grad = gxn[at_rows, :]
-            d_normed = grad * gain1
+            d_normed = grad * gains[0:1, :]
             d_x = scale * (d_normed - normed * jnp.mean(d_normed * normed, axis=1, keepdims=True))
             input_grad_ref[at_rows, :] = d_x + grad_mid_ref[at_rows, :]
             return total + jnp.sum(grad * normed, axis=0, keepdims=True)
 
-        total = lax.fori_loop(
-            0, tokens // 128, lambda i, t: back(pl.ds(pl.multiple_of(i * 128, 128), 128), t), d_gain1[0]
-        )
+        total = row_sums(tokens, back, gxn.shape[1])
         line = lax.broadcasted_iota(jnp.int32, (128, total.shape[1]), 0)
-        gains = jnp.where(line == 16, total, jnp.where(line == 17, d_gain2_ref[0:1, :], 0.0))
-        own = jnp.dot(xnt_ref[...], d_logits, preferred_element_type=F32) + gains.T
+        lines = jnp.where(line == 16, total, jnp.where(line == 17, gains[2:3, :], 0.0))
+        own = jnp.dot(xnt_ref[...], d_logits, preferred_element_type=F32) + lines.T
         d_small[:, :, :, :, 0:SMALL] = own.astype(BF16).reshape(d_small.shape[:4] + (SMALL,))
 
-    for number in range(5):
+    at(step + 4, work.core_step)
+    for number in range(len(Total.bits) + 1):
         pl.when(step == 2 * HEADS + number)(lambda number=number: small_sum.step(number))
 
 
-def backward(planes, dwf, gb, gbt, xnt, w, proj, mixed, inv, upd, core, small, cols, seq_rows, logs, factor, gain, x,
-             grad_mid, d_gain2):
-    tokens, width = gb.shape
-    rows = small.shape[2]
+def backward(planes, dwf, middle, nm_sum, cot, xnt, w, proj, mixed, inv, upd, core, small, cols, seq_rows, logs, factor,
+             gain, x):
+    tokens, width = middle.shape
+    rows = small.shape[4]
     tiles = dwf.shape[1] // (3 * TILE)
-    chunks = tiles + HEADS + 1
+    chunks = FIRST + 2 * HEADS
+    assert tiles == FIRST + HEADS - 1
     hbm = pl.BlockSpec(memory_space=pl.ANY)
     head = head_step
     save = pl.BlockSpec((1, tokens, SEQ), lambda i: (head(i), 0, 0))
     shape = jax.ShapeDtypeStruct
     widest = HEAD_COLS + DV
     depth = Scatter.depths
-    kinds = 3 + planes
     outs = [
         ((tokens, width), F32),
         ((rows, HEADS * HEAD_COLS), F32),
@@ -886,23 +1028,28 @@
     ]
     return pl.pallas_call(
         partial(backward_body, planes, tiles, chunks),
-        grid=(chunks + 3 * LAG,),
+        grid=(chunks + 4,),
         in_specs=[
             hbm,
             once((tokens, width)),
+            once((tokens, width)),
+            once((tokens, width)),
             once((width, tokens)),
-            once((width, tokens)),
-            pl.BlockSpec((planes, 8, rows, widest), lambda i: (0, 0, 0, head(i))),
+            pl.BlockSpec((planes, 2, 2, 2, rows, widest), lambda i: (0, 0, 0, 0, 0, head(i))),
             pl.BlockSpec((tokens, HEAD_COLS), lambda i: (0, head(i))),
             pl.BlockSpec((tokens, DV), lambda i: (0, head(i))),
             save,
             save,
             save,
         ]
-        + [once(a.shape) for a in (small, cols, seq_rows, logs, factor, gain, x, grad_mid, d_gain2)],
+        + [once(a.shape) for a in (small, cols, seq_rows, logs, factor, gain, x)],
         out_specs=[once(o[0]) for o in outs],
         out_shape=[shape(*o) for o in outs],
         scratch_shapes=[
+            pltpu.VMEM((tokens, width), BF16),
+            pltpu.VMEM((width, tokens), BF16),
+            pltpu.VMEM((tokens, width), F32),
+            pltpu.VMEM((8, width), F32),
             pltpu.VMEM((2, planes, 4, 2, rows, widest), BF16),
             pltpu.VMEM((planes, 4, 2, rows, 2 * SMALL), BF16),
             pltpu.VMEM((tokens, width), F32),
@@ -911,28 +1058,30 @@
             pltpu.VMEM((8, DV), F32),
             pltpu.VMEM((tokens, HEAD_COLS), BF16),
             pltpu.VMEM((8, 128), F32),
-            pltpu.VMEM((depth["core"], planes, 4, rows, widest), BF16),
-            pltpu.VMEM((depth["keep"], planes, 4, rows, 3 * TILE), BF16),
-            pltpu.VMEM((depth["sums"], planes, 4, rows, widest), BF16),
-            pltpu.VMEM((depth["x"], planes, rows, widest), BF16),
-            pltpu.VMEM((depth["y"], planes, rows, widest), BF16),
-            pltpu.VMEM((depth["xy"], planes, rows, widest), BF16),
-            pltpu.VMEM((depth["z"], planes - 1, rows, widest), BF16),
-            pltpu.VMEM((3 + planes, 8, 128), F32),
-            pltpu.VMEM((4, 8, 128), F32),
+            pltpu.VMEM((depth[B_CORE], planes, 4, rows, widest), BF16),
+            pltpu.VMEM((depth[B_KEEP], planes, 4, rows, 3 * TILE), BF16),
+            pltpu.VMEM((depth[B_SUMS], planes, 4, rows, widest), BF16),
+            pltpu.VMEM((depth[B_XY], planes, rows, HEAD_COLS), BF16),
+            pltpu.VMEM((depth[B_X], planes, rows, HEAD_COLS), BF16),
+            pltpu.VMEM((depth[B_Y], planes, rows, HEAD_COLS), BF16),
+            pltpu.VMEM((depth[B_Z], 3, rows, HEAD_COLS), BF16),
+            pltpu.VMEM((depth[B_TWO_Z], 3, 4, rows, DV), BF16),
+            pltpu.VMEM((depth[B_TWO], 3, rows, DV), BF16),
+            pltpu.VMEM((len(Total.bits), 8, 128), F32),
+            pltpu.VMEM((len(Total.bits), 8, 128), F32),
             pltpu.SemaphoreType.DMA((chunks,)),
-            pltpu.SemaphoreType.DMA((chunks, kinds)),
-            pltpu.SemaphoreType.DMA((chunks, kinds)),
-            pltpu.SemaphoreType.DMA((2 + planes,)),
-            pltpu.SemaphoreType.DMA((2 + planes,)),
+            pltpu.SemaphoreType.DMA((chunks, Scatter.copies)),
+            pltpu.SemaphoreType.DMA((chunks, Scatter.copies)),
+            pltpu.SemaphoreType.DMA((len(Total.bits),)),
+            pltpu.SemaphoreType.DMA((len(Total.bits),)),
         ],
         compiler_params=pltpu.CompilerParams(
             collective_id=1, has_side_effects=True, vmem_limit_bytes=63 * MIB
         ),
         name="backward",
     )(
-        dwf.reshape(planes, 4, 2, rows, dwf.shape[1]), gb, gbt, xnt, w, proj, mixed, inv, upd, core, small, cols,
-        seq_rows, logs, factor, gain, x, grad_mid, d_gain2,
+        dwf.reshape(planes, 4, 2, rows, dwf.shape[1]), middle, nm_sum, cot, xnt, w, proj, mixed, inv, upd, core, small,
+        cols, seq_rows, logs, factor, gain, x,
     )
 
 
@@ -1360,11 +1509,11 @@
 
     (
         _, full_heads, _, small, xnt, cols, seq_rows, logs, factor, proj, mixed, inverse, update, core, dwf,
-        output, grad_mid, branch, brancht, d_gain2,
+        output, middle, nm_sum,
     ) = forward(planes, [shard_small, shard_heads, shard_tiles], tokens, cotangent, aux, seg_rows, consts, gain)
     input_grad, own_mixer, own_out, own_ffn, own_down, own_small, shared = backward(
-        planes, dwf, branch, brancht, xnt, full_heads, proj, mixed, inverse, update, core, small, cols, seq_rows, logs,
-        factor, gain, tokens, grad_mid, d_gain2,
+        planes, dwf, middle, nm_sum, cotangent, xnt, full_heads, proj, mixed, inverse, update, core, small, cols,
+        seq_rows, logs, factor, gain, tokens,
     )
     return (
         output,

time: 428 us -> 356 us (0.83)
  Pallas kernels: 398 us -> 327 us
    pallas_call x1, Pallas kernels: 220 us -> 173 us  [forward(): pl.pallas_call(partial(forward_body, planes, tiles), grid=(chunks,), in_s...]
    pallas_call x1, Pallas kernels: 178 us -> 154 us  [backward(): pl.pallas_call(partial(backward_body, planes, tiles, chunks), grid=(chunk...]
where the time goes in v3:
time: 356 us; the launch traced here: 355 us
  Pallas kernels  327 us (92%)
  local copies, waits for them, and re-layouts  18.4 us (5%)
  other arithmetic  9.09 us (3%)
    pallas_call x1, Pallas kernels, forward(): pl.pallas_call(partial(forward_body, planes, tiles), grid=(chunks,), in_s...  173 us
    pallas_call x1, Pallas kernels, backward(): pl.pallas_call(partial(backward_body, planes, tiles, chunks), grid=(chunk...  154 us
    unnamed x33, local copies, waits for them, and re-layouts  10 us

profile of v3, /device:TPU:0, one launch (start us, length us, event | category | flops | bytes accessed | tf_op | source)
XLA Modules:
  0.0 355.1 jit_solution(4426617611107902653)
XLA Ops:
  0.7 0.7 convert_bitcast_fusion.2
  2.7 0.7 convert_element_type.41
  3.4 0.7 convert_element_type.46
  4.1 1.3 select_maximum_fusion.consts_ref
  5.3 0.7 convert_element_type.38
  6.1 0.9 fusion.17
  8.6 1.0 convert_element_type.43
  9.6 1.0 convert_bitcast_fusion
  10.9 0.7 pad.33.aux_ref
  12.0 1.0 copy.55
  13.3 1.1 copy.54
  14.4 172.6 %forward.1 = (bf16[4,2,2,2,32,256]{5,4,3,2,1,0:T(8,128)(2,1)}, bf16[4,2,2,2,32,8192]{5,4,3,2,1,0:T(8,128)(2,1)}, bf16[4,2,2,2,32,8448]{5,4,3,2,1,0:T(8,128)(2,1)...) custom-call(bf16[32,256]{1,0:T(8,128)(2,1)} %fusion.1.shard_small, ...), custom_call_target="tpu_custom_call" | custom-call | tf_op jit(solution)/shard_map/forward/pallas_call | solution.py:743
  187.0 154.1 %backward.1 = (f32[512,1024]{1,0:T(8,128)}, f32[32,6144]{1,0:T(8,128)}, f32[32,2048]{1,0:T(8,128)}, f32[32,5632]{1,0:T(8,128)}, f32[32,2816]{1,0:T(8,128)}, /*index=5*/f32[32,256]{1,0:T(8,128)}, f32[8,128]{1,0:T(8,128)}) custom-call(bf16[4,4,2,32,8448]{4,3,2,1,0:T(8,128)(2,1)} %bitcast.43, f32[512,1024]{1,0:T(8,128)} %get-tuple-element.38.middle_ref, ...), custom_call_target="tpu_custom_call" | custom-call | tf_op jit(solution)/shard_map/backward/pallas_call | solution.py:1029
  341.2 1.4 slice_bitcast_fusion.2
  342.6 1.3 slice_bitcast_fusion.3
  343.8 1.5 slice_reduce_fusion
  345.3 1.3 slice.59
  346.6 0.7 slice.58
  348.0 2.3 copy.66
  350.2 1.3 copy.67
  351.9 0.9 copy.68
  352.8 0.7 copy.69
  353.5 0.9 copy.70
  354.4 0.7 copy.71
  (45 shorter events, 4.9 us)
Async XLA Ops:
  0.6 10.9 %copy-start.3 = (f32[32,5632]{1,0:T(8,128)S(1)}, f32[32,5632]{1,0:T(8,128)}, u32[]{:S(2)}) copy-start(f32[32,5632]{1,0:T(8,128)} %param.26) | copy-start | bytes 2162692
  11.6 1.4 copy-start.1
  341.2 9.1 %copy-start = (f32[512,1024]{1,0:T(8,128)S(1)}, f32[512,1024]{1,0:T(8,128)}, u32[]{:S(2)}) copy-start(f32[512,1024]{1,0:T(8,128)} %get-tuple-element.138) | copy-start | bytes 6291460
  350.2 1.7 copy-start.2
  350.2 2.6 copy-start.6
  351.9 1.6 copy-start.4
  351.9 2.5 copy-start.5

commit v4 on v3

--- a/solution.py
+++ b/solution.py
@@ -55,19 +55,29 @@
 
 
 def unit_inverses(couplings):
-    size = couplings[0].shape[0]
-    rows, cols = grid_of(size)
+    half = couplings[0].shape[0] // 2
+    rows, cols = grid_of(half)
     apart = rows ^ cols
     eye = jnp.where(apart == 0, 1.0, 0.0)
-    lows = [a.astype(BF16) for a in couplings]
-    inverses = [eye - jnp.where(apart < 2, a, 0.0) for a in couplings]
+    corners = [a[s : s + half, s : s + half] for a in couplings for s in (0, half)]
+    lows = [a.astype(BF16) for a in corners]
+    inverses = [eye - jnp.where(apart < 2, a, 0.0) for a in corners]
+    rounded = [inv.astype(BF16) for inv in inverses]
     block = 2
-    while block < size:
+    while block < half:
         here = jnp.where((apart >= block) & (apart < 2 * block), 1.0, 0.0).astype(BF16)
-        firsts = [dot1(low * here, inv, NN) for low, inv in zip(lows, inverses)]
-        inverses = [inv - dot1(inv, first, NN) for inv, first in zip(inverses, firsts)]
+        firsts = [dot1(low * here, inv, NN) for low, inv in zip(lows, rounded)]
+        added = [dot1(inv, first, NN) for inv, first in zip(rounded, firsts)]
+        inverses = [inv - new for inv, new in zip(inverses, added)]
+        rounded = [inv - new.astype(BF16) for inv, new in zip(rounded, added)]
         block *= 2
-    return inverses
+    results = []
+    for i, a in enumerate(couplings):
+        first, second = inverses[2 * i], inverses[2 * i + 1]
+        below = -dot1(rounded[2 * i + 1], dot1(a[half:, :half], rounded[2 * i], NN), NN)
+        top = jnp.concatenate([first, jnp.zeros_like(first)], axis=1)
+        results.append(jnp.concatenate([top, jnp.concatenate([below, second], axis=1)], axis=0))
+    return results
 
 
 def pick_lane(columns, lane):
@@ -111,14 +121,13 @@
     return number + bit - 2 * bit * ((number // bit) % 2)
 
 
-def enter():
-    me = lax.axis_index("dp")
+def enter(me, before=lambda: None):
     barrier = pltpu.get_barrier_semaphore()
     partners = [flip(me, bit) for bit in (1, 2, 4, 8, 16)]
     for other in partners:
         pl.semaphore_signal(barrier, inc=1, device_id=(other,), device_id_type=MESH)
+    before()
     pl.semaphore_wait(barrier, len(partners))
-    return me
 
 
 def span(k, width, start, size):
@@ -465,8 +474,8 @@
 class Total:
     bits = (1, 2, 4, 8, 16)
 
-    def __init__(self, me, value_ref, out_ref, got, stage, send_sem, recv_sem):
-        self.me, self.value_ref, self.out_ref = me, value_ref, out_ref
+    def __init__(self, me, value_ref, store, got, stage, send_sem, recv_sem):
+        self.me, self.value_ref, self.store = me, value_ref, store
         self.got, self.stage, self.send_sem, self.recv_sem = got, stage, send_sem, recv_sem
 
     def copy(self, number):
@@ -483,7 +492,7 @@
             self.stage[number] = value
             self.copy(number).start()
         else:
-            self.out_ref[...] = value
+            self.store(value)
             for number in range(last):
                 self.copy(number).wait_send()
 
@@ -532,10 +541,12 @@
 
 def forward_body(
     planes, tiles,
-    shard_small, shard_heads, shard_tiles, x_ref, cot_ref, aux_ref, seg_ref, consts_ref, gain_ref,
+    mixer_in_ref, mixer_out_ref, ffn_in_ref, ffn_out_ref, decay_in_ref, gain1_ref, gain2_ref, conv_ref,
+    x_ref, cot_ref, seg_ref, log_ref, bias_ref, gain_ref,
     full_small, full_heads, full_tiles, small_ref, xnt_ref, cols_ref, rows_ref, logs_ref, factor_ref,
     proj_ref, mixed_ref, inv_ref, upd_ref, core_ref, dw_ref,
     output_ref, middle, nm_sum,
+    shard_small, shard_heads, shard_tiles, turn, consts_ref,
     w_buf, xn, cott, nm, nmt, out_sum, gains, copy_sem, w_sem, local_sem, send_sem, recv_sem,
 ):
     step = pl.program_id(0)
@@ -553,10 +564,17 @@
         pl.when((chunk >= 0) & (chunk < HEADS))(lambda: act(HEAD, chunk))
         pl.when((chunk >= HEADS) & (chunk < chunks))(lambda: act(FFN_TILE, chunk - HEADS))
 
-    def weights(kind, k, slot):
+    def weights(kind, k, slot, plane=None):
         full, width = kinds[kind][1], SHAPES[kind][0]
+        source = full.at[:, :, :, :, :, span(k, width, 0, width)]
         place = w_buf.at[slot, :, :, :, :, :, pl.ds(0, width)]
-        return pltpu.make_async_copy(full.at[:, :, :, :, :, span(k, width, 0, width)], place, w_sem.at[slot])
+        if plane is not None:
+            source, place = source.at[plane], place.at[plane]
+        return pltpu.make_async_copy(source, place, w_sem.at[slot])
+
+    def load_weights(kind, k, slot):
+        for plane in range(planes):
+            weights(kind, k, slot, plane).start()
 
     ahead = ((6, work.start), (5, work.relay), (4, work.square), (2, work.corner), (1, work.across))
 
@@ -569,13 +587,46 @@
         for lead, act in ahead[:3]:
             at(step + lead, act)
         at(step + 1, work.complete)
-        at(step + 1, lambda kind, k: weights(kind, k, (step + 1) % 2).start())
+        at(step + 1, lambda kind, k: load_weights(kind, k, (step + 1) % 2))
+
+    def pack_heads():
+        turn[...] = jnp.zeros_like(turn)
+        turn[0:16, 0 : conv_ref.shape[1] // 4] = decay_in_ref[...]
+        turn[16:17, 0 : conv_ref.shape[1] // 4] = gain1_ref[...]
+        turn[17:18, 0 : conv_ref.shape[1] // 4] = gain2_ref[...]
+        rows = shard_small.shape[0]
+        shard_small[:, 0:SMALL] = turn[...].T[0:rows].astype(BF16)
+        taps = jnp.concatenate([conv_ref[...], jnp.zeros((rows - 4, SMALL), F32)], axis=0)
+        shard_small[:, SMALL:] = taps.astype(BF16)
+        for h in range(HEADS):
+            at_col = h * (HEAD_COLS + DV)
+            key, val = HEADS * DK, HEADS * DV
+            for ref, start, size in (
+                (mixer_in_ref, h * DK, DK),
+                (mixer_in_ref, key + h * DK, DK),
+                (mixer_in_ref, 2 * key + h * DV, DV),
+                (mixer_in_ref, 2 * key + val + h * DV, DV),
+                (mixer_out_ref, h * DV, DV),
+            ):
+                shard_heads[:, at_col : at_col + size] = ref[:, start : start + size].astype(BF16)
+                at_col += size
+
+    def pack_tiles():
+        for t in range(tiles):
+            at_col = t * 3 * TILE
+            for ref, start in ((ffn_in_ref, t * TILE), (ffn_in_ref, (tiles + t) * TILE), (ffn_out_ref, t * TILE)):
+                shard_tiles[:, at_col : at_col + TILE] = ref[:, start : start + TILE].astype(BF16)
+                at_col += TILE
 
     @pl.when(step == 0)
     def _():
-        enter()
+        enter(me, pack_heads)
         work.start(SMALLS, 0)
         early(-6)
+        pack_tiles()
+        consts_ref[...] = jnp.zeros_like(consts_ref)
+        consts_ref[0:1, 0:HEADS] = -jnp.exp(log_ref[...])
+        consts_ref[1:2, 0:HEADS] = bias_ref[...]
 
         def prepare(rows):
             middle[rows, :] = x_ref[rows, :].astype(F32)
@@ -619,18 +670,23 @@
         factor_ref[...] = jnp.where(
             lanes < 8, decay_scale * sigmoid(shifted), jnp.where(lanes < 16, rate * (1.0 - rate), 0.0)
         )
+        seg_row = jnp.broadcast_to(seg_ref[...].astype(F32), (128, tokens))
+        segment = seg_row.T
+        rows_ref[8:16, :] = seg_row[0:8]
+        inside = lax.broadcasted_iota(jnp.int32, segment.shape, 0) % SEQ
+        aux = segment
+        for back in (1, 2, 3):
+            linked = (pltpu.roll(segment, back, 0) == segment) & (inside >= back)
+            aux = jnp.where(lanes == 15 + back, jnp.where(linked, 1.0, 0.0), aux)
         for start in range(0, tokens, SEQ):
             part = slice(start, start + SEQ)
             cum = triangle_sum(log_decay[part], NN)
-            cols_ref[part, :] = jnp.where(
-                lanes[part] < 8, cum, jnp.where(lanes[part] < 16, rate[part], aux_ref[part, :])
-            )
+            cols_ref[part, :] = jnp.where(lanes[part] < 8, cum, jnp.where(lanes[part] < 16, rate[part], aux[part]))
             rows_ref[0:8, part] = cum.T[0:8]
-        rows_ref[8:16, :] = seg_ref[...]
         early(-1)
         work.finish(SMALLS, 0)
         work.complete(HEAD, 0)
-        weights(HEAD, 0, 0).start()
+        load_weights(HEAD, 0, 0)
 
     for lead, act in ahead[3:]:
         at(step + lead, act)
@@ -710,16 +766,17 @@
     return pl.BlockSpec(shape, lambda i: (0,) * len(shape), pipeline_mode=pl.Buffered(1))
 
 
-def forward(planes, shards, x, cot, aux, seg_rows, consts, gain):
-    rows, tokens, width = shards[0].shape[0], *x.shape
-    tiles = shards[2].shape[1] // (3 * TILE)
+def forward(planes, masters, x, cot, *others):
+    rows, tokens, width = masters[0].shape[0], *x.shape
+    tiles = masters[3].shape[1] // TILE
     chunks = HEADS + tiles
+    widths = (2 * SMALL, HEADS * (HEAD_COLS + DV), tiles * 3 * TILE)
     hbm = pl.BlockSpec(memory_space=pl.ANY)
     head = lambda i: jnp.minimum(i, HEADS - 1)
     tile = lambda i: jnp.maximum(i - HEADS, 0)
     save = pl.BlockSpec((1, tokens, SEQ), lambda i: (head(i), 0, 0))
     shape = jax.ShapeDtypeStruct
-    whole = [((planes, 2, 2, 2, rows, s.shape[1]), BF16) for s in shards]
+    whole = [((planes, 2, 2, 2, rows, w), BF16) for w in widths]
     outs = [
         (hbm, *whole[0]),
         (hbm, *whole[1]),
@@ -743,10 +800,13 @@
     return pl.pallas_call(
         partial(forward_body, planes, tiles),
         grid=(chunks,),
-        in_specs=[hbm, hbm, hbm] + [once(a.shape) for a in (x, cot, aux, seg_rows, consts, gain)],
+        in_specs=[once(a.shape) for a in (*masters, x, cot, *others)],
         out_specs=[o[0] for o in outs],
         out_shape=[shape(o[1], o[2]) for o in outs],
-        scratch_shapes=[
+        scratch_shapes=[pltpu.VMEM((rows, w), BF16) for w in widths]
+        + [
+            pltpu.VMEM((128, 128), F32),
+            pltpu.VMEM((8, 128), F32),
             pltpu.VMEM((2, planes, 2, 2, 2, rows, HEAD_COLS + DV), BF16),
             pltpu.VMEM((tokens, width), BF16),
             pltpu.VMEM((width, tokens), BF16),
@@ -764,7 +824,7 @@
             collective_id=0, has_side_effects=True, vmem_limit_bytes=60 * MIB
         ),
         name="forward",
-    )(*shards, x, cot, aux, seg_rows, consts, gain)
+    )(*masters, x, cot, *others)
 
 
 FIRST = 4
@@ -785,14 +845,14 @@
     planes, tiles, total_chunks,
     dwf_ref, middle_ref, nm_sum_ref, cot_ref, xnt_ref, w_ref, proj_ref, mixed_ref, inv_ref, upd_ref, core_ref,
     small_ref, cols_ref, rows_ref, logs_ref, factor_ref, gain_ref, x_ref,
-    input_grad_ref, own_mixer, own_out, own_ffn, own_down, own_small, shared_ref,
-    gb_ref, gbt_ref, grad_mid_ref, gains, dw, d_small, gxn, dcols, drows, dgain, dproj, value_ref,
+    input_grad_ref, own_gain1, own_mixer, own_decay, own_conv, own_log, own_bias, own_gain, own_out, own_gain2, own_ffn,
+    own_down, gb_ref, gbt_ref, grad_mid_ref, gains, dw, d_small, gxn, dcols, drows, dgain, dproj, value_ref,
     *scratch,
 ):
     *buffers, got, stage, local_sem, send_sem, recv_sem, total_send, total_recv = scratch
     step = pl.program_id(0)
     tokens = middle_ref.shape[0]
-    rows = own_small.shape[0]
+    rows = own_mixer.shape[0]
     hidden = tiles * TILE
     me = lax.axis_index("dp")
 
@@ -816,7 +876,11 @@
             ref[:, pl.ds(pl.multiple_of(start, 128), width)] = total[:, source : source + width]
 
         if kind == SMALLS:
-            own_small[...] = total
+            turned = jnp.concatenate([total[:, :SMALL], jnp.zeros((SMALL - rows, SMALL), F32)], axis=0).T
+            own_decay[...] = turned[0:16, 0:rows]
+            own_gain1[...] = turned[16:17, 0:rows]
+            own_gain2[...] = turned[17:18, 0:rows]
+            own_conv[...] = total[0:4, SMALL:]
         elif kind == HEAD:
             put(own_mixer, k * DK, 0, DK)
             put(own_mixer, HEADS * DK + k * DK, DK, DK)
@@ -829,7 +893,12 @@
             put(own_down, k * TILE, 2 * TILE, TILE)
 
     work = Scatter(me, kinds, store, *buffers, local_sem, send_sem, recv_sem)
-    small_sum = Total(me, value_ref, shared_ref, got, stage, total_send, total_recv)
+    def share(value):
+        own_log[...] = value[0:1, 0:HEADS]
+        own_bias[...] = value[1:2, 0:HEADS]
+        own_gain[...] = jnp.concatenate([value[2:3], value[3:4]], axis=1)
+
+    small_sum = Total(me, value_ref, share, got, stage, total_send, total_recv)
 
     last = total_chunks - 1
 
@@ -844,7 +913,7 @@
 
     @pl.when(step == 0)
     def _():
-        enter()
+        enter(me)
         work.core_step(FFN_TILE, 0, 0)
         work.core_step(FFN_TILE, 1, 1)
         work.load_step(FFN_TILE, 0, 0)
@@ -1019,12 +1088,17 @@
     depth = Scatter.depths
     outs = [
         ((tokens, width), F32),
+        ((1, rows), F32),
         ((rows, HEADS * HEAD_COLS), F32),
+        ((16, rows), F32),
+        ((4, SMALL), F32),
+        ((1, HEADS), F32),
+        ((1, HEADS), F32),
+        ((1, DV), F32),
         ((rows, HEADS * DV), F32),
+        ((1, rows), F32),
         ((rows, 2 * tiles * TILE), F32),
         ((rows, tiles * TILE), F32),
-        ((rows, 2 * SMALL), F32),
-        ((8, 128), F32),
     ]
     return pl.pallas_call(
         partial(backward_body, planes, tiles, chunks),
@@ -1085,6 +1159,32 @@
     )
 
 
+def hand_over_body(count, *refs):
+    for source, target in zip(refs[:count], refs[count:]):
+        target[...] = source[...]
+
+
+def hand_over(arrays, steps=4):
+    specs = []
+    for a in arrays:
+        rows, cols = a.shape
+        if rows % (32 * steps) == 0:
+            specs.append(pl.BlockSpec((rows // steps, cols), lambda i: (i, 0)))
+        elif cols % (128 * steps) == 0:
+            specs.append(pl.BlockSpec((rows, cols // steps), lambda i: (0, i)))
+        else:
+            specs.append(pl.BlockSpec((rows, cols), lambda i: (0, 0)))
+    return pl.pallas_call(
+        partial(hand_over_body, len(arrays)),
+        grid=(steps,),
+        in_specs=specs,
+        out_specs=specs,
+        out_shape=[jax.ShapeDtypeStruct(a.shape, a.dtype) for a in arrays],
+        compiler_params=pltpu.CompilerParams(vmem_limit_bytes=60 * MIB),
+        name="hand_over",
+    )(*arrays)
+
+
 def mixer_fwd_body(xn_ref, w_ref, taps_ref, cols_ref, rows_ref, gain_ref, proj_ref, mixed_ref, inv_ref, upd_ref, core_ref):
     head = pl.program_id(0)
     tokens = xn_ref.shape[0]
@@ -1479,56 +1579,28 @@
     devices, tokens, segment_ids, cotangent, norm1_gain, mixer_in, decay_in, conv_weight, decay_log, decay_bias,
     head_gain, mixer_out, norm2_gain, ffn_in, ffn_out,
 ):
-    rows = decay_in.shape[0]
-    count = tokens.shape[0]
-    hidden = ffn_out.shape[0]
-    tiles = hidden // TILE
     planes = devices // 8
-    low = lambda v: v.astype(BF16)
-    pad = lambda v, lanes: jnp.pad(v, ((0, 0), (0, lanes - v.shape[1])))
-
-    first = pad(jnp.concatenate([low(decay_in), low(norm1_gain)[:, None], low(norm2_gain)[:, None]], axis=1), SMALL)
-    second = jnp.pad(low(conv_weight), ((0, rows - 4), (0, 0)))
-    shard_small = jnp.concatenate([first, second], axis=1)
-    shard_heads = by_head(split_heads(low(mixer_in)) + [low(mixer_out).T])
-    ffn_low = low(ffn_in)
-    pieces = [ffn_low[:, :hidden], ffn_low[:, hidden:], low(ffn_out).T]
-    shard_tiles = jnp.concatenate([p.reshape(rows, tiles, TILE) for p in pieces], axis=2).reshape(rows, -1)
-
-    position = jnp.arange(count) % SEQ
-    keeps = [jnp.zeros((count, 16), F32)]
-    for back in (1, 2, 3):
-        earlier = jnp.pad(segment_ids[:-back], (back, 0), constant_values=-1)
-        keeps.append(((earlier == segment_ids) & (position >= back)).astype(F32)[:, None])
-    segment = segment_ids.astype(F32)
-    aux = pad(jnp.concatenate(keeps + [segment[:, None]], axis=1), 128)
-    seg_rows = jnp.broadcast_to(segment[None], (8, count))
-    lines = jnp.stack([-jnp.exp(decay_log), decay_bias])
-    consts = jnp.pad(lines, ((0, 6), (0, 128 - HEADS)))
     gain = head_gain[None]
-
+    masters = [
+        mixer_in, mixer_out.T, ffn_in, ffn_out.T, decay_in.T, norm1_gain[None], norm2_gain[None], conv_weight,
+    ]
     (
         _, full_heads, _, small, xnt, cols, seq_rows, logs, factor, proj, mixed, inverse, update, core, dwf,
         output, middle, nm_sum,
-    ) = forward(planes, [shard_small, shard_heads, shard_tiles], tokens, cotangent, aux, seg_rows, consts, gain)
-    input_grad, own_mixer, own_out, own_ffn, own_down, own_small, shared = backward(
+    ) = forward(
+        planes, masters, tokens, cotangent, segment_ids[None], decay_log[None], decay_bias[None], gain
+    )
+    results = backward(
         planes, dwf, middle, nm_sum, cotangent, xnt, full_heads, proj, mixed, inverse, update, core, small, cols,
         seq_rows, logs, factor, gain, tokens,
     )
+    (
+        output, input_grad, d_gain1, d_mixer_in, d_decay_in, d_conv, d_log, d_bias, d_gain, d_mixer_out, d_gain2, d_ffn_in,
+        d_ffn_out,
+    ) = hand_over([output, *results])
     return (
-        output,
-        input_grad,
-        own_small[:, 16],
-        own_mixer,
-        own_small[:, :16],
-        own_small[:4, SMALL:],
-        shared[0, :HEADS],
-        shared[1, :HEADS],
-        shared[2:4].reshape(-1),
-        own_out.T,
-        own_small[:, 17],
-        own_ffn,
-        own_down.T,
+        output, input_grad, d_gain1[0], d_mixer_in, d_decay_in.T, d_conv, d_log[0], d_bias[0], d_gain[0], d_mixer_out.T,
+        d_gain2[0], d_ffn_in, d_ffn_out.T,
     )
 
 

time: 356 us -> 332 us (0.933)
  local copies, waits for them, and re-layouts: 18.4 us -> 0 us
  other arithmetic: 9.09 us -> 0 us
  Pallas kernels: 327 us -> 331 us
    unnamed x33 -> x0, local copies, waits for them, and re-layouts: 10 us -> none
    pallas_call x0 -> x1, Pallas kernels: none -> 5.53 us  [hand_over(): pl.pallas_call(partial(hand_over_body, len(arrays)), grid=(steps,), in_sp...]
where the time goes in v4:
time: 332 us
  Pallas kernels  331 us (100%)
    pallas_call x1, Pallas kernels, forward(): pl.pallas_call(partial(forward_body, planes, tiles), grid=(chunks,), in_s...  173 us
    pallas_call x1, Pallas kernels, backward(): pl.pallas_call(partial(backward_body, planes, tiles, chunks), grid=(chunk...  153 us

profile of v4, /device:TPU:0, one launch (start us, length us, event | category | flops | bytes accessed | tf_op | source)
XLA Modules:
  0.0 331.8 jit_solution(18216135942058667542)
XLA Ops:
  0.6 172.5 %forward.1 = (bf16[4,2,2,2,32,256]{5,4,3,2,1,0:T(8,128)(2,1)}, bf16[4,2,2,2,32,8192]{5,4,3,2,1,0:T(8,128)(2,1)}, bf16[4,2,2,2,32,8448]{5,4,3,2,1,0:T(8,128)(2,1)...) custom-call(f32[32,6144]{1,0:T(8,128)} %mixer_in_ref.1, ...), custom_call_target="tpu_custom_call" | custom-call | tf_op jit(solution)/shard_map/forward/pallas_call | solution.py:800
  173.2 152.9 %backward.1 = (f32[512,1024]{1,0:T(8,128)}, f32[1,32]{1,0:T(1,128)}, f32[32,6144]{1,0:T(8,128)}, f32[16,32]{1,0:T(8,128)}, f32[4,128]{1,0:T(4,128)}, /*index=5*/...) custom-call(bf16[4,4,2,32,8448]{4,3,2,1,0:T(8,128)(2,1)} %bitcast.18, ...), custom_call_target="tpu_custom_call" | custom-call | tf_op jit(solution)/shard_map/backward/pallas_call | solution.py:1103
  326.1 5.5 %hand_over.1 = (bf16[512,1024]{1,0:T(8,128)(2,1)}, f32[512,1024]{1,0:T(8,128)}, f32[1,32]{1,0:T(1,128)}, f32[32,6144]{1,0:T(8,128)}, f32[16,32]{1,0:T(8,128)}, /...) custom-call(bf16[512,1024]{1,0:T(8,128)(2,1)} %get-tuple-element.54., ...), custom_call_target="tpu_custom_call" | custom-call | tf_op jit(solution)/shard_map/hand_over/pallas_call | solution.py:1177

commit v5 on v4

--- a/solution.py
+++ b/solution.py
@@ -275,7 +275,7 @@
 
 class Scatter:
     copies = 16
-    depths = {B_CORE: 4, B_KEEP: 2, B_SUMS: 6, B_XY: 4, B_X: 8, B_Y: 8, B_Z: 4, B_TWO_Z: 8, B_TWO: 4}
+    depths = {B_CORE: 4, B_KEEP: 2, B_SUMS: 8, B_XY: 4, B_X: 8, B_Y: 8, B_Z: 8, B_TWO_Z: 8, B_TWO: 8}
 
     def __init__(self, me, kinds, store, core, keep, sums, xy, x, y, z, two_z, two, local_sem, send_sem, recv_sem):
         self.me, self.kinds, self.store = me, kinds, store
@@ -542,10 +542,10 @@
 def forward_body(
     planes, tiles,
     mixer_in_ref, mixer_out_ref, ffn_in_ref, ffn_out_ref, decay_in_ref, gain1_ref, gain2_ref, conv_ref,
-    x_ref, cot_ref, seg_ref, log_ref, bias_ref, gain_ref,
-    full_small, full_heads, full_tiles, small_ref, xnt_ref, cols_ref, rows_ref, logs_ref, factor_ref,
-    proj_ref, mixed_ref, inv_ref, upd_ref, core_ref, dw_ref,
-    output_ref, middle, nm_sum,
+    x_in, cot_in, seg_ref, log_ref, bias_ref, gain_ref,
+    full_small, full_heads, full_tiles, small_out, xnt_out, cols_out, rows_out, logs_out, factor_out, middle_out,
+    proj_ref, mixed_ref, inv_ref, upd_ref, core_ref, dw_ref, output_ref, nm_sum,
+    small_ref, xnt_ref, cols_ref, rows_ref, logs_ref, factor_ref, middle, x_ref, cot_ref, load_sem, flush_sem,
     shard_small, shard_heads, shard_tiles, turn, consts_ref,
     w_buf, xn, cott, nm, nmt, out_sum, gains, copy_sem, w_sem, local_sem, send_sem, recv_sem,
 ):
@@ -576,20 +576,46 @@
         for plane in range(planes):
             weights(kind, k, slot, plane).start()
 
-    ahead = ((6, work.start), (5, work.relay), (4, work.square), (2, work.corner), (1, work.across))
+    def arrive(kind, k):
+        work.complete(kind, k)
+        load_weights(kind, k, k % 2 if isinstance(k, int) else (step + 1) % 2)
+
+    def arrive_early(kind, k):
+        pl.when(step + 1 != chunks - 1)(lambda: arrive(kind, k))
+
+    def arrive_late(kind, k):
+        pl.when(step + 1 == chunks - 1)(lambda: arrive(kind, k))
+
+    at_start = ((3, work.corner), (1, arrive_early))
+    at_middle = ((7, work.start), (6, work.relay), (5, work.square), (2, work.across))
 
     def early(step):
-        for lead, act in ahead:
+        for lead, act in sorted(at_start[:1] + at_middle + ((1, arrive),), key=lambda item: -item[0]):
             if step + lead >= 0:
                 act(HEAD, step + lead)
 
     def midway():
-        for lead, act in ahead[:3]:
+        for lead, act in at_middle:
             at(step + lead, act)
-        at(step + 1, work.complete)
-        at(step + 1, lambda kind, k: load_weights(kind, k, (step + 1) % 2))
+        at(step + 1, arrive_late)
+
+    loads = [
+        pltpu.make_async_copy(source, target, load_sem.at[i])
+        for i, (source, target) in enumerate(((x_in, x_ref), (cot_in, cot_ref)))
+    ]
+    flushes = [
+        pltpu.make_async_copy(source, target, flush_sem.at[i])
+        for i, (source, target) in enumerate(
+            (
+                (small_ref, small_out), (xnt_ref, xnt_out), (cols_ref, cols_out), (rows_ref, rows_out),
+                (logs_ref, logs_out), (factor_ref, factor_out), (middle, middle_out),
+            )
+        )
+    ]
 
     def pack_heads():
+        for copy in loads:
+            copy.start()
         turn[...] = jnp.zeros_like(turn)
         turn[0:16, 0 : conv_ref.shape[1] // 4] = decay_in_ref[...]
         turn[16:17, 0 : conv_ref.shape[1] // 4] = gain1_ref[...]
@@ -622,7 +648,7 @@
     def _():
         enter(me, pack_heads)
         work.start(SMALLS, 0)
-        early(-6)
+        early(-7)
         pack_tiles()
         consts_ref[...] = jnp.zeros_like(consts_ref)
         consts_ref[0:1, 0:HEADS] = -jnp.exp(log_ref[...])
@@ -632,16 +658,19 @@
             middle[rows, :] = x_ref[rows, :].astype(F32)
             cott[:, rows] = cot_ref[rows, :].astype(F32).T.astype(BF16)
 
+        for copy in loads:
+            copy.wait()
         row_blocks(tokens, prepare)
         work.relay(SMALLS, 0)
+        early(-6)
+        work.square(SMALLS, 0)
         early(-5)
-        work.square(SMALLS, 0)
+        work.corner(SMALLS, 0)
         early(-4)
-        work.corner(SMALLS, 0)
-        early(-3)
         work.across(SMALLS, 0)
         out_sum[...] = jnp.zeros_like(out_sum)
         nm_sum[...] = jnp.zeros_like(nm_sum)
+        early(-3)
         work.complete(SMALLS, 0)
         early(-2)
         copy = pltpu.make_async_copy(full_small, small_ref, copy_sem)
@@ -685,13 +714,16 @@
             rows_ref[0:8, part] = cum.T[0:8]
         early(-1)
         work.finish(SMALLS, 0)
-        work.complete(HEAD, 0)
-        load_weights(HEAD, 0, 0)
-
-    for lead, act in ahead[3:]:
+
+    for lead, act in at_start:
         at(step + lead, act)
     at(step, lambda kind, k: weights(kind, k, step % 2).wait())
     at(step - 1, work.finish)
+
+    @pl.when(step == 1)
+    def _():
+        for copy in flushes[:-1]:
+            copy.start()
 
     @pl.when(step < HEADS)
     def _():
@@ -733,6 +765,7 @@
             nm[rows, :] = normed.astype(BF16)
             nmt[:, rows] = normed.T.astype(BF16)
 
+        flushes[-1].start()
         row_blocks(tokens, norm)
 
     @pl.when(step >= HEADS)
@@ -760,6 +793,8 @@
 
         row_blocks(tokens, add)
         work.finish(FFN_TILE, tiles - 1)
+        for copy in flushes:
+            copy.wait()
 
 
 def once(shape):
@@ -781,12 +816,13 @@
         (hbm, *whole[0]),
         (hbm, *whole[1]),
         (hbm, *whole[2]),
-        (once(whole[0][0]), *whole[0]),
-        (once((width, tokens)), (width, tokens), BF16),
-        (once((tokens, 128)), (tokens, 128), F32),
-        (once((16, tokens)), (16, tokens), F32),
-        (once((tokens, 128)), (tokens, 128), F32),
-        (once((tokens, 128)), (tokens, 128), F32),
+        (hbm, *whole[0]),
+        (hbm, (width, tokens), BF16),
+        (hbm, (tokens, 128), F32),
+        (hbm, (16, tokens), F32),
+        (hbm, (tokens, 128), F32),
+        (hbm, (tokens, 128), F32),
+        (hbm, (tokens, width), F32),
         (pl.BlockSpec((tokens, HEAD_COLS), lambda i: (0, head(i))), (tokens, HEADS * HEAD_COLS), F32),
         (pl.BlockSpec((tokens, DV), lambda i: (0, head(i))), (tokens, HEADS * DV), BF16),
         (save, (HEADS, tokens, SEQ), BF16),
@@ -795,15 +831,21 @@
         (pl.BlockSpec((width, 3 * TILE), lambda i: (0, tile(i))), (width, tiles * 3 * TILE), BF16),
         (once((tokens, width)), (tokens, width), BF16),
         (once((tokens, width)), (tokens, width), F32),
-        (once((tokens, width)), (tokens, width), F32),
     ]
     return pl.pallas_call(
         partial(forward_body, planes, tiles),
         grid=(chunks,),
-        in_specs=[once(a.shape) for a in (*masters, x, cot, *others)],
+        in_specs=[once(a.shape) for a in masters] + [hbm, hbm] + [once(a.shape) for a in others],
         out_specs=[o[0] for o in outs],
         out_shape=[shape(o[1], o[2]) for o in outs],
-        scratch_shapes=[pltpu.VMEM((rows, w), BF16) for w in widths]
+        scratch_shapes=[pltpu.VMEM(o[1], o[2]) for o in outs[3:10]]
+        + [
+            pltpu.VMEM((tokens, width), BF16),
+            pltpu.VMEM((tokens, width), BF16),
+            pltpu.SemaphoreType.DMA((2,)),
+            pltpu.SemaphoreType.DMA((7,)),
+        ]
+        + [pltpu.VMEM((rows, w), BF16) for w in widths]
         + [
             pltpu.VMEM((128, 128), F32),
             pltpu.VMEM((8, 128), F32),
@@ -843,12 +885,14 @@
 
 def backward_body(
     planes, tiles, total_chunks,
-    dwf_ref, middle_ref, nm_sum_ref, cot_ref, xnt_ref, w_ref, proj_ref, mixed_ref, inv_ref, upd_ref, core_ref,
-    small_ref, cols_ref, rows_ref, logs_ref, factor_ref, gain_ref, x_ref,
-    input_grad_ref, own_gain1, own_mixer, own_decay, own_conv, own_log, own_bias, own_gain, own_out, own_gain2, own_ffn,
-    own_down, gb_ref, gbt_ref, grad_mid_ref, gains, dw, d_small, gxn, dcols, drows, dgain, dproj, value_ref,
-    *scratch,
+    dwf_ref, middle_in, nm_sum_in, cot_in, xnt_in, x_in, w_ref, proj_ref, mixed_ref, inv_ref, upd_ref, core_ref,
+    small_ref, cols_ref, rows_ref, logs_ref, factor_ref, gain_ref,
+    input_grad_out, own_gain1, own_mixer, own_decay, own_conv, own_log, own_bias, own_gain, own_out, own_gain2, own_ffn,
+    own_down,
+    middle_ref, nm_sum_ref, cot_ref, xnt_ref, x_ref, load_sem, flush_sem, gbt_ref, gains, dw, d_small, dcols, drows, dgain, dproj,
+    value_ref, *scratch,
 ):
+    gxn, grad_mid_ref, gb_ref = middle_ref, nm_sum_ref, cot_ref
     *buffers, got, stage, local_sem, send_sem, recv_sem, total_send, total_recv = scratch
     step = pl.program_id(0)
     tokens = middle_ref.shape[0]
@@ -911,24 +955,34 @@
         pl.when(is_head)(lambda: act(HEAD, r, (r - FIRST) // 2))
         pl.when(r == last)(lambda: act(SMALLS, r, 0))
 
+    loads = [
+        pltpu.make_async_copy(source, target, load_sem.at[i])
+        for i, (source, target) in enumerate(
+            (
+                (middle_in, middle_ref), (nm_sum_in, nm_sum_ref), (cot_in, cot_ref), (xnt_in, xnt_ref), (x_in, x_ref),
+            )
+        )
+    ]
+
     @pl.when(step == 0)
     def _():
         enter(me)
         work.core_step(FFN_TILE, 0, 0)
         work.core_step(FFN_TILE, 1, 1)
         work.load_step(FFN_TILE, 0, 0)
-        gxn[...] = jnp.zeros_like(gxn)
         dcols[...] = jnp.zeros_like(dcols)
         drows[...] = jnp.zeros_like(drows)
         dgain[...] = jnp.zeros_like(dgain)
         d_small[...] = jnp.zeros_like(d_small)
+        for copy in loads:
+            copy.start()
         for r in (0, 1):
             work.chip_step(FFN_TILE, r, r)
             work.core_step(FFN_TILE, r + 2, r + 2)
             work.load_step(FFN_TILE, r + 1, r + 1)
 
-    at(step - 4, work.last_step)
-    at(step - 3, work.relay_step)
+    at(step - 6, work.last_step)
+    at(step - 4, work.relay_step)
     at(step - 2, work.square_step)
     at(step, work.corner_step)
     at(step + 2, work.chip_step)
@@ -936,6 +990,8 @@
 
     @pl.when(step == 0)
     def _():
+        for copy in loads:
+            copy.wait()
         turned = merge(small_ref[..., 0:SMALL]).astype(F32).T
         gains[0:1, :] = turned[16:17, :]
         gains[1:2, :] = turned[17:18, :]
@@ -948,6 +1004,7 @@
             d_normed = grad * gains[1:2, :]
             d_mid = scale * (d_normed - normed * jnp.mean(d_normed * normed, axis=1, keepdims=True))
             d_mid = d_mid + cot_ref[rows, :].astype(F32)
+            gxn[rows, :] = jnp.zeros_like(mid)
             grad_mid_ref[rows, :] = d_mid
             gb_ref[rows, :] = d_mid.astype(BF16)
             gbt_ref[:, rows] = d_mid.T.astype(BF16)
@@ -1059,7 +1116,7 @@
             grad = gxn[at_rows, :]
             d_normed = grad * gains[0:1, :]
             d_x = scale * (d_normed - normed * jnp.mean(d_normed * normed, axis=1, keepdims=True))
-            input_grad_ref[at_rows, :] = d_x + grad_mid_ref[at_rows, :]
+            grad_mid_ref[at_rows, :] = d_x + grad_mid_ref[at_rows, :]
             return total + jnp.sum(grad * normed, axis=0, keepdims=True)
 
         total = row_sums(tokens, back, gxn.shape[1])
@@ -1067,6 +1124,10 @@
         lines = jnp.where(line == 16, total, jnp.where(line == 17, gains[2:3, :], 0.0))
         own = jnp.dot(xnt_ref[...], d_logits, preferred_element_type=F32) + lines.T
         d_small[:, :, :, :, 0:SMALL] = own.astype(BF16).reshape(d_small.shape[:4] + (SMALL,))
+
+    flush = pltpu.make_async_copy(grad_mid_ref, input_grad_out, flush_sem)
+    pl.when(step == 2 * HEADS)(flush.start)
+    pl.when(step == pl.num_programs(0) - 1)(flush.wait)
 
     at(step + 4, work.core_step)
     for number in range(len(Total.bits) + 1):
@@ -1102,13 +1163,14 @@
     ]
     return pl.pallas_call(
         partial(backward_body, planes, tiles, chunks),
-        grid=(chunks + 4,),
+        grid=(chunks + 6,),
         in_specs=[
             hbm,
-            once((tokens, width)),
-            once((tokens, width)),
-            once((tokens, width)),
-            once((width, tokens)),
+            hbm,
+            hbm,
+            hbm,
+            hbm,
+            hbm,
             pl.BlockSpec((planes, 2, 2, 2, rows, widest), lambda i: (0, 0, 0, 0, 0, head(i))),
             pl.BlockSpec((tokens, HEAD_COLS), lambda i: (0, head(i))),
             pl.BlockSpec((tokens, DV), lambda i: (0, head(i))),
@@ -1116,17 +1178,21 @@
             save,
             save,
         ]
-        + [once(a.shape) for a in (small, cols, seq_rows, logs, factor, gain, x)],
-        out_specs=[once(o[0]) for o in outs],
+        + [once(a.shape) for a in (small, cols, seq_rows, logs, factor, gain)],
+        out_specs=[hbm] + [once(o[0]) for o in outs[1:]],
         out_shape=[shape(*o) for o in outs],
         scratch_shapes=[
+            pltpu.VMEM((tokens, width), F32),
+            pltpu.VMEM((tokens, width), F32),
             pltpu.VMEM((tokens, width), BF16),
             pltpu.VMEM((width, tokens), BF16),
-            pltpu.VMEM((tokens, width), F32),
+            pltpu.VMEM((tokens, width), BF16),
+            pltpu.SemaphoreType.DMA((5,)),
+            pltpu.SemaphoreType.DMA,
+            pltpu.VMEM((width, tokens), BF16),
             pltpu.VMEM((8, width), F32),
             pltpu.VMEM((2, planes, 4, 2, rows, widest), BF16),
             pltpu.VMEM((planes, 4, 2, rows, 2 * SMALL), BF16),
-            pltpu.VMEM((tokens, width), F32),
             pltpu.VMEM((tokens, 128), F32),
             pltpu.VMEM((HEADS, tokens), F32),
             pltpu.VMEM((8, DV), F32),
@@ -1154,8 +1220,8 @@
         ),
         name="backward",
     )(
-        dwf.reshape(planes, 4, 2, rows, dwf.shape[1]), middle, nm_sum, cot, xnt, w, proj, mixed, inv, upd, core, small,
-        cols, seq_rows, logs, factor, gain, x,
+        dwf.reshape(planes, 4, 2, rows, dwf.shape[1]), middle, nm_sum, cot, xnt, x, w, proj, mixed, inv, upd, core, small,
+        cols, seq_rows, logs, factor, gain,
     )
 
 
@@ -1585,8 +1651,8 @@
         mixer_in, mixer_out.T, ffn_in, ffn_out.T, decay_in.T, norm1_gain[None], norm2_gain[None], conv_weight,
     ]
     (
-        _, full_heads, _, small, xnt, cols, seq_rows, logs, factor, proj, mixed, inverse, update, core, dwf,
-        output, middle, nm_sum,
+        _, full_heads, _, small, xnt, cols, seq_rows, logs, factor, middle, proj, mixed, inverse, update, core, dwf,
+        output, nm_sum,
     ) = forward(
         planes, masters, tokens, cotangent, segment_ids[None], decay_log[None], decay_bias[None], gain
     )

time: 332 us -> 315 us (0.949)
  Pallas kernels: 331 us -> 313 us
    pallas_call x1, Pallas kernels: 173 us -> 161 us  [forward(): pl.pallas_call(partial(forward_body, planes, tiles), grid=(chunks,), in_s...]
    pallas_call x1, Pallas kernels: 153 us -> 147 us  [backward(): pl.pallas_call(partial(backward_body, planes, tiles, chunks), grid=(chunk...]
where the time goes in v5:
time: 315 us; the launch traced here: 314 us
  Pallas kernels  313 us (99%)
    pallas_call x1, Pallas kernels, forward(): pl.pallas_call(partial(forward_body, planes, tiles), grid=(chunks,), in_s...  161 us
    pallas_call x1, Pallas kernels, backward(): pl.pallas_call(partial(backward_body, planes, tiles, chunks), grid=(chunk...  147 us

profile of v5, /device:TPU:0, one launch (start us, length us, event | category | flops | bytes accessed | tf_op | source)
XLA Modules:
  0.0 314.3 jit_solution(8485966880840513818)
XLA Ops:
  0.6 160.6 %forward.1 = (bf16[4,2,2,2,32,256]{5,4,3,2,1,0:T(8,128)(2,1)}, bf16[4,2,2,2,32,8192]{5,4,3,2,1,0:T(8,128)(2,1)}, bf16[4,2,2,2,32,8448]{5,4,3,2,1,0:T(8,128)(2,1)...) custom-call(f32[32,6144]{1,0:T(8,128)} %mixer_in_ref.1, ...), custom_call_target="tpu_custom_call" | custom-call | tf_op jit(solution)/shard_map/forward/pallas_call | solution.py:835
  161.2 147.3 %backward.1 = (f32[512,1024]{1,0:T(8,128)}, f32[1,32]{1,0:T(1,128)}, f32[32,6144]{1,0:T(8,128)}, f32[16,32]{1,0:T(8,128)}, f32[4,128]{1,0:T(4,128)}, /*index=5*/...) custom-call(bf16[4,4,2,32,8448]{4,3,2,1,0:T(8,128)(2,1)} %bitcast.18, ...), custom_call_target="tpu_custom_call" | custom-call | tf_op jit(solution)/shard_map/backward/pallas_call | solution.py:1164
  308.6 5.5 %hand_over.1 = (bf16[512,1024]{1,0:T(8,128)(2,1)}, f32[512,1024]{1,0:T(8,128)}, f32[1,32]{1,0:T(1,128)}, f32[32,6144]{1,0:T(8,128)}, f32[16,32]{1,0:T(8,128)}, /...) custom-call(bf16[512,1024]{1,0:T(8,128)(2,1)} %get-tuple-element.54., ...), custom_call_target="tpu_custom_call" | custom-call | tf_op jit(solution)/shard_map/hand_over/pallas_call | solution.py:1243

commit v6 on v5

--- a/solution.py
+++ b/solution.py
@@ -42,6 +42,11 @@
     lh, ll = split(left)
     rh, rl = split(right)
     return dot1(lh, rh, dims) + (dot1(lh, rl, dims) + dot1(ll, rh, dims))
+
+
+def dot_high(left, right, dims):
+    rh, rl = split(right)
+    return dot1(left, rh, dims) + dot1(left, rl, dims)
 
 
 def sigmoid(value):
@@ -1051,9 +1056,9 @@
             key_dots = dot3(ks, ks, NT)
             query_dots = dot3(qs, ks, NT)
             d_scores = dot3(d_core, update, NT)
-            d_update = dot1(pair * query_dots, d_core, TN)
-            solved = dot1(inverse, d_update, TN)
-            d_coupling = strict(-dot1(solved, update, NT)) * pair
+            d_update = dot3(pair * query_dots, d_core, TN)
+            solved = dot_high(inverse, d_update, TN)
+            d_coupling = strict(-dot3(solved, update, NT)) * pair
             d_query_dots = pair * d_scores
             d_key_dots = d_coupling * rs
             weighed = d_coupling * key_dots
@@ -1230,7 +1235,7 @@
         target[...] = source[...]
 
 
-def hand_over(arrays, steps=4):
+def hand_over(arrays, steps=2):
     specs = []
     for a in arrays:
         rows, cols = a.shape

time: 315 us -> 314 us (level)
  no operation moved by 1% of the time
where the time goes in v6:
time: 314 us; the launch traced here: 313 us
  Pallas kernels  312 us (99%)
    pallas_call x1, Pallas kernels, forward(): pl.pallas_call(partial(forward_body, planes, tiles), grid=(chunks,), in_s...  161 us
    pallas_call x1, Pallas kernels, backward(): pl.pallas_call(partial(backward_body, planes, tiles, chunks), grid=(chunk...  147 us

profile of v6, /device:TPU:0, one launch (start us, length us, event | category | flops | bytes accessed | tf_op | source)
XLA Modules:
  0.0 313.3 jit_solution(10025714981939406108)
XLA Ops:
  0.6 160.6 %forward.1 = (bf16[4,2,2,2,32,256]{5,4,3,2,1,0:T(8,128)(2,1)}, bf16[4,2,2,2,32,8192]{5,4,3,2,1,0:T(8,128)(2,1)}, bf16[4,2,2,2,32,8448]{5,4,3,2,1,0:T(8,128)(2,1)...) custom-call(f32[32,6144]{1,0:T(8,128)} %mixer_in_ref.1, ...), custom_call_target="tpu_custom_call" | custom-call | tf_op jit(solution)/shard_map/forward/pallas_call | solution.py:840
  161.2 147.3 %backward.1 = (f32[512,1024]{1,0:T(8,128)}, f32[1,32]{1,0:T(1,128)}, f32[32,6144]{1,0:T(8,128)}, f32[16,32]{1,0:T(8,128)}, f32[4,128]{1,0:T(4,128)}, /*index=5*/...) custom-call(bf16[4,4,2,32,8448]{4,3,2,1,0:T(8,128)(2,1)} %bitcast.18, ...), custom_call_target="tpu_custom_call" | custom-call | tf_op jit(solution)/shard_map/backward/pallas_call | solution.py:1169
  308.6 4.5 %hand_over.1 = (bf16[512,1024]{1,0:T(8,128)(2,1)}, f32[512,1024]{1,0:T(8,128)}, f32[1,32]{1,0:T(1,128)}, f32[32,6144]{1,0:T(8,128)}, f32[16,32]{1,0:T(8,128)}, /...) custom-call(bf16[512,1024]{1,0:T(8,128)(2,1)} %get-tuple-element.54., ...), custom_call_target="tpu_custom_call" | custom-call | tf_op jit(solution)/shard_map/hand_over/pallas_call | solution.py:1248

commit v7 on v6

--- a/solution.py
+++ b/solution.py
@@ -191,7 +191,6 @@
         near, far = flip(z, 1), flip(z, 2)
         here = lambda cols: (shard.at[:, cols], full.at[z, y, x, core, :, cols])
         same = lambda ref: (ref, ref)
-        by_y = kind == FFN_TILE
         (source, target), bit = {
             G_NEAR: lambda: (here(one), 8),
             G_FAR: lambda: (here(one), 16),
@@ -204,11 +203,7 @@
             G_CORE_OTHER: lambda: (same(full.at[:, 1 - y, :, core, :, one]), 1),
             G_TWO_X: lambda: (here(two), 2),
             G_TWO_Y: lambda: (here(two), 4),
-            G_TWO_CORNER: lambda: (
-                (same(full.at[z, 1 - y, x, core, :, two]), 2)
-                if by_y
-                else (same(full.at[z, y, 1 - x, core, :, two]), 4)
-            ),
+            G_TWO_CORNER: lambda: (same(full.at[z, 1 - y, x, core, :, two]), 2),
             G_TWO_NEAR: lambda: (same(full.at[z, :, :, core, :, two]), 8),
             G_TWO_FAR: lambda: (same(full.at[z, :, :, core, :, two]), 16),
             G_TWO_RELAY: lambda: (same(full.at[far, :, :, core, :, two]), 8),
@@ -238,7 +233,7 @@
         self.wait(kind, k, G_FAR)
         self.send(kind, k, G_RELAY)
         if self.two(kind):
-            self.wait(kind, k, *((G_TWO_Y,) if kind == FFN_TILE else (G_TWO_X,)))
+            self.wait(kind, k, G_TWO_Y)
             self.send(kind, k, G_TWO_CORNER)
 
     def square(self, kind, k):
@@ -246,7 +241,7 @@
         self.wait(kind, k, G_NEAR, G_RELAY)
         self.send(kind, k, G_X, G_Y)
         if self.two(kind):
-            self.wait(kind, k, *((G_TWO_X,) if kind == FFN_TILE else (G_TWO_Y,)), G_TWO_CORNER)
+            self.wait(kind, k, G_TWO_X, G_TWO_CORNER)
             self.send(kind, k, G_TWO_FAR, G_TWO_NEAR)
 
     def corner(self, kind, k):
@@ -306,7 +301,6 @@
         rest = pl.ds(0, width - part)
         sums = self.sums.at[self.slot(B_SUMS, r)]
         here, across_x, across_y, both, z = self.here, self.across_x, self.across_y, self.both, self.z
-        by_y = kind == FFN_TILE
         place = lambda where, cols: sums.at[:, where, :, cols]
         origin, target, bit = {
             S_CORE: lambda: (
@@ -331,7 +325,7 @@
                 sums.at[self.far, :, :, two], self.two_z.at[self.slot(B_TWO_Z, r), 2, :, :, rest], 16
             ),
             S_TWO_XY: lambda: (
-                sums.at[z, both, :, two], self.from_two.at[self.slot(B_TWO, r), 0, :, rest], 4 if by_y else 2
+                sums.at[z, both, :, two], self.from_two.at[self.slot(B_TWO, r), 0, :, rest], 4
             ),
             S_TWO_X: lambda: (sums.at[z, across_x, :, two], self.from_two.at[self.slot(B_TWO, r), 1, :, rest], 2),
             S_TWO_Y: lambda: (sums.at[z, across_y, :, two], self.from_two.at[self.slot(B_TWO, r), 2, :, rest], 4),
@@ -436,7 +430,7 @@
                 r, self.z, two,
                 [lambda place, i=i: self.two_z[self.slot(B_TWO_Z, r), i, place, :, rest] for i in (1, 2)],
             )
-            self.send(kind, r, k, S_TWO_XY, S_TWO_X if kind != FFN_TILE else S_TWO_Y)
+            self.send(kind, r, k, S_TWO_XY, S_TWO_Y)
 
     def relay_step(self, kind, r, k):
         width, part, half = SHAPES[kind]
@@ -448,12 +442,12 @@
         self.send(kind, r, k, S_FAR)
         if self.two(kind):
             two, rest = pl.ds(part, width - part), pl.ds(0, width - part)
-            place = self.across_x if kind == FFN_TILE else self.across_y
+            place = self.across_x
             self.wait(kind, r, k, S_TWO_XY)
             total = self.sums[slot, self.z, place, :, two].astype(F32)
             total = total + self.from_two[self.slot(B_TWO, r), 0, :, rest].astype(F32)
             self.sums[slot, self.z, place, :, two] = total.astype(BF16)
-            self.send(kind, r, k, S_TWO_X if kind == FFN_TILE else S_TWO_Y)
+            self.send(kind, r, k, S_TWO_X)
 
     def last_step(self, kind, r, k):
         width, part, half = SHAPES[kind]

time: 314 us -> 311 us (level)
  no operation moved by 1% of the time
where the time goes in v7:
time: 311 us
  Pallas kernels  310 us (100%)
    pallas_call x1, Pallas kernels, forward(): pl.pallas_call(partial(forward_body, planes, tiles), grid=(chunks,), in_s...  160 us
    pallas_call x1, Pallas kernels, backward(): pl.pallas_call(partial(backward_body, planes, tiles, chunks), grid=(chunk...  145 us

profile of v7, /device:TPU:0, one launch (start us, length us, event | category | flops | bytes accessed | tf_op | source)
XLA Modules:
  0.0 310.5 jit_solution(16671085663251598666)
XLA Ops:
  0.6 160.2 %forward.1 = (bf16[4,2,2,2,32,256]{5,4,3,2,1,0:T(8,128)(2,1)}, bf16[4,2,2,2,32,8192]{5,4,3,2,1,0:T(8,128)(2,1)}, bf16[4,2,2,2,32,8448]{5,4,3,2,1,0:T(8,128)(2,1)...) custom-call(f32[32,6144]{1,0:T(8,128)} %mixer_in_ref.1, ...), custom_call_target="tpu_custom_call" | custom-call | tf_op jit(solution)/shard_map/forward/pallas_call | solution.py:834
  160.8 145.0 %backward.1 = (f32[512,1024]{1,0:T(8,128)}, f32[1,32]{1,0:T(1,128)}, f32[32,6144]{1,0:T(8,128)}, f32[16,32]{1,0:T(8,128)}, f32[4,128]{1,0:T(4,128)}, /*index=5*/...) custom-call(bf16[4,4,2,32,8448]{4,3,2,1,0:T(8,128)(2,1)} %bitcast.18, ...), custom_call_target="tpu_custom_call" | custom-call | tf_op jit(solution)/shard_map/backward/pallas_call | solution.py:1163
  305.8 4.5 %hand_over.1 = (bf16[512,1024]{1,0:T(8,128)(2,1)}, f32[512,1024]{1,0:T(8,128)}, f32[1,32]{1,0:T(1,128)}, f32[32,6144]{1,0:T(8,128)}, f32[16,32]{1,0:T(8,128)}, /...) custom-call(bf16[512,1024]{1,0:T(8,128)(2,1)} %get-tuple-element.54., ...), custom_call_target="tpu_custom_call" | custom-call | tf_op jit(solution)/shard_map/hand_over/pallas_call | solution.py:1242
